TPU v7x, 32 devices: a whole 2x2x4 slice. The times are simulated.
32 devices in a mesh: kring: 16 (over z, x, core), slab: 2 (over y).
Axes of the slice: x: 2, y: 2, z: 4, core: 2. Of those that a mesh axis runs over, the one named last changes fastest.
Arguments:
- targets: float32 [16, 2, 2, 16, 256], P('kring', None, None, 'slab'), may hold values from -6 to 6
- orbitals: float32 [16, 32, 2, 16, 256], P('kring', None, None, 'slab'), may hold values from -6 to 6
- block_index: int32 [16], P('kring'), may hold values from 0 to 1
- occupied: int32 [16, 32], P('kring'), may hold values 0 or 1
- kpoint: int32 [16], replicated, may hold values from 0 to 15, each once
Outputs:
- exchange: float32 [16, 2, 2, 16, 256], P('kring', None, None, 'slab')
- projection: float32 [16, 2, 2, 2], P('kring')
Inputs may be any that keep to these rules, and one draw needn't show every extreme that they name: `kpoint`: every label appears at exactly one cycle position.
All inputs are finite; a program needn't handle non-finite values. No bound on the sum of `occupied` on one device may be relied on, other than what follows from the above.
Results may differ from a plain program's by a relative error of at most 0.0003.
Values sent between devices are 32-bit elements; how exact they have to be, the bound alone decides.
No kernel may reach another device: no remote copies, remote signals or barrier semaphores. Data moves between devices by JAX's collectives and lax.ppermute only.
A program may use at most 64 MiB of HBM per device.

v0:
```python
import math

import jax
import jax.numpy as jnp
from jax import lax
from jax.sharding import PartitionSpec as P

CX = 2
CY = 128
BLOCK = 16
HALF = 2


DIAG = 7.0


def extended(block, sides, width):
    for axis, dim in sides:
        count = lax.axis_size(axis)
        forward = [(i, i + 1) for i in range(count - 1)]
        forward.append((count - 1, 0))
        backward = [(target, source) for source, target in forward]
        low = lax.ppermute(
            lax.slice_in_dim(block, block.shape[dim] - width, None, axis=dim), axis, forward
        )
        high = lax.ppermute(lax.slice_in_dim(block, 0, width, axis=dim), axis, backward)
        block = jnp.concatenate([low, block, high], axis=dim)
    return block


def from_behind(block, axis, distance):
    devices = range(lax.axis_size(axis))
    route = [((i - distance) % len(devices), i) for i in devices]
    return lax.ppermute(block, axis, route)


def pair_density(psi, phi):
    psi_re = psi[:, None, 0]
    psi_im = psi[:, None, 1]
    phi_re = phi[None, :, 0]
    phi_im = phi[None, :, 1]
    rho_re = phi_re * psi_re + phi_im * psi_im
    rho_im = phi_re * psi_im - phi_im * psi_re
    return jnp.stack([rho_re, rho_im], axis=2)


def plane_sum(field):
    cells = field.shape[-1]
    column = jnp.mod(jnp.arange(cells, dtype=jnp.int32), CY)
    below_y = jnp.where(column == 0, jnp.roll(field, -(CY - 1), -1), jnp.roll(field, 1, -1))
    above_y = jnp.where(column == CY - 1, jnp.roll(field, CY - 1, -1), jnp.roll(field, -1, -1))
    below_x = jnp.roll(field, CY, -1)
    above_x = jnp.roll(field, -CY, -1)
    return below_y + above_y + below_x + above_x


def contribution(psi_use, phi_use, theta):
    cosine = jnp.cos(theta)
    sine = jnp.sin(theta)
    rho = pair_density(psi_use, phi_use)
    padded = extended(rho / DIAG, (("slab", 3),), 1)
    middle = padded[:, :, :, 1:-1]
    upper = padded[:, :, :, 2:]
    lower = padded[:, :, :, :-2]
    plane = plane_sum(middle)
    near_re = (
        plane[:, :, 0]
        + cosine * (upper[:, :, 0] + lower[:, :, 0])
        - sine * (upper[:, :, 1] - lower[:, :, 1])
    )
    near_im = (
        plane[:, :, 1]
        + cosine * (upper[:, :, 1] + lower[:, :, 1])
        + sine * (upper[:, :, 0] - lower[:, :, 0])
    )
    second = (rho + jnp.stack([near_re, near_im], axis=2)) / DIAG
    phi_re = phi_use[None, :, 0]
    phi_im = phi_use[None, :, 1]
    out_re = -jnp.sum(second[:, :, 0] * phi_re - second[:, :, 1] * phi_im, axis=1)
    out_im = -jnp.sum(second[:, :, 0] * phi_im + second[:, :, 1] * phi_re, axis=1)
    return jnp.stack([out_re, out_im], axis=1)


def fetch_left(block):
    return from_behind(block, "kring", 1)


def fetch_right(block):
    return from_behind(block, "kring", -1)


def body(targets, orbitals, block_index, occupied, kpoint):
    psi = targets[0]
    first_band = block_index[0] * BLOCK
    own = lax.dynamic_slice_in_dim(orbitals[0], first_band, BLOCK, 0)
    weight = lax.dynamic_slice_in_dim(occupied[0], first_band, BLOCK, 0).astype(jnp.float32)
    own = own * weight[:, None, None, None]
    cycle = lax.axis_size("kring")
    place = lax.axis_index("kring")
    positions = jnp.arange(cycle, dtype=jnp.int32)

    def label_at(where):
        return jnp.sum(jnp.where(positions == jnp.mod(where, cycle), kpoint, 0))

    mine = label_at(place)

    def phase(offset):
        return (mine - label_at(place + offset)).astype(jnp.float32) * (2.0 * math.pi / cycle)

    count = psi.shape[0]
    total = contribution(psi, own, phase(0))
    left = own
    for step in range(1, HALF + 1):
        left = fetch_left(left)
        total = total + contribution(psi, left, phase(-step))
    right = own
    for step in range(1, HALF + 1):
        right = fetch_right(right)
        total = total + contribution(psi, right, phase(step))
    flat_psi = psi.reshape(count, 2, -1)
    flat_out = total.reshape(count, 2, -1)
    real_part = jnp.einsum("apc,bpc->ab", flat_psi, flat_out, precision=lax.Precision.HIGHEST)
    imag_part = jnp.einsum(
        "ac,bc->ab", flat_psi[:, 0], flat_out[:, 1], precision=lax.Precision.HIGHEST
    ) - jnp.einsum("ac,bc->ab", flat_psi[:, 1], flat_out[:, 0], precision=lax.Precision.HIGHEST)
    tile = jnp.stack([real_part, imag_part], axis=-1)
    summed = lax.psum(tile, "slab")
    cells_all = psi.shape[2] * lax.axis_size("slab") * CX * CY
    return (total[None], (summed / cells_all)[None])


def solution(mesh):
    placed = (
        P("kring", None, None, "slab", None),
        P("kring", None, None, "slab", None),
        P("kring"),
        P("kring", None),
        P(),
    )
    return jax.shard_map(
        body,
        mesh=mesh,
        in_specs=placed,
        out_specs=(P("kring", None, None, "slab", None), P("kring", None, None, None)),
        check_vma=False,
    )
```

profile of v0, /device:TPU:0, one launch (start us, length us, event | category | flops | bytes accessed | tf_op | source)
XLA Modules:
  0.0 60.2 jit_solution(17388385391200009638)
XLA Ops:
  1.3 0.6 %copy-done.2 = s32[1,32]{1,0:T(1,128)S(1)} copy-done((s32[1,32]{1,0:T(1,128)S(1)}, s32[1,32]{1,0:T(1,128)}, u32[]{:S(2)}) %copy-start.2) | copy-done | bytes 152
  2.0 1.0 %bitcast_multiply_fusion = f32[16,2,8,256]{3,2,1,0:T(8,128)S(1)} fusion(f32[1,32,2,8,256]{4,3,2,1,0:T(8,128)} %param.6, s32[]{:T(128)S(6)} %select_n.109, f32[16]{0:T(128)S(1)} %convert_bitcast_fusion), kind=kLoop, calls=%fused_computation.93 | loop fusion | flops 65536 | bytes 524356 | tf_op jit(solution)/shard_map/mul | solution.py:97
  3.1 5.5 %collective-permute-start.8 = (f32[16,2,8,256]{3,2,1,0:T(8,128)S(1)}, f32[16,2,8,256]{3,2,1,0:T(8,128)S(1)}, u32[]{:S(2)}, u32[]{:S(2)}) collective-permute-start(f32[16,2,8,256]{3,2,1,0:T(8,128)S(1)} %bitcast_multiply_fusion), channel_id=1, source_target_pairs={{2,0},{4,2},{6,4},{8,6},{10,8},{12,10},{14,12},{16,14},{18,16},{20... | collective-permute-start | bytes 786440 | tf_op jit(solution)/shard_map/ppermute | solution.py:34
  8.7 0.6 %copy-done.1 = s32[16]{0:T(128)S(1)} copy-done((s32[16]{0:T(128)S(1)}, s32[16]{0:T(128)}, u32[]{:S(2)}) %copy-start.1) | copy-done | bytes 88
  9.4 0.8 %fusion.42 = (s32[]{:T(128)}, s32[]{:T(128)}, s32[]{:T(128)}, s32[]{:T(128)}, s32[]{:T(128)}) fusion(s32[16]{0:T(128)S(1)} %copy-done.1, s32[]{:T(128)S(6)} %select_n.129, s32[]{:T(128)S(6)} %select_n.121, s32[]{:T(128)S(6)} %select_n.117, s32[]{:T(128)S(6)} %select_n.115, s32[]{:T(128)S(6)} %select_n.125), kind=kLoop, calls=%fused_computation.154 | loop fusion | flops 235 | bytes 104 | tf_op jit(solution)/shard_map/reduce_sum | solution.py:103
  15.7 4.5 %collective-permute-start.11 = (f32[16,2,8,256]{3,2,1,0:T(8,128)S(1)}, f32[16,2,8,256]{3,2,1,0:T(8,128)S(1)}, u32[]{:S(2)}, u32[]{:S(2)}) collective-permute-start(f32[16,2,8,256]{3,2,1,0:T(8,128)S(1)} %collective-permute-done.8), channel_id=1, source_target_pairs={{2,0},{4,2},{6,4},{8,6},{10,8},{12,10},{14,12},{16,14},{18,16},{20... | collective-permute-start | bytes 786440 | tf_op jit(solution)/shard_map/ppermute | solution.py:34
  20.3 3.8 %collective-permute-done.11 = f32[16,2,8,256]{3,2,1,0:T(8,128)S(1)} collective-permute-done((f32[16,2,8,256]{3,2,1,0:T(8,128)S(1)}, f32[16,2,8,256]{3,2,1,0:T(8,128)S(1)}, u32[]{:S(2)}, u32[]{:S(2)}) %collective-permute-start.11) | collective-permute-done | bytes 262176 | tf_op jit(solution)/shard_map/ppermute | solution.py:34
  24.1 4.7 %collective-permute-done.5 = f32[16,2,8,256]{3,2,1,0:T(8,128)S(1)} collective-permute-done((f32[16,2,8,256]{3,2,1,0:T(8,128)S(1)}, f32[16,2,8,256]{3,2,1,0:T(8,128)S(1)}, u32[]{:S(2)}, u32[]{:S(2)}) %collective-permute-start.5) | collective-permute-done | bytes 262176 | tf_op jit(solution)/shard_map/ppermute | solution.py:34
  33.5 1.6 %collective-permute-start.12 = (f32[2,16,2,1,256]{4,3,1,0,2:T(1,128)S(1)}, f32[2,16,2,1,256]{4,3,1,0,2:T(1,128)S(1)}, u32[]{:S(2)}, u32[]{:S(2)}) collective-permute-start(f32[2,16,2,1,256]{4,3,1,0,2:T(1,128)S(1)} %get-tuple-element.22), channel_id=1, source_target_pairs={{1,0},{0,1},{3,2},{2,3},{5,4},{4,5},{7,6},{6,7},{9,8},{8,9},{11,10... | collective-permute-start | bytes 196616 | tf_op jit(solution)/shard_map/ppermute | solution.py:26
  35.1 0.5 collective-permute-start.13
  35.6 1.5 %collective-permute-start.10 = (f32[2,16,2,1,256]{4,3,1,0,2:T(1,128)S(1)}, f32[2,16,2,1,256]{4,3,1,0,2:T(1,128)S(1)}, u32[]{:S(2)}, u32[]{:S(2)}) collective-permute-start(f32[2,16,2,1,256]{4,3,1,0,2:T(1,128)S(1)} %get-tuple-element.33), channel_id=1, source_target_pairs={{0,1},{1,0},{2,3},{3,2},{4,5},{5,4},{6,7},{7,6},{8,9},{9,8},{10,11... | collective-permute-start | bytes 196616 | tf_op jit(solution)/shard_map/ppermute | solution.py:23
  37.1 0.5 collective-permute-start.9
  37.6 1.5 %collective-permute-start.6 = (f32[2,16,2,1,256]{4,3,1,0,2:T(1,128)S(1)}, f32[2,16,2,1,256]{4,3,1,0,2:T(1,128)S(1)}, u32[]{:S(2)}, u32[]{:S(2)}) collective-permute-start(f32[2,16,2,1,256]{4,3,1,0,2:T(1,128)S(1)} %get-tuple-element.46), channel_id=1, source_target_pairs={{1,0},{0,1},{3,2},{2,3},{5,4},{4,5},{7,6},{6,7},{9,8},{8,9},{11,10... | collective-permute-start | bytes 196616 | tf_op jit(solution)/shard_map/ppermute | solution.py:26
  39.1 0.5 add_add_fusion
  41.6 0.6 collective-permute-start.7
  42.2 1.5 %collective-permute-start.3 = (f32[2,16,2,1,256]{4,3,1,0,2:T(1,128)S(1)}, f32[2,16,2,1,256]{4,3,1,0,2:T(1,128)S(1)}, u32[]{:S(2)}, u32[]{:S(2)}) collective-permute-start(f32[2,16,2,1,256]{4,3,1,0,2:T(1,128)S(1)} %get-tuple-element.58), channel_id=1, source_target_pairs={{1,0},{0,1},{3,2},{2,3},{5,4},{4,5},{7,6},{6,7},{9,8},{8,9},{11,10... | collective-permute-start | bytes 196616 | tf_op jit(solution)/shard_map/ppermute | solution.py:26
  44.2 0.6 collective-permute-start.4
  44.8 1.5 %collective-permute-start = (f32[2,16,2,1,256]{4,3,1,0,2:T(1,128)S(1)}, f32[2,16,2,1,256]{4,3,1,0,2:T(1,128)}, u32[]{:S(2)}, u32[]{:S(2)}) collective-permute-start(f32[2,16,2,1,256]{4,3,1,0,2:T(1,128)S(1)} %get-tuple-element.70), channel_id=1, source_target_pairs={{1,0},{0,1},{3,2},{2,3},{5,4},{4,5},{7,6},{6,7},{9,8},{8,9},{11,10... | collective-permute-start | bytes 196616 | tf_op jit(solution)/shard_map/ppermute | solution.py:26
  46.9 0.6 collective-permute-start.1
  49.4 1.9 %collective-permute-done.1 = f32[2,16,2,1,256]{4,3,1,0,2:T(1,128)} collective-permute-done((f32[2,16,2,1,256]{4,3,1,0,2:T(1,128)S(1)}, f32[2,16,2,1,256]{4,3,1,0,2:T(1,128)}, u32[]{:S(2)}, u32[]{:S(2)}) %collective-permute-start.1) | collective-permute-done | bytes 65568 | tf_op jit(solution)/shard_map/ppermute | solution.py:23
  51.3 1.1 %fusion.25 = (f32[2,16,1,8,256]{4,3,1,0,2:T(8,128)S(1)}, f32[2,16,1,8,256]{4,3,1,0,2:T(8,128)S(1)}) fusion(f32[2,16,2,8,256]{4,3,1,0,2:T(8,128)S(1)} %add_add_fusion.4, f32[2,16,2,1,256]{4,3,1,0,2:T(1,128)} %collective-permute-done, f32[2,16,2,8,256]{4,3,1,0,2:T(8,128)S(1)} %fusion.15, f32[2,16,2,1,256]{4,3,1,0,2:T(1,128)} %collective-permute-done.1), kind=kLoop, calls=%fused_computation.92 | loop fusion | flops 917504 | bytes 1703936 | tf_op jit(solution)/shard_map/sub | solution.py:67
  54.0 5.0 %psum.7 = f32[2,2,2]{1,0,2:T(2,128)S(1)} all-reduce(f32[2,2,2]{1,0,2:T(2,128)S(1)} %pad_maximum_fusion.25), channel_id=1, replica_groups=mesh['kring'=16,'slab'=2] {'slab'}, use_global_device_ids=true, to_apply=%region_15.16 | all-reduce | flops 8 | bytes 64 | tf_op jit(solution)/shard_map/psum | solution.py:127
  58.9 0.7 %copy.19 = f32[2,2,2]{2,1,0:T(2,128)} copy(f32[2,2,2]{1,0,2:T(2,128)S(1)} %broadcast_multiply_fusion) | data formatting | bytes 64 | tf_op jit(solution)/shard_map/div | solution.py:129
  59.6 0.6 %copy.20 = f32[1,2,2,8,256]{4,3,2,1,0:T(8,128)} copy(f32[1,2,2,8,256]{4,3,1,2,0:T(8,128)S(1)} %fusion.28) | data formatting | bytes 65536
  (112 shorter events, 11.1 us)
Async XLA Ops:
  1.3 0.7 %copy-start.2 = (s32[1,32]{1,0:T(1,128)S(1)}, s32[1,32]{1,0:T(1,128)}, u32[]{:S(2)}) copy-start(s32[1,32]{1,0:T(1,128)} %param.8) | copy-start | bytes 388
  3.0 5.5 %copy-start = (f32[1,2,2,8,256]{4,3,2,1,0:T(8,128)S(1)}, f32[1,2,2,8,256]{4,3,2,1,0:T(8,128)}, u32[]{:S(2)}) copy-start(f32[1,2,2,8,256]{4,3,2,1,0:T(8,128)} %param.5) | copy-start | bytes 98308
  3.1 12.6 %collective-permute-start.8 = (f32[16,2,8,256]{3,2,1,0:T(8,128)S(1)}, f32[16,2,8,256]{3,2,1,0:T(8,128)S(1)}, u32[]{:S(2)}, u32[]{:S(2)}) collective-permute-start(f32[16,2,8,256]{3,2,1,0:T(8,128)S(1)} %bitcast_multiply_fusion), channel_id=1, source_target_pairs={{2,0},{4,2},{6,4},{8,6},{10,8},{12,10},{14,12},{16,14},{18,16},{20... | collective-permute-start | bytes 786440 | tf_op jit(solution)/shard_map/ppermute | solution.py:34
  8.5 11.7 %collective-permute-start.2 = (f32[16,2,8,256]{3,2,1,0:T(8,128)S(1)}, f32[16,2,8,256]{3,2,1,0:T(8,128)S(1)}, u32[]{:S(2)}, u32[]{:S(2)}) collective-permute-start(f32[16,2,8,256]{3,2,1,0:T(8,128)S(1)} %bitcast_multiply_fusion), channel_id=1, source_target_pairs={{30,0},{0,2},{2,4},{4,6},{6,8},{8,10},{10,12},{12,14},{14,16},{16,... | collective-permute-start | bytes 786440 | tf_op jit(solution)/shard_map/ppermute | solution.py:34
  8.7 0.7 %copy-start.1 = (s32[16]{0:T(128)S(1)}, s32[16]{0:T(128)}, u32[]{:S(2)}) copy-start(s32[16]{0:T(128)} %param.9) | copy-start | bytes 196
  15.7 8.4 %collective-permute-start.11 = (f32[16,2,8,256]{3,2,1,0:T(8,128)S(1)}, f32[16,2,8,256]{3,2,1,0:T(8,128)S(1)}, u32[]{:S(2)}, u32[]{:S(2)}) collective-permute-start(f32[16,2,8,256]{3,2,1,0:T(8,128)S(1)} %collective-permute-done.8), channel_id=1, source_target_pairs={{2,0},{4,2},{6,4},{8,6},{10,8},{12,10},{14,12},{16,14},{18,16},{20... | collective-permute-start | bytes 786440 | tf_op jit(solution)/shard_map/ppermute | solution.py:34
  20.2 8.5 %collective-permute-start.5 = (f32[16,2,8,256]{3,2,1,0:T(8,128)S(1)}, f32[16,2,8,256]{3,2,1,0:T(8,128)S(1)}, u32[]{:S(2)}, u32[]{:S(2)}) collective-permute-start(f32[16,2,8,256]{3,2,1,0:T(8,128)S(1)} %collective-permute-done.2), channel_id=1, source_target_pairs={{30,0},{0,2},{2,4},{4,6},{6,8},{8,10},{10,12},{12,14},{14,16},{16,... | collective-permute-start | bytes 786440 | tf_op jit(solution)/shard_map/ppermute | solution.py:34
  33.5 8.1 %collective-permute-start.12 = (f32[2,16,2,1,256]{4,3,1,0,2:T(1,128)S(1)}, f32[2,16,2,1,256]{4,3,1,0,2:T(1,128)S(1)}, u32[]{:S(2)}, u32[]{:S(2)}) collective-permute-start(f32[2,16,2,1,256]{4,3,1,0,2:T(1,128)S(1)} %get-tuple-element.22), channel_id=1, source_target_pairs={{1,0},{0,1},{3,2},{2,3},{5,4},{4,5},{7,6},{6,7},{9,8},{8,9},{11,10... | collective-permute-start | bytes 196616 | tf_op jit(solution)/shard_map/ppermute | solution.py:26
  35.1 7.1 %collective-permute-start.13 = (f32[2,16,2,1,256]{4,3,1,0,2:T(1,128)S(1)}, f32[2,16,2,1,256]{4,3,1,0,2:T(1,128)S(1)}, u32[]{:S(2)}, u32[]{:S(2)}) collective-permute-start(f32[2,16,2,1,256]{4,3,1,0,2:T(1,128)S(1)} %get-tuple-element.21), channel_id=1, source_target_pairs={{0,1},{1,0},{2,3},{3,2},{4,5},{5,4},{6,7},{7,6},{8,9},{9,8},{10,11... | collective-permute-start | bytes 196616 | tf_op jit(solution)/shard_map/ppermute | solution.py:23
  35.6 8.6 %collective-permute-start.10 = (f32[2,16,2,1,256]{4,3,1,0,2:T(1,128)S(1)}, f32[2,16,2,1,256]{4,3,1,0,2:T(1,128)S(1)}, u32[]{:S(2)}, u32[]{:S(2)}) collective-permute-start(f32[2,16,2,1,256]{4,3,1,0,2:T(1,128)S(1)} %get-tuple-element.33), channel_id=1, source_target_pairs={{0,1},{1,0},{2,3},{3,2},{4,5},{5,4},{6,7},{7,6},{8,9},{9,8},{10,11... | collective-permute-start | bytes 196616 | tf_op jit(solution)/shard_map/ppermute | solution.py:23
  37.1 7.7 %collective-permute-start.9 = (f32[2,16,2,1,256]{4,3,1,0,2:T(1,128)S(1)}, f32[2,16,2,1,256]{4,3,1,0,2:T(1,128)S(1)}, u32[]{:S(2)}, u32[]{:S(2)}) collective-permute-start(f32[2,16,2,1,256]{4,3,1,0,2:T(1,128)S(1)} %get-tuple-element.34), channel_id=1, source_target_pairs={{1,0},{0,1},{3,2},{2,3},{5,4},{4,5},{7,6},{6,7},{9,8},{8,9},{11,10... | collective-permute-start | bytes 196616 | tf_op jit(solution)/shard_map/ppermute | solution.py:26
  37.6 9.2 %collective-permute-start.6 = (f32[2,16,2,1,256]{4,3,1,0,2:T(1,128)S(1)}, f32[2,16,2,1,256]{4,3,1,0,2:T(1,128)S(1)}, u32[]{:S(2)}, u32[]{:S(2)}) collective-permute-start(f32[2,16,2,1,256]{4,3,1,0,2:T(1,128)S(1)} %get-tuple-element.46), channel_id=1, source_target_pairs={{1,0},{0,1},{3,2},{2,3},{5,4},{4,5},{7,6},{6,7},{9,8},{8,9},{11,10... | collective-permute-start | bytes 196616 | tf_op jit(solution)/shard_map/ppermute | solution.py:26
  41.6 5.9 %collective-permute-start.7 = (f32[2,16,2,1,256]{4,3,1,0,2:T(1,128)S(1)}, f32[2,16,2,1,256]{4,3,1,0,2:T(1,128)S(1)}, u32[]{:S(2)}, u32[]{:S(2)}) collective-permute-start(f32[2,16,2,1,256]{4,3,1,0,2:T(1,128)S(1)} %get-tuple-element.45), channel_id=1, source_target_pairs={{0,1},{1,0},{2,3},{3,2},{4,5},{5,4},{6,7},{7,6},{8,9},{9,8},{10,11... | collective-permute-start | bytes 196616 | tf_op jit(solution)/shard_map/ppermute | solution.py:23
  42.2 6.1 %collective-permute-start.3 = (f32[2,16,2,1,256]{4,3,1,0,2:T(1,128)S(1)}, f32[2,16,2,1,256]{4,3,1,0,2:T(1,128)S(1)}, u32[]{:S(2)}, u32[]{:S(2)}) collective-permute-start(f32[2,16,2,1,256]{4,3,1,0,2:T(1,128)S(1)} %get-tuple-element.58), channel_id=1, source_target_pairs={{1,0},{0,1},{3,2},{2,3},{5,4},{4,5},{7,6},{6,7},{9,8},{8,9},{11,10... | collective-permute-start | bytes 196616 | tf_op jit(solution)/shard_map/ppermute | solution.py:26
  44.2 4.3 %collective-permute-start.4 = (f32[2,16,2,1,256]{4,3,1,0,2:T(1,128)S(1)}, f32[2,16,2,1,256]{4,3,1,0,2:T(1,128)S(1)}, u32[]{:S(2)}, u32[]{:S(2)}) collective-permute-start(f32[2,16,2,1,256]{4,3,1,0,2:T(1,128)S(1)} %get-tuple-element.57), channel_id=1, source_target_pairs={{0,1},{1,0},{2,3},{3,2},{4,5},{5,4},{6,7},{7,6},{8,9},{9,8},{10,11... | collective-permute-start | bytes 196616 | tf_op jit(solution)/shard_map/ppermute | solution.py:23
  44.8 4.5 %collective-permute-start = (f32[2,16,2,1,256]{4,3,1,0,2:T(1,128)S(1)}, f32[2,16,2,1,256]{4,3,1,0,2:T(1,128)}, u32[]{:S(2)}, u32[]{:S(2)}) collective-permute-start(f32[2,16,2,1,256]{4,3,1,0,2:T(1,128)S(1)} %get-tuple-element.70), channel_id=1, source_target_pairs={{1,0},{0,1},{3,2},{2,3},{5,4},{4,5},{7,6},{6,7},{9,8},{8,9},{11,10... | collective-permute-start | bytes 196616 | tf_op jit(solution)/shard_map/ppermute | solution.py:26
  46.9 4.4 %collective-permute-start.1 = (f32[2,16,2,1,256]{4,3,1,0,2:T(1,128)S(1)}, f32[2,16,2,1,256]{4,3,1,0,2:T(1,128)}, u32[]{:S(2)}, u32[]{:S(2)}) collective-permute-start(f32[2,16,2,1,256]{4,3,1,0,2:T(1,128)S(1)} %get-tuple-element.69), channel_id=1, source_target_pairs={{0,1},{1,0},{2,3},{3,2},{4,5},{5,4},{6,7},{7,6},{8,9},{9,8},{10,11... | collective-permute-start | bytes 196616 | tf_op jit(solution)/shard_map/ppermute | solution.py:23
where the time goes:
time: 60.6 us; the launch traced here: 60.2 us
  starting transfers between devices  20.4 us (34%)
  waiting for transfers between devices  10.8 us (18%)
  other arithmetic  8.6 us (14%)
  between operations  7.48 us (12%)
  local copies, waits for them, and re-layouts  7.07 us (12%)
  blocking collectives  4.97 us (8%)
  matrix products  0.86 us (1%)
    ppermute x4, starting transfers between devices, from_behind(): return lax.ppermute(block, axis, route)  10 us
    ppermute x4, waiting for transfers between devices, from_behind(): return lax.ppermute(block, axis, route)  8.44 us
    ppermute x5, starting transfers between devices, extended(): lax.ppermute(lax.slice_in_dim(block, 0, width, axis=dim), axis, backward)  6.61 us
    psum x1, blocking collectives, body(): summed = lax.psum(tile, 'slab')  4.97 us
    ppermute x5, starting transfers between devices, extended(): lax.ppermute(lax.slice_in_dim(block, block.shape[dim] - width, None, axis...  3.79 us
    add x5, other arithmetic, plane_sum(): return below_y + above_y + below_x + above_x  2.4 us
    ppermute x5, waiting for transfers between devices, extended(): lax.ppermute(lax.slice_in_dim(block, block.shape[dim] - width, None, axis...  2.2 us
    sub x5, other arithmetic, contribution(): plane[:, :, 0] + cosine * (upper[:, :, 0] + lower[:, :, 0])  1.99 us
  transfers between devices with their start and end apart: 14, of which 5 were waited for; matrix products, arithmetic and copies ran while one was open for 10% of the time, Pallas kernels for 0%

commit v1 on v0

v1 whole, which is shorter than its diff:
```python
import math

import jax
import jax.numpy as jnp
from jax import lax
from jax.experimental import pallas as pl
from jax.experimental.pallas import tpu as pltpu
from jax.sharding import PartitionSpec as P

CX = 2
CY = 128
CELLS = CX * CY
BLOCK = 16
FIELDS = 6
DIAG = 7.0

VMEM = pl.BlockSpec(memory_space=pltpu.VMEM)
SMEM = pl.BlockSpec(memory_space=pltpu.SMEM)
ANY = pl.BlockSpec(memory_space=pl.ANY)


def halves(field):
    return field[:, :CY], field[:, CY:]


def turn(field, shift):
    a, b = halves(field)
    amount = (-shift) % CY
    return jnp.concatenate([pltpu.roll(a, amount, 1), pltpu.roll(b, amount, 1)], axis=1)


def swap_x(field):
    a, b = halves(field)
    return jnp.concatenate([b, a], axis=1)


def bond(ar, ai, br, bi):
    return ar * br + ai * bi, ai * br - ar * bi


def gather_kernel(planes, index_ref, occupied_ref, psi_hbm, orb_hbm, pack_ref, orb, sems):
    rows = 2 * planes
    field_rows = FIELDS * planes
    end_rows = 4 * BLOCK
    psi_rows = psi_hbm.shape[0]
    loads = [pltpu.make_async_copy(orb_hbm.at[:, pl.ds(x * CY, CY)], orb.at[x], sems.at[x]) for x in range(CX)]
    for load in loads:
        load.start()
    keep = pltpu.make_async_copy(psi_hbm, pack_ref.at[pl.ds(field_rows + end_rows, psi_rows)], sems.at[CX])
    keep.start()
    first = index_ref[0] * BLOCK
    weights = [occupied_ref[0, first + m].astype(jnp.float32) for m in range(BLOCK)]
    for load in loads:
        load.wait()
    dens = jnp.zeros((planes, CELLS), jnp.float32)
    dx_re = jnp.zeros((planes, CY), jnp.float32)
    dx_im = jnp.zeros((planes, CY), jnp.float32)
    dy_re, dy_im, dz_re, dz_im = dens, dens, dens, dens
    for m in range(BLOCK):
        base = pl.multiple_of((first + m) * rows, 8)
        re = jnp.concatenate([orb[x, pl.ds(base, planes), :] for x in range(CX)], axis=1) * weights[m]
        im = jnp.concatenate([orb[x, pl.ds(base + planes, planes), :] for x in range(CX)], axis=1) * weights[m]
        dens = dens + re * re + im * im
        re0, re1 = halves(re)
        im0, im1 = halves(im)
        part = bond(re0, im0, re1, im1)
        dx_re, dx_im = dx_re + part[0], dx_im + part[1]
        part = bond(re, im, turn(re, 1), turn(im, 1))
        dy_re, dy_im = dy_re + part[0], dy_im + part[1]
        part = bond(re, im, pltpu.roll(re, planes - 1, 0), pltpu.roll(im, planes - 1, 0))
        dz_re, dz_im = dz_re + part[0], dz_im + part[1]
    for i, field in enumerate((dens, jnp.concatenate([dx_re, dx_im], axis=1), dy_re, dy_im, dz_re, dz_im)):
        pack_ref[pl.ds(i * planes, planes), :] = field
    band = lax.broadcasted_iota(jnp.int32, (BLOCK, 1), 0)
    column = jnp.zeros((BLOCK, 1), jnp.float32)
    for m in range(BLOCK):
        column = jnp.where(band == m, weights[m], column)
    for e, plane in enumerate((0, planes - 1)):
        for c in range(2):
            start = first * rows + c * planes + plane
            for x in range(CX):
                ends = orb[x, pl.ds(start, BLOCK, stride=rows), :] * column
                pack_ref[pl.ds(field_rows + (2 * e + c) * BLOCK, BLOCK), pl.ds(x * CY, CY)] = ends
    keep.wait()


def gather(block_index, occupied, psi, orb, planes):
    psi_rows = psi.shape[0]
    total = FIELDS * planes + 4 * BLOCK + psi_rows

    def body(*refs):
        gather_kernel(planes, *refs)

    return pl.pallas_call(
        body,
        out_shape=jax.ShapeDtypeStruct((total, CELLS), jnp.float32),
        in_specs=[SMEM, SMEM, ANY, ANY],
        out_specs=VMEM,
        scratch_shapes=[pltpu.VMEM((CX, orb.shape[0], CY), jnp.float32), pltpu.SemaphoreType.DMA((CX + 1,))],
        name="local_fields",
    )(block_index, occupied, psi, orb)


def join(phase, packs, planes):
    count = len(packs)
    field_rows = FIELDS * planes

    def body(phase_ref, *refs):
        ins, out = refs[:count], refs[count]
        cosine, sine = phase_ref[0], phase_ref[1]
        last = lax.broadcasted_iota(jnp.int32, (planes, CELLS), 0) == planes - 1

        def end(ref, e, c):
            return ref[pl.ds(field_rows + (2 * e + c) * BLOCK, BLOCK), :]

        for d in range(count):
            here, there = ins[d], ins[(d + 1) % count]
            out[pl.ds(d * field_rows, 4 * planes), :] = here[pl.ds(0, 4 * planes), :]
            re, im = bond(end(here, 1, 0), end(here, 1, 1), end(there, 0, 0), end(there, 0, 1))
            re = jnp.sum(re, axis=0, keepdims=True)
            im = jnp.sum(im, axis=0, keepdims=True)
            re = jnp.where(last, re, here[pl.ds(4 * planes, planes), :])
            im = jnp.where(last, im, here[pl.ds(5 * planes, planes), :])
            out[pl.ds(d * field_rows + 4 * planes, planes), :] = re * cosine + im * sine
            out[pl.ds(d * field_rows + 5 * planes, planes), :] = im * cosine - re * sine

    return pl.pallas_call(
        body,
        out_shape=jax.ShapeDtypeStruct((count * field_rows, CELLS), jnp.float32),
        in_specs=[SMEM] + [VMEM] * count,
        out_specs=VMEM,
        name="join_slabs",
    )(phase, *packs)


def apply(phase, parts, packs, planes, bands):
    count = len(packs)
    field_rows = FIELDS * planes
    psi_start = field_rows + 4 * BLOCK
    scale = 1.0 / (count * planes * CELLS)

    def body(phase_ref, *refs):
        part_refs, ins = refs[: len(parts)], refs[len(parts) : len(parts) + count]
        out_ref, tile_ref = refs[len(parts) + count :]
        cosine, sine = phase_ref[0], phase_ref[1]
        row = lax.broadcasted_iota(jnp.int32, (planes, CELLS), 0)

        def window(d, i, offset=0):
            at = pl.ds(d * field_rows + i * planes, planes)
            total = part_refs[0][at, :]
            for ref in part_refs[1:]:
                total = total + ref[at, :]
            return total

        def psi_at(d, b, c):
            return ins[d % count][pl.ds(psi_start + (2 * b + c) * planes, planes), :]

        def above(d, field):
            return jnp.where(row == planes - 1, pltpu.roll(field(d + 1), planes - 1, 0), pltpu.roll(field(d), planes - 1, 0))

        def below(d, field):
            return jnp.where(row == 0, pltpu.roll(field(d - 1), 1, 0), pltpu.roll(field(d), 1, 0))

        up = []
        for d in range(count):
            re, im = window(d, 4), window(d, 5)
            up.append((re * cosine - im * sine, im * cosine + re * sine))
        sums = [[[None, None] for _ in range(bands)] for _ in range(bands)]
        for d in range(count):
            dens = window(d, 0) * (1.0 / DIAG)
            dx_re, dx_im = halves(window(d, 1))
            x_re = jnp.concatenate([dx_re, dx_re], axis=1) * 2.0
            x_im = jnp.concatenate([dx_im, -dx_im], axis=1) * 2.0
            y_re, y_im = window(d, 2), window(d, 3)
            yb_re, yb_im = turn(y_re, -1), -turn(y_im, -1)
            z_re, z_im = up[d]
            zb_re = below(d, lambda e: up[e % count][0])
            zb_im = -below(d, lambda e: up[e % count][1])
            results = []
            for b in range(bands):
                re, im = psi_at(d, b, 0), psi_at(d, b, 1)
                acc_re = jnp.zeros_like(re)
                acc_im = jnp.zeros_like(re)
                terms = (
                    (x_re, x_im, swap_x(re), swap_x(im)),
                    (y_re, y_im, turn(re, 1), turn(im, 1)),
                    (yb_re, yb_im, turn(re, -1), turn(im, -1)),
                    (z_re, z_im, above(d, lambda e: psi_at(e, b, 0)), above(d, lambda e: psi_at(e, b, 1))),
                    (zb_re, zb_im, below(d, lambda e: psi_at(e, b, 0)), below(d, lambda e: psi_at(e, b, 1))),
                )
                for wr, wi, vr, vi in terms:
                    acc_re = acc_re + (wr * vr - wi * vi)
                    acc_im = acc_im + (wr * vi + wi * vr)
                out_re = -(dens * re + acc_re * (1.0 / (DIAG * DIAG)))
                out_im = -(dens * im + acc_im * (1.0 / (DIAG * DIAG)))
                results.append((out_re, out_im))
                if d == 0:
                    out_ref[pl.ds(2 * b * planes, planes), :] = out_re
                    out_ref[pl.ds((2 * b + 1) * planes, planes), :] = out_im
            for a in range(bands):
                re, im = psi_at(d, a, 0), psi_at(d, a, 1)
                for b in range(bands):
                    out_re, out_im = results[b]
                    both = (re * out_re + im * out_im, re * out_im - im * out_re)
                    for c in range(2):
                        old = sums[a][b][c]
                        sums[a][b][c] = both[c] if old is None else old + both[c]
        shape = (bands, 2)
        first = lax.broadcasted_iota(jnp.int32, shape, 0)
        second = lax.broadcasted_iota(jnp.int32, shape, 1)
        for a in range(bands):
            tile = jnp.zeros(shape, jnp.float32)
            for b in range(bands):
                for c in range(2):
                    folded = sums[a][b][c]
                    folded = folded[:, :CY] + folded[:, CY:]
                    value = jnp.sum(jnp.sum(folded, axis=0, keepdims=True), axis=1, keepdims=True)
                    tile = jnp.where((first == b) & (second == c), value * scale, tile)
            tile_ref[0, a] = tile

    return pl.pallas_call(
        body,
        out_shape=(
            jax.ShapeDtypeStruct((2 * bands * planes, CELLS), jnp.float32),
            jax.ShapeDtypeStruct((1, bands, bands, 2), jnp.float32),
        ),
        in_specs=[SMEM] + [VMEM] * (len(parts) + count),
        out_specs=(VMEM, VMEM),
        name="apply_window",
    )(phase, *parts, *packs)


def shift(value, axis, distance):
    count = lax.axis_size(axis)
    return lax.ppermute(value, axis, [((i + distance) % count, i) for i in range(count)])


def body(targets, orbitals, block_index, occupied, kpoint):
    bands, planes = targets.shape[1], targets.shape[3]
    cycle, slabs = lax.axis_size("kring"), lax.axis_size("slab")
    place = lax.axis_index("kring")
    psi = targets.reshape(2 * bands * planes, CELLS)
    orb = orbitals.reshape(-1, CELLS)

    angle = lax.dynamic_index_in_dim(kpoint, place, 0, False).astype(jnp.float32) * (2.0 * math.pi / cycle)
    phase = jnp.stack([jnp.cos(angle), jnp.sin(angle)])

    own = gather(block_index, occupied, psi, orb, planes)
    packs = [own] + [shift(own, "slab", d) for d in range(1, slabs)]
    mine = join(phase, packs, planes)

    other = lax.ppermute(mine, "kring", [(i, i ^ 1) for i in range(cycle)])
    pair = mine + other
    even = lax.rem(place, 2) == 0
    left = shift(jnp.where(even, pair, mine), "kring", -2)
    right = shift(jnp.where(even, mine, pair), "kring", 2)
    exchange, tile = apply(phase, [pair, left, right], packs, planes, bands)
    return exchange.reshape(targets.shape), tile


def solution(mesh):
    placed = (
        P("kring", None, None, "slab", None),
        P("kring", None, None, "slab", None),
        P("kring"),
        P("kring", None),
        P(),
    )
    return jax.shard_map(
        body,
        mesh=mesh,
        in_specs=placed,
        out_specs=(P("kring", None, None, "slab", None), P("kring", None, None, None)),
        check_vma=False,
    )
```

time: 60.6 us -> 31.2 us (0.51)
  starting transfers between devices: 20.4 us -> 7.79 us
  other arithmetic: 8.6 us -> 1.57 us
  Pallas kernels: 0 us -> 6.13 us
  between operations: 7.48 us -> 2.13 us
  blocking collectives: 4.97 us -> 0 us
  local copies, waits for them, and re-layouts: 7.07 us -> 3.12 us
  matrix products: 0.86 us -> 0 us
    ppermute x14 -> x4, starting transfers between devices: 20.4 us -> 7.79 us  [the longest x3 7.78 us: shift(): lax.ppermute(value, axis, [((i + distance) % count, i) for i in range(cou...]
    pallas_call x0 -> x3, Pallas kernels: none -> 6.13 us  [the longest x1 2.54 us: gather(): pl.pallas_call(body, out_shape=jax.ShapeDtypeStruct((total, CELLS), jnp.f...]
    psum x1 -> x0, blocking collectives: 4.97 us -> none  [body(): summed = lax.psum(tile, 'slab')]
    slice x31 -> x0, local copies, waits for them, and re-layouts: 4.01 us -> none  [the longest x10 1.72 us: plane_sum(): jnp.roll(field, CY - 1, -1)]
    add x12 -> x0, other arithmetic: 3.68 us -> none  [the longest x5 2.4 us: plane_sum(): return below_y + above_y + below_x + above_x]
    sub x5 -> x0, other arithmetic: 1.99 us -> none  [contribution(): plane[:, :, 0] + cosine * (upper[:, :, 0] + lower[:, :, 0])]
    reduce_sum x6 -> x0, other arithmetic: 1.13 us -> none  [the longest x1 0.76 us: label_at(): return jnp.sum(jnp.where(positions == jnp.mod(where, cycle), kpoint, 0))]
    mul x1 -> x0, other arithmetic: 1.03 us -> none  [body(): own = own * weight[:, None, None, None]]
  transfers between devices with their start and end apart: 14 -> 4, of which waited for: 5 -> 4; matrix products, arithmetic and copies ran while one was open for 10% -> 4% of each run, Pallas kernels for 0% -> 0%
where the time goes in v1:
time: 31.2 us; the launch traced here: 30.9 us
  waiting for transfers between devices  10.2 us (33%)
  starting transfers between devices  7.79 us (25%)
  Pallas kernels  6.13 us (20%)
  local copies, waits for them, and re-layouts  3.12 us (10%)
  between operations  2.13 us (7%)
  other arithmetic  1.57 us (5%)
    ppermute x3, waiting for transfers between devices, shift(): lax.ppermute(value, axis, [((i + distance) % count, i) for i in range(cou...  8.67 us
    ppermute x3, starting transfers between devices, shift(): lax.ppermute(value, axis, [((i + distance) % count, i) for i in range(cou...  7.78 us
    pallas_call x1, Pallas kernels, gather(): pl.pallas_call(body, out_shape=jax.ShapeDtypeStruct((total, CELLS), jnp.f...  2.54 us
    unnamed x12, local copies, waits for them, and re-layouts  2.54 us
    pallas_call x1, Pallas kernels, apply(): pl.pallas_call(body, out_shape=(jax.ShapeDtypeStruct((2 * bands * planes,...  1.93 us
    pallas_call x1, Pallas kernels, join(): pl.pallas_call(body, out_shape=jax.ShapeDtypeStruct((count * field_rows,...  1.66 us
    ppermute x1, waiting for transfers between devices, body(): other = lax.ppermute(mine, 'kring', [(i, i ^ 1) for i in range(cycle)])  1.51 us
    select_n x1, other arithmetic, body(): right = shift(jnp.where(even, mine, pair), 'kring', 2)  0.91 us
  transfers between devices with their start and end apart: 4, of which 4 were waited for; matrix products, arithmetic and copies ran while one was open for 4% of the time, Pallas kernels for 0%

profile of v1, /device:TPU:0, one launch (start us, length us, event | category | flops | bytes accessed | tf_op | source)
XLA Modules:
  0.0 30.9 jit_solution(9148806301583583348)
XLA Ops:
  1.3 2.5 %local_fields.1.refs_0_.refs_3_ = f32[144,256]{1,0:T(8,128)} custom-call(s32[1]{0:T(128)S(6)} %copy.7.refs_0_, s32[1,32]{1,0:T(1,128)} %refs_1_.1, f32[32,256]{1,0:T(8,128)} %bitcast.4, f32[512,256]{1,0:T(8,128)} %bitcast.3), custom_call_target="tpu_custom_call" | custom-call | tf_op jit(solution)/shard_map/local_fields/pallas_call | solution.py:94
  3.8 3.0 %collective-permute-start = (f32[144,256]{1,0:T(8,128)}, f32[144,256]{1,0:T(8,128)S(1)}, u32[]{:S(2)}, u32[]{:S(2)}) collective-permute-start(f32[144,256]{1,0:T(8,128)} %local_fields.1.refs_0_.refs_3_), channel_id=1, source_target_pairs={{1,0},{0,1},{3,2},{2,3},{5,4},{4,5},{7,6},{6,7},{9,8},{8,9},{11,10... | collective-permute-start | bytes 442376 | tf_op jit(solution)/shard_map/ppermute | solution.py:235
  6.9 0.0 copy-start.5
  6.9 0.7 %copy-done.5 = s32[16]{0:T(128)S(1)} copy-done((s32[16]{0:T(128)S(1)}, s32[16]{0:T(128)}, u32[]{:S(2)}) %copy-start.5) | copy-done | bytes 88
  7.5 0.6 %dynamic_slice.4 = s32[1]{0:T(128)} dynamic-slice(s32[16]{0:T(128)S(1)} %copy-done.5, s32[]{:T(128)S(6)} %select_n.16), dynamic_slice_sizes={1} | dynamic-slice | bytes 12 | tf_op jit(solution)/shard_map/jit(dynamic_index_in_dim)/dynamic_slice | solution.py:245
  8.9 0.6 %pad_maximum_fusion.phase_ref = f32[2]{0:T(128)} fusion(f32[1]{0:T(128)S(6)} %sin.4, f32[1]{0:T(128)S(6)} %cos.4), kind=kLoop, calls=%fused_computation.2 | loop fusion | flops 2 | bytes 16 | tf_op jit(solution)/shard_map/stack | solution.py:246
  9.6 1.4 %collective-permute-done.refs_1_.refs_4_ = f32[144,256]{1,0:T(8,128)S(1)} collective-permute-done((f32[144,256]{1,0:T(8,128)}, f32[144,256]{1,0:T(8,128)S(1)}, u32[]{:S(2)}, u32[]{:S(2)}) %collective-permute-start) | collective-permute-done | bytes 147488 | tf_op jit(solution)/shard_map/ppermute | solution.py:235
  10.9 0.0 copy-start.2
  10.9 0.6 %copy-done.2 = f32[144,256]{1,0:T(8,128)} copy-done((f32[144,256]{1,0:T(8,128)}, f32[144,256]{1,0:T(8,128)S(1)}, u32[]{:S(2)}) %copy-start.2) | copy-done | bytes 147480
  11.6 1.7 %join_slabs.1 = f32[96,256]{1,0:T(8,128)} custom-call(f32[2]{0:T(128)} %pad_maximum_fusion.phase_ref, f32[144,256]{1,0:T(8,128)} %local_fields.1.refs_0_.refs_3_, f32[144,256]{1,0:T(8,128)} %copy-done.2), custom_call_target="tpu_custom_call" | custom-call | tf_op jit(solution)/shard_map/join_slabs/pallas_call | solution.py:127
  13.2 0.0 collective-permute-start.1
  13.2 1.5 %collective-permute-done.1 = f32[96,256]{1,0:T(8,128)S(1)} collective-permute-done((f32[96,256]{1,0:T(8,128)}, f32[96,256]{1,0:T(8,128)S(1)}, u32[]{:S(2)}, u32[]{:S(2)}) %collective-permute-start.1) | collective-permute-done | bytes 98336 | tf_op jit(solution)/shard_map/ppermute | solution.py:252
  14.7 0.9 %broadcast_select_fusion = (f32[96,256]{1,0:T(8,128)S(1)}, f32[96,256]{1,0:T(8,128)S(1)}) fusion(f32[96,256]{1,0:T(8,128)} %join_slabs.1, pred[]{:T(512)S(6)} %eq.3, f32[96,256]{1,0:T(8,128)S(1)} %collective-permute-done.1), kind=kLoop, calls=%fused_computation | loop fusion | flops 49152 | bytes 393217 | tf_op jit(solution)/shard_map/jit(_where)/select_n | solution.py:256
  15.6 0.0 copy-start.1
  15.7 0.0 copy-done
  15.7 0.6 %copy-done.1 = f32[96,256]{1,0:T(8,128)} copy-done((f32[96,256]{1,0:T(8,128)}, f32[96,256]{1,0:T(8,128)S(1)}, u32[]{:S(2)}) %copy-start.1) | copy-done | bytes 98328
  16.3 4.8 %collective-permute-start.3 = (f32[96,256]{1,0:T(8,128)S(1)}, f32[96,256]{1,0:T(8,128)S(1)}, u32[]{:S(2)}, u32[]{:S(2)}) collective-permute-start(f32[96,256]{1,0:T(8,128)S(1)} %get-tuple-element.6), channel_id=1, source_target_pairs={{4,0},{6,2},{8,4},{10,6},{12,8},{14,10},{16,12},{18,14},{20,16},{2... | collective-permute-start | bytes 294920 | tf_op jit(solution)/shard_map/ppermute | solution.py:235
  21.0 0.0 collective-permute-start.2
  21.0 2.4 %collective-permute-done.3.refs_2_ = f32[96,256]{1,0:T(8,128)S(1)} collective-permute-done((f32[96,256]{1,0:T(8,128)S(1)}, f32[96,256]{1,0:T(8,128)S(1)}, u32[]{:S(2)}, u32[]{:S(2)}) %collective-permute-start.3) | collective-permute-done | bytes 98336 | tf_op jit(solution)/shard_map/ppermute | solution.py:235
  23.4 0.0 copy-start.3
  23.4 4.9 %collective-permute-done.2.refs_1_ = f32[96,256]{1,0:T(8,128)S(1)} collective-permute-done((f32[96,256]{1,0:T(8,128)S(1)}, f32[96,256]{1,0:T(8,128)S(1)}, u32[]{:S(2)}, u32[]{:S(2)}) %collective-permute-start.2) | collective-permute-done | bytes 98336 | tf_op jit(solution)/shard_map/ppermute | solution.py:235
  28.3 0.0 copy-done.3
  28.3 0.6 %copy-done.4 = f32[96,256]{1,0:T(8,128)} copy-done((f32[96,256]{1,0:T(8,128)}, f32[96,256]{1,0:T(8,128)S(1)}, u32[]{:S(2)}) %copy-start.4) | copy-done | bytes 98328
  29.0 1.9 %apply_window.1 = (f32[32,256]{1,0:T(8,128)}, f32[1,2,2,2]{3,2,1,0:T(2,128)}) custom-call(f32[2]{0:T(128)} %pad_maximum_fusion.phase_ref, f32[96,256]{1,0:T(8,128)} %copy-done.1, f32[96,256]{1,0:T(8,128)} %copy-done.4, f32[96,256]{1,0:T(8,128)} %copy-done.3, f32[144,256]{1,0:T(8,128)} %local_fields.1.refs_0_.refs_3_, f32[144,256]{1,0:T(8,128)} %copy-done.2), custom_call_target="tpu_custom_call" | custom-call | tf_op jit(solution)/shard_map/apply_window/pallas_call | solution.py:221
  (3 shorter events, 0.0 us)
Async XLA Ops:
  3.8 7.1 %collective-permute-start = (f32[144,256]{1,0:T(8,128)}, f32[144,256]{1,0:T(8,128)S(1)}, u32[]{:S(2)}, u32[]{:S(2)}) collective-permute-start(f32[144,256]{1,0:T(8,128)} %local_fields.1.refs_0_.refs_3_), channel_id=1, source_target_pairs={{1,0},{0,1},{3,2},{2,3},{5,4},{4,5},{7,6},{6,7},{9,8},{8,9},{11,10... | collective-permute-start | bytes 442376 | tf_op jit(solution)/shard_map/ppermute | solution.py:235
  6.9 0.7 %copy-start.5 = (s32[16]{0:T(128)S(1)}, s32[16]{0:T(128)}, u32[]{:S(2)}) copy-start(s32[16]{0:T(128)} %param.9) | copy-start | bytes 196
  10.9 0.6 %copy-start.2 = (f32[144,256]{1,0:T(8,128)}, f32[144,256]{1,0:T(8,128)S(1)}, u32[]{:S(2)}) copy-start(f32[144,256]{1,0:T(8,128)S(1)} %collective-permute-done.refs_1_.refs_4_) | copy-start | bytes 442372
  13.2 1.5 %collective-permute-start.1 = (f32[96,256]{1,0:T(8,128)}, f32[96,256]{1,0:T(8,128)S(1)}, u32[]{:S(2)}, u32[]{:S(2)}) collective-permute-start(f32[96,256]{1,0:T(8,128)} %join_slabs.1), channel_id=1, source_target_pairs={{0,2},{2,0},{4,6},{6,4},{8,10},{10,8},{12,14},{14,12},{16,18},{18,... | collective-permute-start | bytes 294920 | tf_op jit(solution)/shard_map/ppermute | solution.py:252
  13.2 2.4 %copy-start = (f32[96,256]{1,0:T(8,128)S(1)}, f32[96,256]{1,0:T(8,128)}, u32[]{:S(2)}) copy-start(f32[96,256]{1,0:T(8,128)} %join_slabs.1) | copy-start | bytes 294916
  15.6 0.6 %copy-start.1 = (f32[96,256]{1,0:T(8,128)}, f32[96,256]{1,0:T(8,128)S(1)}, u32[]{:S(2)}) copy-start(f32[96,256]{1,0:T(8,128)S(1)} %get-tuple-element.7.refs_0_) | copy-start | bytes 294916
  16.3 7.1 %collective-permute-start.3 = (f32[96,256]{1,0:T(8,128)S(1)}, f32[96,256]{1,0:T(8,128)S(1)}, u32[]{:S(2)}, u32[]{:S(2)}) collective-permute-start(f32[96,256]{1,0:T(8,128)S(1)} %get-tuple-element.6), channel_id=1, source_target_pairs={{4,0},{6,2},{8,4},{10,6},{12,8},{14,10},{16,12},{18,14},{20,16},{2... | collective-permute-start | bytes 294920 | tf_op jit(solution)/shard_map/ppermute | solution.py:235
  21.0 7.3 %collective-permute-start.2 = (f32[96,256]{1,0:T(8,128)S(1)}, f32[96,256]{1,0:T(8,128)S(1)}, u32[]{:S(2)}, u32[]{:S(2)}) collective-permute-start(f32[96,256]{1,0:T(8,128)S(1)} %broadcast_select_fusion.1), channel_id=1, source_target_pairs={{28,0},{30,2},{0,4},{2,6},{4,8},{6,10},{8,12},{10,14},{12,16},{14,... | collective-permute-start | bytes 294920 | tf_op jit(solution)/shard_map/ppermute | solution.py:235
  23.4 4.9 %copy-start.3 = (f32[96,256]{1,0:T(8,128)}, f32[96,256]{1,0:T(8,128)S(1)}, u32[]{:S(2)}) copy-start(f32[96,256]{1,0:T(8,128)S(1)} %collective-permute-done.3.refs_2_) | copy-start | bytes 294916
  28.3 0.6 %copy-start.4 = (f32[96,256]{1,0:T(8,128)}, f32[96,256]{1,0:T(8,128)S(1)}, u32[]{:S(2)}) copy-start(f32[96,256]{1,0:T(8,128)S(1)} %collective-permute-done.2.refs_1_) | copy-start | bytes 294916

commit v2 on v1

--- a/solution.py
+++ b/solution.py
@@ -16,7 +16,8 @@
 
 VMEM = pl.BlockSpec(memory_space=pltpu.VMEM)
 SMEM = pl.BlockSpec(memory_space=pltpu.SMEM)
-ANY = pl.BlockSpec(memory_space=pl.ANY)
+HBM = pl.BlockSpec(memory_space=pltpu.HBM)
+PARAMS = pltpu.CompilerParams(vmem_limit_bytes=4 * 1024 * 1024)
 
 
 def halves(field):
@@ -38,7 +39,7 @@
     return ar * br + ai * bi, ai * br - ar * bi
 
 
-def gather_kernel(planes, index_ref, occupied_ref, psi_hbm, orb_hbm, pack_ref, orb, sems):
+def gather_kernel(planes, index_ref, occupied_hbm, psi_hbm, orb_hbm, pack_ref, orb, occupied_ref, sems):
     rows = 2 * planes
     field_rows = FIELDS * planes
     end_rows = 4 * BLOCK
@@ -48,6 +49,9 @@
         load.start()
     keep = pltpu.make_async_copy(psi_hbm, pack_ref.at[pl.ds(field_rows + end_rows, psi_rows)], sems.at[CX])
     keep.start()
+    masks = pltpu.make_async_copy(occupied_hbm, occupied_ref, sems.at[CX + 1])
+    masks.start()
+    masks.wait()
     first = index_ref[0] * BLOCK
     weights = [occupied_ref[0, first + m].astype(jnp.float32) for m in range(BLOCK)]
     for load in loads:
@@ -84,6 +88,31 @@
     keep.wait()
 
 
+def phase_of(kpoint, place, cycle):
+    def body(place_ref, kpoint_hbm, out_ref, labels, sem):
+        load = pltpu.make_async_copy(kpoint_hbm, labels, sem)
+        load.start()
+        load.wait()
+        label = labels[place_ref[0]].astype(jnp.float32)
+        angle = jnp.full((8, CY), label * (2.0 * math.pi / cycle), jnp.float32)
+        out_ref[pl.ds(0, 8), :] = jnp.cos(angle)
+        out_ref[pl.ds(8, 8), :] = jnp.sin(angle)
+
+    return pl.pallas_call(
+        body,
+        out_shape=jax.ShapeDtypeStruct((16, CY), jnp.float32),
+        in_specs=[SMEM, HBM],
+        out_specs=VMEM,
+        scratch_shapes=[pltpu.SMEM(kpoint.shape, jnp.int32), pltpu.SemaphoreType.DMA],
+        compiler_params=PARAMS,
+        name="phase",
+    )(place.reshape(1), kpoint)
+
+
+def phase_rows(ref):
+    return [jnp.concatenate([ref[pl.ds(8 * i, 1), :]] * CX, axis=1) for i in range(2)]
+
+
 def gather(block_index, occupied, psi, orb, planes):
     psi_rows = psi.shape[0]
     total = FIELDS * planes + 4 * BLOCK + psi_rows
@@ -94,9 +123,14 @@
     return pl.pallas_call(
         body,
         out_shape=jax.ShapeDtypeStruct((total, CELLS), jnp.float32),
-        in_specs=[SMEM, SMEM, ANY, ANY],
+        in_specs=[SMEM, HBM, HBM, HBM],
         out_specs=VMEM,
-        scratch_shapes=[pltpu.VMEM((CX, orb.shape[0], CY), jnp.float32), pltpu.SemaphoreType.DMA((CX + 1,))],
+        scratch_shapes=[
+            pltpu.VMEM((CX, orb.shape[0], CY), jnp.float32),
+            pltpu.SMEM(occupied.shape, jnp.int32),
+            pltpu.SemaphoreType.DMA((CX + 2,)),
+        ],
+        compiler_params=PARAMS,
         name="local_fields",
     )(block_index, occupied, psi, orb)
 
@@ -107,7 +141,7 @@
 
     def body(phase_ref, *refs):
         ins, out = refs[:count], refs[count]
-        cosine, sine = phase_ref[0], phase_ref[1]
+        cosine, sine = phase_rows(phase_ref)
         last = lax.broadcasted_iota(jnp.int32, (planes, CELLS), 0) == planes - 1
 
         def end(ref, e, c):
@@ -127,8 +161,9 @@
     return pl.pallas_call(
         body,
         out_shape=jax.ShapeDtypeStruct((count * field_rows, CELLS), jnp.float32),
-        in_specs=[SMEM] + [VMEM] * count,
+        in_specs=[VMEM] + [VMEM] * count,
         out_specs=VMEM,
+        compiler_params=PARAMS,
         name="join_slabs",
     )(phase, *packs)
 
@@ -142,7 +177,7 @@
     def body(phase_ref, *refs):
         part_refs, ins = refs[: len(parts)], refs[len(parts) : len(parts) + count]
         out_ref, tile_ref = refs[len(parts) + count :]
-        cosine, sine = phase_ref[0], phase_ref[1]
+        cosine, sine = phase_rows(phase_ref)
         row = lax.broadcasted_iota(jnp.int32, (planes, CELLS), 0)
 
         def window(d, i, offset=0):
@@ -224,8 +259,9 @@
             jax.ShapeDtypeStruct((2 * bands * planes, CELLS), jnp.float32),
             jax.ShapeDtypeStruct((1, bands, bands, 2), jnp.float32),
         ),
-        in_specs=[SMEM] + [VMEM] * (len(parts) + count),
+        in_specs=[VMEM] + [VMEM] * (len(parts) + count),
         out_specs=(VMEM, VMEM),
+        compiler_params=PARAMS,
         name="apply_window",
     )(phase, *parts, *packs)
 
@@ -242,9 +278,9 @@
     psi = targets.reshape(2 * bands * planes, CELLS)
     orb = orbitals.reshape(-1, CELLS)
 
-    angle = lax.dynamic_index_in_dim(kpoint, place, 0, False).astype(jnp.float32) * (2.0 * math.pi / cycle)
-    phase = jnp.stack([jnp.cos(angle), jnp.sin(angle)])
-
+    phase = phase_of(kpoint, place, cycle)
+
+    occupied, psi, orb = [pltpu.with_memory_space_constraint(v, pltpu.HBM) for v in (occupied, psi, orb)]
     own = gather(block_index, occupied, psi, orb, planes)
     packs = [own] + [shift(own, "slab", d) for d in range(1, slabs)]
     mine = join(phase, packs, planes)
@@ -252,9 +288,9 @@
     other = lax.ppermute(mine, "kring", [(i, i ^ 1) for i in range(cycle)])
     pair = mine + other
     even = lax.rem(place, 2) == 0
+    right = shift(jnp.where(even, mine, pair), "kring", 2)
     left = shift(jnp.where(even, pair, mine), "kring", -2)
-    right = shift(jnp.where(even, mine, pair), "kring", 2)
-    exchange, tile = apply(phase, [pair, left, right], packs, planes, bands)
+    exchange, tile = apply(phase, [pair, right, left], packs, planes, bands)
     return exchange.reshape(targets.shape), tile
 
 

time: 31.2 us -> 20.3 us (0.65)
  Pallas kernels: 6.13 us -> 2.67 us
  waiting for transfers between devices: 10.2 us -> 7.49 us
  local copies, waits for them, and re-layouts: 3.12 us -> 0.65 us
  other arithmetic: 1.57 us -> 0.03 us
  between operations: 2.13 us -> 1.32 us
    ppermute x3, waiting for transfers between devices: 8.67 us -> 6.21 us  [shift(): lax.ppermute(value, axis, [((i + distance) % count, i) for i in range(cou...]
    unnamed x12 -> x2, local copies, waits for them, and re-layouts: 2.54 us -> 0.65 us
    pallas_call x1, Pallas kernels: 1.66 us -> 0.03 us  [join(): pl.pallas_call(body, out_shape=jax.ShapeDtypeStruct((count * field_rows,...]
    pallas_call x1, Pallas kernels: 2.54 us -> 1.24 us  [gather(): pl.pallas_call(body, out_shape=jax.ShapeDtypeStruct((total, CELLS), jnp.f...]
    pallas_call x1, Pallas kernels: 1.93 us -> 0.81 us  [apply(): pl.pallas_call(body, out_shape=(jax.ShapeDtypeStruct((2 * bands * planes,...]
    select_n x1, other arithmetic: 0.91 us -> 0.01 us  [body(): right = shift(jnp.where(even, mine, pair), 'kring', 2)]
    another operation x1 -> x0, other arithmetic: 0.65 us -> none  [body(): phase = jnp.stack([jnp.cos(angle), jnp.sin(angle)])]
    pallas_call x0 -> x1, Pallas kernels: none -> 0.6 us  [phase_of(): pl.pallas_call(body, out_shape=jax.ShapeDtypeStruct((16, CY), jnp.float32...]
  transfers between devices with their start and end apart: 4 -> 4, of which waited for: 4 -> 4; matrix products, arithmetic and copies ran while one was open for 4% -> 0% of each run, Pallas kernels for 0% -> 3%
where the time goes in v2:
time: 20.3 us; the launch traced here: 20.1 us
  starting transfers between devices  7.97 us (39%)
  waiting for transfers between devices  7.49 us (37%)
  Pallas kernels  2.67 us (13%)
  between operations  1.32 us (7%)
  local copies, waits for them, and re-layouts  0.65 us (3%)
    ppermute x3, starting transfers between devices, shift(): lax.ppermute(value, axis, [((i + distance) % count, i) for i in range(cou...  7.9 us
    ppermute x3, waiting for transfers between devices, shift(): lax.ppermute(value, axis, [((i + distance) % count, i) for i in range(cou...  6.21 us
    ppermute x1, waiting for transfers between devices, body(): other = lax.ppermute(mine, 'kring', [(i, i ^ 1) for i in range(cycle)])  1.28 us
    pallas_call x1, Pallas kernels, gather(): pl.pallas_call(body, out_shape=jax.ShapeDtypeStruct((total, CELLS), jnp.f...  1.24 us
    pallas_call x1, Pallas kernels, apply(): pl.pallas_call(body, out_shape=(jax.ShapeDtypeStruct((2 * bands * planes,...  0.81 us
    unnamed x2, local copies, waits for them, and re-layouts  0.65 us
    pallas_call x1, Pallas kernels, phase_of(): pl.pallas_call(body, out_shape=jax.ShapeDtypeStruct((16, CY), jnp.float32...  0.6 us
  transfers between devices with their start and end apart: 4, of which 4 were waited for; matrix products, arithmetic and copies ran while one was open for 0% of the time, Pallas kernels for 3%

profile of v2, /device:TPU:0, one launch (start us, length us, event | category | flops | bytes accessed | tf_op | source)
XLA Modules:
  0.0 20.1 jit_solution(2006472367117919261)
XLA Ops:
  1.3 1.2 %local_fields.1.refs_0_.refs_3_ = f32[144,256]{1,0:T(8,128)S(1)} custom-call(s32[1]{0:T(128)S(6)} %copy.7.refs_0_, s32[1,32]{1,0:T(1,128)} %refs_1_.1, f32[32,256]{1,0:T(8,128)} %bitcast.5, f32[512,256]{1,0:T(8,128)} %bitcast.4), custom_call_target="tpu_custom_call" | custom-call | tf_op jit(solution)/shard_map/local_fields/pallas_call | solution.py:123
  2.5 3.0 %collective-permute-start = (f32[144,256]{1,0:T(8,128)S(1)}, f32[144,256]{1,0:T(8,128)S(1)}, u32[]{:S(2)}, u32[]{:S(2)}) collective-permute-start(f32[144,256]{1,0:T(8,128)S(1)} %local_fields.1.refs_0_.refs_3_), channel_id=1, source_target_pairs={{1,0},{0,1},{3,2},{2,3},{5,4},{4,5},{7,6},{6,7},{9,8},{8,9},{11,10... | collective-permute-start | bytes 442376 | tf_op jit(solution)/shard_map/ppermute | solution.py:271
  5.6 0.0 copy-start
  5.6 0.7 %copy-done = s32[16]{0:T(128)S(1)} copy-done((s32[16]{0:T(128)S(1)}, s32[16]{0:T(128)}, u32[]{:S(2)}) %copy-start) | copy-done | bytes 88
  6.2 0.6 %phase.1.phase_ref = f32[16,128]{1,0:T(8,128)S(1)} custom-call(s32[1]{0:T(128)} %bitcast.place_ref, s32[16]{0:T(128)S(1)} %copy-done), custom_call_target="tpu_custom_call" | custom-call | tf_op jit(solution)/shard_map/phase/pallas_call | solution.py:101
  6.8 2.6 %collective-permute-done.refs_1_.refs_4_ = f32[144,256]{1,0:T(8,128)S(1)} collective-permute-done((f32[144,256]{1,0:T(8,128)S(1)}, f32[144,256]{1,0:T(8,128)S(1)}, u32[]{:S(2)}, u32[]{:S(2)}) %collective-permute-start) | collective-permute-done | bytes 147488 | tf_op jit(solution)/shard_map/ppermute | solution.py:271
  9.4 0.1 collective-permute-start.1
  9.5 1.3 %collective-permute-done.1 = f32[96,256]{1,0:T(8,128)S(1)} collective-permute-done((f32[96,256]{1,0:T(8,128)S(1)}, f32[96,256]{1,0:T(8,128)S(1)}, u32[]{:S(2)}, u32[]{:S(2)}) %collective-permute-start.1) | collective-permute-done | bytes 98336 | tf_op jit(solution)/shard_map/ppermute | solution.py:288
  10.8 1.8 %collective-permute-start.3 = (f32[96,256]{1,0:T(8,128)S(1)}, f32[96,256]{1,0:T(8,128)S(1)}, u32[]{:S(2)}, u32[]{:S(2)}) collective-permute-start(f32[96,256]{1,0:T(8,128)S(1)} %get-tuple-element.6), channel_id=1, source_target_pairs={{28,0},{30,2},{0,4},{2,6},{4,8},{6,10},{8,12},{10,14},{12,16},{14,... | collective-permute-start | bytes 294920 | tf_op jit(solution)/shard_map/ppermute | solution.py:271
  12.6 3.1 %collective-permute-start.2 = (f32[96,256]{1,0:T(8,128)S(1)}, f32[96,256]{1,0:T(8,128)S(1)}, u32[]{:S(2)}, u32[]{:S(2)}) collective-permute-start(f32[96,256]{1,0:T(8,128)S(1)} %broadcast_select_fusion.1), channel_id=1, source_target_pairs={{4,0},{6,2},{8,4},{10,6},{12,8},{14,10},{16,12},{18,14},{20,16},{2... | collective-permute-start | bytes 294920 | tf_op jit(solution)/shard_map/ppermute | solution.py:271
  15.7 3.2 %collective-permute-done.3.refs_2_ = f32[96,256]{1,0:T(8,128)S(1)} collective-permute-done((f32[96,256]{1,0:T(8,128)S(1)}, f32[96,256]{1,0:T(8,128)S(1)}, u32[]{:S(2)}, u32[]{:S(2)}) %collective-permute-start.3) | collective-permute-done | bytes 98336 | tf_op jit(solution)/shard_map/ppermute | solution.py:271
  18.9 0.5 %collective-permute-done.2.refs_1_ = f32[96,256]{1,0:T(8,128)S(1)} collective-permute-done((f32[96,256]{1,0:T(8,128)S(1)}, f32[96,256]{1,0:T(8,128)S(1)}, u32[]{:S(2)}, u32[]{:S(2)}) %collective-permute-start.2) | collective-permute-done | bytes 98336 | tf_op jit(solution)/shard_map/ppermute | solution.py:271
  19.3 0.8 %apply_window.1 = (f32[32,256]{1,0:T(8,128)}, f32[1,2,2,2]{3,2,1,0:T(2,128)}) custom-call(f32[16,128]{1,0:T(8,128)S(1)} %phase.1.phase_ref, f32[96,256]{1,0:T(8,128)S(1)} %get-tuple-element.7.refs_0_, f32[96,256]{1,0:T(8,128)S(1)} %collective-permute-done.2.refs_1_, f32[96,256]{1,0:T(8,128)S(1)} %collective-permute-done.3.refs_2_, ...), custom_call_target="tpu_custom_call" | custom-call | tf_op jit(solution)/shard_map/apply_window/pallas_call | solution.py:256
  (3 shorter events, 0.1 us)
Async XLA Ops:
  2.5 6.9 %collective-permute-start = (f32[144,256]{1,0:T(8,128)S(1)}, f32[144,256]{1,0:T(8,128)S(1)}, u32[]{:S(2)}, u32[]{:S(2)}) collective-permute-start(f32[144,256]{1,0:T(8,128)S(1)} %local_fields.1.refs_0_.refs_3_), channel_id=1, source_target_pairs={{1,0},{0,1},{3,2},{2,3},{5,4},{4,5},{7,6},{6,7},{9,8},{8,9},{11,10... | collective-permute-start | bytes 442376 | tf_op jit(solution)/shard_map/ppermute | solution.py:271
  5.6 0.7 %copy-start = (s32[16]{0:T(128)S(1)}, s32[16]{0:T(128)}, u32[]{:S(2)}) copy-start(s32[16]{0:T(128)} %kpoint_hbm.1) | copy-start | bytes 196
  9.4 1.4 %collective-permute-start.1 = (f32[96,256]{1,0:T(8,128)S(1)}, f32[96,256]{1,0:T(8,128)S(1)}, u32[]{:S(2)}, u32[]{:S(2)}) collective-permute-start(f32[96,256]{1,0:T(8,128)S(1)} %join_slabs.1), channel_id=1, source_target_pairs={{0,2},{2,0},{4,6},{6,4},{8,10},{10,8},{12,14},{14,12},{16,18},{18,... | collective-permute-start | bytes 294920 | tf_op jit(solution)/shard_map/ppermute | solution.py:288
  10.8 8.0 %collective-permute-start.3 = (f32[96,256]{1,0:T(8,128)S(1)}, f32[96,256]{1,0:T(8,128)S(1)}, u32[]{:S(2)}, u32[]{:S(2)}) collective-permute-start(f32[96,256]{1,0:T(8,128)S(1)} %get-tuple-element.6), channel_id=1, source_target_pairs={{28,0},{30,2},{0,4},{2,6},{4,8},{6,10},{8,12},{10,14},{12,16},{14,... | collective-permute-start | bytes 294920 | tf_op jit(solution)/shard_map/ppermute | solution.py:271
  12.6 6.7 %collective-permute-start.2 = (f32[96,256]{1,0:T(8,128)S(1)}, f32[96,256]{1,0:T(8,128)S(1)}, u32[]{:S(2)}, u32[]{:S(2)}) collective-permute-start(f32[96,256]{1,0:T(8,128)S(1)} %broadcast_select_fusion.1), channel_id=1, source_target_pairs={{4,0},{6,2},{8,4},{10,6},{12,8},{14,10},{16,12},{18,14},{20,16},{2... | collective-permute-start | bytes 294920 | tf_op jit(solution)/shard_map/ppermute | solution.py:271

commit v3 on v2

--- a/solution.py
+++ b/solution.py
@@ -12,6 +12,7 @@
 CELLS = CX * CY
 BLOCK = 16
 FIELDS = 6
+CHUNKS = 2
 DIAG = 7.0
 
 VMEM = pl.BlockSpec(memory_space=pltpu.VMEM)
@@ -39,53 +40,82 @@
     return ar * br + ai * bi, ai * br - ar * bi
 
 
-def gather_kernel(planes, index_ref, occupied_hbm, psi_hbm, orb_hbm, pack_ref, orb, occupied_ref, sems):
+def gather_kernel(planes, index_ref, occupied_hbm, psi_hbm, orb_hbm, pack_ref, psi_ref, orb, occupied_ref, sems):
     rows = 2 * planes
     field_rows = FIELDS * planes
-    end_rows = 4 * BLOCK
-    psi_rows = psi_hbm.shape[0]
-    loads = [pltpu.make_async_copy(orb_hbm.at[:, pl.ds(x * CY, CY)], orb.at[x], sems.at[x]) for x in range(CX)]
-    for load in loads:
-        load.start()
-    keep = pltpu.make_async_copy(psi_hbm, pack_ref.at[pl.ds(field_rows + end_rows, psi_rows)], sems.at[CX])
+    chunk = BLOCK // CHUNKS
+    masks = pltpu.make_async_copy(occupied_hbm, occupied_ref, sems.at[0])
+    masks.start()
+    first = index_ref[0] * BLOCK
+    loads = []
+    for g in range(CHUNKS):
+        source = pl.ds(pl.multiple_of((first + g * chunk) * rows, 8), chunk * rows)
+        target = pl.ds(g * chunk * rows, chunk * rows)
+        group = [
+            pltpu.make_async_copy(
+                orb_hbm.at[source, pl.ds(x * CY, CY)], orb.at[x, target], sems.at[2 + g * CX + x]
+            )
+            for x in range(CX)
+        ]
+        for load in group:
+            load.start()
+        loads.append(group)
+    keep = pltpu.make_async_copy(psi_hbm, psi_ref, sems.at[1])
     keep.start()
-    masks = pltpu.make_async_copy(occupied_hbm, occupied_ref, sems.at[CX + 1])
-    masks.start()
     masks.wait()
-    first = index_ref[0] * BLOCK
     weights = [occupied_ref[0, first + m].astype(jnp.float32) for m in range(BLOCK)]
-    for load in loads:
-        load.wait()
-    dens = jnp.zeros((planes, CELLS), jnp.float32)
-    dx_re = jnp.zeros((planes, CY), jnp.float32)
-    dx_im = jnp.zeros((planes, CY), jnp.float32)
-    dy_re, dy_im, dz_re, dz_im = dens, dens, dens, dens
-    for m in range(BLOCK):
-        base = pl.multiple_of((first + m) * rows, 8)
-        re = jnp.concatenate([orb[x, pl.ds(base, planes), :] for x in range(CX)], axis=1) * weights[m]
-        im = jnp.concatenate([orb[x, pl.ds(base + planes, planes), :] for x in range(CX)], axis=1) * weights[m]
-        dens = dens + re * re + im * im
-        re0, re1 = halves(re)
-        im0, im1 = halves(im)
-        part = bond(re0, im0, re1, im1)
-        dx_re, dx_im = dx_re + part[0], dx_im + part[1]
-        part = bond(re, im, turn(re, 1), turn(im, 1))
-        dy_re, dy_im = dy_re + part[0], dy_im + part[1]
-        part = bond(re, im, pltpu.roll(re, planes - 1, 0), pltpu.roll(im, planes - 1, 0))
-        dz_re, dz_im = dz_re + part[0], dz_im + part[1]
-    for i, field in enumerate((dens, jnp.concatenate([dx_re, dx_im], axis=1), dy_re, dy_im, dz_re, dz_im)):
-        pack_ref[pl.ds(i * planes, planes), :] = field
     band = lax.broadcasted_iota(jnp.int32, (BLOCK, 1), 0)
     column = jnp.zeros((BLOCK, 1), jnp.float32)
     for m in range(BLOCK):
         column = jnp.where(band == m, weights[m], column)
+    none = jnp.zeros((planes, CY), jnp.float32)
+    dens, dy_re, dy_im, dz_re, dz_im = [[none] * CX for _ in range(5)]
+    dx_re, dx_im = none, none
+    for m in range(BLOCK):
+        if m % chunk == 0:
+            for load in loads[m // chunk]:
+                load.wait()
+        re = [orb[x, pl.ds(m * rows, planes), :] * weights[m] for x in range(CX)]
+        im = [orb[x, pl.ds(m * rows + planes, planes), :] * weights[m] for x in range(CX)]
+        part = bond(re[0], im[0], re[1], im[1])
+        dx_re, dx_im = dx_re + part[0], dx_im + part[1]
+        for x in range(CX):
+            dens[x] = dens[x] + (re[x] * re[x] + im[x] * im[x])
+            part = bond(re[x], im[x], pltpu.roll(re[x], CY - 1, 1), pltpu.roll(im[x], CY - 1, 1))
+            dy_re[x], dy_im[x] = dy_re[x] + part[0], dy_im[x] + part[1]
+            part = bond(re[x], im[x], pltpu.roll(re[x], planes - 1, 0), pltpu.roll(im[x], planes - 1, 0))
+            dz_re[x], dz_im[x] = dz_re[x] + part[0], dz_im[x] + part[1]
+    for i, field in enumerate((dens, (dx_re, dx_im), dy_re, dy_im, dz_re, dz_im)):
+        for x in range(CX):
+            pack_ref[pl.ds(i * planes, planes), pl.ds(x * CY, CY)] = field[x]
     for e, plane in enumerate((0, planes - 1)):
         for c in range(2):
-            start = first * rows + c * planes + plane
             for x in range(CX):
-                ends = orb[x, pl.ds(start, BLOCK, stride=rows), :] * column
+                ends = orb[x, pl.ds(c * planes + plane, BLOCK, stride=rows), :] * column
                 pack_ref[pl.ds(field_rows + (2 * e + c) * BLOCK, BLOCK), pl.ds(x * CY, CY)] = ends
     keep.wait()
+
+
+def gather(block_index, occupied, psi, orb, planes):
+    def body(*refs):
+        gather_kernel(planes, *refs)
+
+    return pl.pallas_call(
+        body,
+        out_shape=(
+            jax.ShapeDtypeStruct((FIELDS * planes + 4 * BLOCK, CELLS), jnp.float32),
+            jax.ShapeDtypeStruct(psi.shape, jnp.float32),
+        ),
+        in_specs=[SMEM, HBM, HBM, HBM],
+        out_specs=(VMEM, VMEM),
+        scratch_shapes=[
+            pltpu.VMEM((CX, 2 * planes * BLOCK, CY), jnp.float32),
+            pltpu.SMEM(occupied.shape, jnp.int32),
+            pltpu.SemaphoreType.DMA((2 + CX * CHUNKS,)),
+        ],
+        compiler_params=PARAMS,
+        name="local_fields",
+    )(block_index, occupied, psi, orb)
 
 
 def phase_of(kpoint, place, cycle):
@@ -113,26 +143,22 @@
     return [jnp.concatenate([ref[pl.ds(8 * i, 1), :]] * CX, axis=1) for i in range(2)]
 
 
-def gather(block_index, occupied, psi, orb, planes):
-    psi_rows = psi.shape[0]
-    total = FIELDS * planes + 4 * BLOCK + psi_rows
+def stack(targets):
+    rows = targets[0].shape[0]
 
     def body(*refs):
-        gather_kernel(planes, *refs)
-
-    return pl.pallas_call(
-        body,
-        out_shape=jax.ShapeDtypeStruct((total, CELLS), jnp.float32),
-        in_specs=[SMEM, HBM, HBM, HBM],
+        for i, ref in enumerate(refs[:-1]):
+            refs[-1][pl.ds(i * rows, rows), :] = ref[...]
+
+    return pl.pallas_call(
+        body,
+        out_shape=jax.ShapeDtypeStruct((len(targets) * rows, CELLS), jnp.float32),
+        in_specs=[VMEM] * len(targets),
         out_specs=VMEM,
-        scratch_shapes=[
-            pltpu.VMEM((CX, orb.shape[0], CY), jnp.float32),
-            pltpu.SMEM(occupied.shape, jnp.int32),
-            pltpu.SemaphoreType.DMA((CX + 2,)),
-        ],
-        compiler_params=PARAMS,
-        name="local_fields",
-    )(block_index, occupied, psi, orb)
+        compiler_params=PARAMS,
+        cost_estimate=pl.CostEstimate(flops=1000000000, bytes_accessed=0, transcendentals=0),
+        name="stack_targets",
+    )(*targets)
 
 
 def join(phase, packs, planes):
@@ -168,15 +194,13 @@
     )(phase, *packs)
 
 
-def apply(phase, parts, packs, planes, bands):
-    count = len(packs)
+def apply(phase, parts, targets, planes, bands, count):
     field_rows = FIELDS * planes
-    psi_start = field_rows + 4 * BLOCK
     scale = 1.0 / (count * planes * CELLS)
 
     def body(phase_ref, *refs):
-        part_refs, ins = refs[: len(parts)], refs[len(parts) : len(parts) + count]
-        out_ref, tile_ref = refs[len(parts) + count :]
+        part_refs, ins = refs[: len(parts)], refs[len(parts)]
+        out_ref, tile_ref = refs[len(parts) + 1 :]
         cosine, sine = phase_rows(phase_ref)
         row = lax.broadcasted_iota(jnp.int32, (planes, CELLS), 0)
 
@@ -188,7 +212,7 @@
             return total
 
         def psi_at(d, b, c):
-            return ins[d % count][pl.ds(psi_start + (2 * b + c) * planes, planes), :]
+            return ins[pl.ds(((d % count) * 2 * bands + 2 * b + c) * planes, planes), :]
 
         def above(d, field):
             return jnp.where(row == planes - 1, pltpu.roll(field(d + 1), planes - 1, 0), pltpu.roll(field(d), planes - 1, 0))
@@ -259,11 +283,11 @@
             jax.ShapeDtypeStruct((2 * bands * planes, CELLS), jnp.float32),
             jax.ShapeDtypeStruct((1, bands, bands, 2), jnp.float32),
         ),
-        in_specs=[VMEM] + [VMEM] * (len(parts) + count),
+        in_specs=[VMEM] * (len(parts) + 2),
         out_specs=(VMEM, VMEM),
         compiler_params=PARAMS,
         name="apply_window",
-    )(phase, *parts, *packs)
+    )(phase, *parts, targets)
 
 
 def shift(value, axis, distance):
@@ -281,16 +305,18 @@
     phase = phase_of(kpoint, place, cycle)
 
     occupied, psi, orb = [pltpu.with_memory_space_constraint(v, pltpu.HBM) for v in (occupied, psi, orb)]
-    own = gather(block_index, occupied, psi, orb, planes)
+    own, psi = gather(block_index, occupied, psi, orb, planes)
     packs = [own] + [shift(own, "slab", d) for d in range(1, slabs)]
+    psis = [psi] + [shift(psi, "slab", d) for d in range(1, slabs)]
     mine = join(phase, packs, planes)
 
-    other = lax.ppermute(mine, "kring", [(i, i ^ 1) for i in range(cycle)])
-    pair = mine + other
+    left = shift(mine, "kring", -2)
+    right = shift(mine, "kring", 2)
     even = lax.rem(place, 2) == 0
-    right = shift(jnp.where(even, mine, pair), "kring", 2)
-    left = shift(jnp.where(even, pair, mine), "kring", -2)
-    exchange, tile = apply(phase, [pair, right, left], packs, planes, bands)
+    lacking = mine + jnp.where(even, right, left)
+    other = lax.ppermute(lacking, "kring", [(i, i ^ 1) for i in range(cycle)])
+    other, psis = lax.optimization_barrier((other, stack(psis)))
+    exchange, tile = apply(phase, [mine, left, right, other], psis, planes, bands, slabs)
     return exchange.reshape(targets.shape), tile
 
 

time: 20.3 us -> 18.8 us (0.926)
  waiting for transfers between devices: 7.49 us -> 4.43 us
  starting transfers between devices: 7.97 us -> 9.62 us
    ppermute x3 -> x4, waiting for transfers between devices: 6.21 us -> 4.05 us  [shift(): lax.ppermute(value, axis, [((i + distance) % count, i) for i in range(cou...]
    ppermute x3 -> x4, starting transfers between devices: 7.9 us -> 9.55 us  [shift(): lax.ppermute(value, axis, [((i + distance) % count, i) for i in range(cou...]
    ppermute x1, waiting for transfers between devices: 1.28 us -> 0.38 us  [body(): other = lax.ppermute(lacking, 'kring', [(i, i ^ 1) for i in range(cycle)])]
    pallas_call x1 -> x2, Pallas kernels: 1.24 us -> 1.18 us  [the longest x1 1.17 us: gather(): pl.pallas_call(body, out_shape=(jax.ShapeDtypeStruct((FIELDS * planes + 4...]
  transfers between devices with their start and end apart: 4 -> 5, of which waited for: 4 -> 5; matrix products, arithmetic and copies ran while one was open for 0% -> 0% of each run, Pallas kernels for 3% -> 3%
where the time goes in v3:
time: 18.8 us; the launch traced here: 18.6 us
  starting transfers between devices  9.62 us (51%)
  waiting for transfers between devices  4.43 us (24%)
  Pallas kernels  2.6 us (14%)
  between operations  1.31 us (7%)
  local copies, waits for them, and re-layouts  0.65 us (3%)
    ppermute x4, starting transfers between devices, shift(): lax.ppermute(value, axis, [((i + distance) % count, i) for i in range(cou...  9.55 us
    ppermute x4, waiting for transfers between devices, shift(): lax.ppermute(value, axis, [((i + distance) % count, i) for i in range(cou...  4.05 us
    pallas_call x1, Pallas kernels, gather(): pl.pallas_call(body, out_shape=(jax.ShapeDtypeStruct((FIELDS * planes + 4...  1.17 us
    pallas_call x1, Pallas kernels, apply(): pl.pallas_call(body, out_shape=(jax.ShapeDtypeStruct((2 * bands * planes,...  0.8 us
    unnamed x2, local copies, waits for them, and re-layouts  0.65 us
    pallas_call x1, Pallas kernels, phase_of(): pl.pallas_call(body, out_shape=jax.ShapeDtypeStruct((16, CY), jnp.float32...  0.6 us
    ppermute x1, waiting for transfers between devices, body(): other = lax.ppermute(lacking, 'kring', [(i, i ^ 1) for i in range(cycle)])  0.38 us
  transfers between devices with their start and end apart: 5, of which 5 were waited for; matrix products, arithmetic and copies ran while one was open for 0% of the time, Pallas kernels for 3%

profile of v3, /device:TPU:0, one launch (start us, length us, event | category | flops | bytes accessed | tf_op | source)
XLA Modules:
  0.0 18.6 jit_solution(10712821353380396192)
XLA Ops:
  1.3 1.2 %local_fields.1 = (f32[112,256]{1,0:T(8,128)S(1)}, f32[32,256]{1,0:T(8,128)S(1)}) custom-call(s32[1]{0:T(128)S(6)} %copy.7.refs_0_, s32[1,32]{1,0:T(1,128)} %refs_1_.1, f32[32,256]{1,0:T(8,128)} %bitcast.5, f32[512,256]{1,0:T(8,128)} %bitcast.4), custom_call_target="tpu_custom_call" | custom-call | tf_op jit(solution)/shard_map/local_fields/pallas_call | solution.py:103
  2.5 3.0 %collective-permute-start = (f32[112,256]{1,0:T(8,128)S(1)}, f32[112,256]{1,0:T(8,128)S(1)}, u32[]{:S(2)}, u32[]{:S(2)}) collective-permute-start(f32[112,256]{1,0:T(8,128)S(1)} %get-tuple-element.8.refs_0_), channel_id=1, source_target_pairs={{1,0},{0,1},{3,2},{2,3},{5,4},{4,5},{7,6},{6,7},{9,8},{8,9},{11,10... | collective-permute-start | bytes 344072 | tf_op jit(solution)/shard_map/ppermute | solution.py:295
  5.5 0.0 copy-start
  5.5 0.7 %copy-done = s32[16]{0:T(128)S(1)} copy-done((s32[16]{0:T(128)S(1)}, s32[16]{0:T(128)}, u32[]{:S(2)}) %copy-start) | copy-done | bytes 88
  6.1 0.6 %phase.1.phase_ref = f32[16,128]{1,0:T(8,128)S(1)} custom-call(s32[1]{0:T(128)} %bitcast.place_ref, s32[16]{0:T(128)S(1)} %copy-done), custom_call_target="tpu_custom_call" | custom-call | tf_op jit(solution)/shard_map/phase/pallas_call | solution.py:131
  6.7 1.9 %collective-permute-done.refs_1_ = f32[112,256]{1,0:T(8,128)S(1)} collective-permute-done((f32[112,256]{1,0:T(8,128)S(1)}, f32[112,256]{1,0:T(8,128)S(1)}, u32[]{:S(2)}, u32[]{:S(2)}) %collective-permute-start) | collective-permute-done | bytes 114720 | tf_op jit(solution)/shard_map/ppermute | solution.py:295
  8.7 1.8 %collective-permute-start.1 = (f32[96,256]{1,0:T(8,128)S(1)}, f32[96,256]{1,0:T(8,128)S(1)}, u32[]{:S(2)}, u32[]{:S(2)}) collective-permute-start(f32[96,256]{1,0:T(8,128)S(1)} %join_slabs.1.refs_0_), channel_id=1, source_target_pairs={{28,0},{30,2},{0,4},{2,6},{4,8},{6,10},{8,12},{10,14},{12,16},{14,... | collective-permute-start | bytes 294920 | tf_op jit(solution)/shard_map/ppermute | solution.py:295
  10.4 3.1 %collective-permute-start.2 = (f32[96,256]{1,0:T(8,128)S(1)}, f32[96,256]{1,0:T(8,128)S(1)}, u32[]{:S(2)}, u32[]{:S(2)}) collective-permute-start(f32[96,256]{1,0:T(8,128)S(1)} %join_slabs.1.refs_0_), channel_id=1, source_target_pairs={{4,0},{6,2},{8,4},{10,6},{12,8},{14,10},{16,12},{18,14},{20,16},{2... | collective-permute-start | bytes 294920 | tf_op jit(solution)/shard_map/ppermute | solution.py:295
  13.5 1.6 %collective-permute-start.4 = (f32[32,256]{1,0:T(8,128)S(1)}, f32[32,256]{1,0:T(8,128)S(1)}, u32[]{:S(2)}, u32[]{:S(2)}) collective-permute-start(f32[32,256]{1,0:T(8,128)S(1)} %get-tuple-element.9.refs_0_), channel_id=1, source_target_pairs={{1,0},{0,1},{3,2},{2,3},{5,4},{4,5},{7,6},{6,7},{9,8},{8,9},{11,10... | collective-permute-start | bytes 98312 | tf_op jit(solution)/shard_map/ppermute | solution.py:295
  15.2 1.0 %collective-permute-done.1.refs_1_ = f32[96,256]{1,0:T(8,128)S(1)} collective-permute-done((f32[96,256]{1,0:T(8,128)S(1)}, f32[96,256]{1,0:T(8,128)S(1)}, u32[]{:S(2)}, u32[]{:S(2)}) %collective-permute-start.1) | collective-permute-done | bytes 98336 | tf_op jit(solution)/shard_map/ppermute | solution.py:295
  16.2 0.3 %collective-permute-done.2.refs_2_ = f32[96,256]{1,0:T(8,128)S(1)} collective-permute-done((f32[96,256]{1,0:T(8,128)S(1)}, f32[96,256]{1,0:T(8,128)S(1)}, u32[]{:S(2)}, u32[]{:S(2)}) %collective-permute-start.2) | collective-permute-done | bytes 98336 | tf_op jit(solution)/shard_map/ppermute | solution.py:295
  16.5 0.1 collective-permute-start.3
  16.5 0.9 %collective-permute-done.4.refs_1_ = f32[32,256]{1,0:T(8,128)S(1)} collective-permute-done((f32[32,256]{1,0:T(8,128)S(1)}, f32[32,256]{1,0:T(8,128)S(1)}, u32[]{:S(2)}, u32[]{:S(2)}) %collective-permute-start.4) | collective-permute-done | bytes 32800 | tf_op jit(solution)/shard_map/ppermute | solution.py:295
  17.5 0.4 %collective-permute-done.3.refs_3_ = f32[96,256]{1,0:T(8,128)S(1)} collective-permute-done((f32[96,256]{1,0:T(8,128)S(1)}, f32[96,256]{1,0:T(8,128)S(1)}, u32[]{:S(2)}, u32[]{:S(2)}) %collective-permute-start.3) | collective-permute-done | bytes 98336 | tf_op jit(solution)/shard_map/ppermute | solution.py:317
  17.8 0.8 %apply_window.1 = (f32[32,256]{1,0:T(8,128)}, f32[1,2,2,2]{3,2,1,0:T(2,128)}) custom-call(f32[16,128]{1,0:T(8,128)S(1)} %phase.1.phase_ref, f32[96,256]{1,0:T(8,128)S(1)} %join_slabs.1.refs_0_, f32[96,256]{1,0:T(8,128)S(1)} %collective-permute-done.1.refs_1_, f32[96,256]{1,0:T(8,128)S(1)} %collective-permute-done.2.refs_2_, ...), custom_call_target="tpu_custom_call" | custom-call | tf_op jit(solution)/shard_map/apply_window/pallas_call | solution.py:280
  (3 shorter events, 0.1 us)
Async XLA Ops:
  2.5 6.2 %collective-permute-start = (f32[112,256]{1,0:T(8,128)S(1)}, f32[112,256]{1,0:T(8,128)S(1)}, u32[]{:S(2)}, u32[]{:S(2)}) collective-permute-start(f32[112,256]{1,0:T(8,128)S(1)} %get-tuple-element.8.refs_0_), channel_id=1, source_target_pairs={{1,0},{0,1},{3,2},{2,3},{5,4},{4,5},{7,6},{6,7},{9,8},{8,9},{11,10... | collective-permute-start | bytes 344072 | tf_op jit(solution)/shard_map/ppermute | solution.py:295
  5.5 0.7 %copy-start = (s32[16]{0:T(128)S(1)}, s32[16]{0:T(128)}, u32[]{:S(2)}) copy-start(s32[16]{0:T(128)} %kpoint_hbm.1) | copy-start | bytes 196
  8.7 7.5 %collective-permute-start.1 = (f32[96,256]{1,0:T(8,128)S(1)}, f32[96,256]{1,0:T(8,128)S(1)}, u32[]{:S(2)}, u32[]{:S(2)}) collective-permute-start(f32[96,256]{1,0:T(8,128)S(1)} %join_slabs.1.refs_0_), channel_id=1, source_target_pairs={{28,0},{30,2},{0,4},{2,6},{4,8},{6,10},{8,12},{10,14},{12,16},{14,... | collective-permute-start | bytes 294920 | tf_op jit(solution)/shard_map/ppermute | solution.py:295
  10.4 6.0 %collective-permute-start.2 = (f32[96,256]{1,0:T(8,128)S(1)}, f32[96,256]{1,0:T(8,128)S(1)}, u32[]{:S(2)}, u32[]{:S(2)}) collective-permute-start(f32[96,256]{1,0:T(8,128)S(1)} %join_slabs.1.refs_0_), channel_id=1, source_target_pairs={{4,0},{6,2},{8,4},{10,6},{12,8},{14,10},{16,12},{18,14},{20,16},{2... | collective-permute-start | bytes 294920 | tf_op jit(solution)/shard_map/ppermute | solution.py:295
  13.5 3.9 %collective-permute-start.4 = (f32[32,256]{1,0:T(8,128)S(1)}, f32[32,256]{1,0:T(8,128)S(1)}, u32[]{:S(2)}, u32[]{:S(2)}) collective-permute-start(f32[32,256]{1,0:T(8,128)S(1)} %get-tuple-element.9.refs_0_), channel_id=1, source_target_pairs={{1,0},{0,1},{3,2},{2,3},{5,4},{4,5},{7,6},{6,7},{9,8},{8,9},{11,10... | collective-permute-start | bytes 98312 | tf_op jit(solution)/shard_map/ppermute | solution.py:295
  16.5 1.4 %collective-permute-start.3 = (f32[96,256]{1,0:T(8,128)S(1)}, f32[96,256]{1,0:T(8,128)S(1)}, u32[]{:S(2)}, u32[]{:S(2)}) collective-permute-start(f32[96,256]{1,0:T(8,128)S(1)} %select_add_fusion), channel_id=1, source_target_pairs={{0,2},{2,0},{4,6},{6,4},{8,10},{10,8},{12,14},{14,12},{16,18},{18,... | collective-permute-start | bytes 294920 | tf_op jit(solution)/shard_map/ppermute | solution.py:317

commit v4 on v3

--- a/solution.py
+++ b/solution.py
@@ -12,7 +12,7 @@
 CELLS = CX * CY
 BLOCK = 16
 FIELDS = 6
-CHUNKS = 2
+CHUNKS = 1
 DIAG = 7.0
 
 VMEM = pl.BlockSpec(memory_space=pltpu.VMEM)
@@ -40,43 +40,18 @@
     return ar * br + ai * bi, ai * br - ar * bi
 
 
-def gather_kernel(planes, index_ref, occupied_hbm, psi_hbm, orb_hbm, pack_ref, psi_ref, orb, occupied_ref, sems):
-    rows = 2 * planes
+def gather_kernel(planes, index_ref, weight_ref, orb, pack_ref):
+    rows = 2 * CX * planes
     field_rows = FIELDS * planes
-    chunk = BLOCK // CHUNKS
-    masks = pltpu.make_async_copy(occupied_hbm, occupied_ref, sems.at[0])
-    masks.start()
     first = index_ref[0] * BLOCK
-    loads = []
-    for g in range(CHUNKS):
-        source = pl.ds(pl.multiple_of((first + g * chunk) * rows, 8), chunk * rows)
-        target = pl.ds(g * chunk * rows, chunk * rows)
-        group = [
-            pltpu.make_async_copy(
-                orb_hbm.at[source, pl.ds(x * CY, CY)], orb.at[x, target], sems.at[2 + g * CX + x]
-            )
-            for x in range(CX)
-        ]
-        for load in group:
-            load.start()
-        loads.append(group)
-    keep = pltpu.make_async_copy(psi_hbm, psi_ref, sems.at[1])
-    keep.start()
-    masks.wait()
-    weights = [occupied_ref[0, first + m].astype(jnp.float32) for m in range(BLOCK)]
-    band = lax.broadcasted_iota(jnp.int32, (BLOCK, 1), 0)
-    column = jnp.zeros((BLOCK, 1), jnp.float32)
-    for m in range(BLOCK):
-        column = jnp.where(band == m, weights[m], column)
     none = jnp.zeros((planes, CY), jnp.float32)
     dens, dy_re, dy_im, dz_re, dz_im = [[none] * CX for _ in range(5)]
     dx_re, dx_im = none, none
     for m in range(BLOCK):
-        if m % chunk == 0:
-            for load in loads[m // chunk]:
-                load.wait()
-        re = [orb[x, pl.ds(m * rows, planes), :] * weights[m] for x in range(CX)]
-        im = [orb[x, pl.ds(m * rows + planes, planes), :] * weights[m] for x in range(CX)]
+        base = pl.multiple_of((first + m) * rows, 8)
+        weight = weight_ref[pl.ds(first + m, 1), :]
+        re = [orb[pl.ds(base + x * planes, planes), :] * weight for x in range(CX)]
+        im = [orb[pl.ds(base + (CX + x) * planes, planes), :] * weight for x in range(CX)]
         part = bond(re[0], im[0], re[1], im[1])
         dx_re, dx_im = dx_re + part[0], dx_im + part[1]
         for x in range(CX):
@@ -88,34 +63,50 @@
     for i, field in enumerate((dens, (dx_re, dx_im), dy_re, dy_im, dz_re, dz_im)):
         for x in range(CX):
             pack_ref[pl.ds(i * planes, planes), pl.ds(x * CY, CY)] = field[x]
+    column = weight_ref[pl.ds(pl.multiple_of(first, BLOCK), BLOCK), :]
     for e, plane in enumerate((0, planes - 1)):
         for c in range(2):
             for x in range(CX):
-                ends = orb[x, pl.ds(c * planes + plane, BLOCK, stride=rows), :] * column
+                ends = orb[pl.ds(first * rows + (c * CX + x) * planes + plane, BLOCK, stride=rows), :] * column
                 pack_ref[pl.ds(field_rows + (2 * e + c) * BLOCK, BLOCK), pl.ds(x * CY, CY)] = ends
-    keep.wait()
-
-
-def gather(block_index, occupied, psi, orb, planes):
+
+
+def spread(occupied):
+    count = occupied.shape[1]
+
+    def body(occupied_hbm, out, masks, sem):
+        load = pltpu.make_async_copy(occupied_hbm, masks, sem)
+        load.start()
+        band = lax.broadcasted_iota(jnp.int32, (count, count), 0)
+        lane = lax.broadcasted_iota(jnp.int32, (count, count), 1)
+        load.wait()
+        chosen = jnp.where(band == lane, masks[...].astype(jnp.float32), 0.0)
+        out[...] = jnp.broadcast_to(jnp.sum(chosen, axis=1, keepdims=True), (count, CY))
+
+    return pl.pallas_call(
+        body,
+        out_shape=jax.ShapeDtypeStruct((count, CY), jnp.float32),
+        in_specs=[HBM],
+        out_specs=VMEM,
+        scratch_shapes=[pltpu.VMEM(occupied.shape, jnp.int32), pltpu.SemaphoreType.DMA],
+        compiler_params=PARAMS,
+        cost_estimate=pl.CostEstimate(flops=1000000000, bytes_accessed=0, transcendentals=0),
+        name="spread_mask",
+    )(occupied)
+
+
+def gather(block_index, weights, orb, planes):
     def body(*refs):
         gather_kernel(planes, *refs)
 
     return pl.pallas_call(
         body,
-        out_shape=(
-            jax.ShapeDtypeStruct((FIELDS * planes + 4 * BLOCK, CELLS), jnp.float32),
-            jax.ShapeDtypeStruct(psi.shape, jnp.float32),
-        ),
-        in_specs=[SMEM, HBM, HBM, HBM],
-        out_specs=(VMEM, VMEM),
-        scratch_shapes=[
-            pltpu.VMEM((CX, 2 * planes * BLOCK, CY), jnp.float32),
-            pltpu.SMEM(occupied.shape, jnp.int32),
-            pltpu.SemaphoreType.DMA((2 + CX * CHUNKS,)),
-        ],
+        out_shape=jax.ShapeDtypeStruct((FIELDS * planes + 4 * BLOCK, CELLS), jnp.float32),
+        in_specs=[SMEM, VMEM, VMEM],
+        out_specs=VMEM,
         compiler_params=PARAMS,
         name="local_fields",
-    )(block_index, occupied, psi, orb)
+    )(block_index, weights, orb)
 
 
 def phase_of(kpoint, place, cycle):
@@ -300,12 +291,12 @@
     cycle, slabs = lax.axis_size("kring"), lax.axis_size("slab")
     place = lax.axis_index("kring")
     psi = targets.reshape(2 * bands * planes, CELLS)
-    orb = orbitals.reshape(-1, CELLS)
+    orb = orbitals.reshape(-1, planes, CX, CY).transpose(0, 2, 1, 3).reshape(-1, CY)
 
     phase = phase_of(kpoint, place, cycle)
 
-    occupied, psi, orb = [pltpu.with_memory_space_constraint(v, pltpu.HBM) for v in (occupied, psi, orb)]
-    own, psi = gather(block_index, occupied, psi, orb, planes)
+    occupied = pltpu.with_memory_space_constraint(occupied, pltpu.HBM)
+    own = gather(block_index, spread(occupied), orb, planes)
     packs = [own] + [shift(own, "slab", d) for d in range(1, slabs)]
     psis = [psi] + [shift(psi, "slab", d) for d in range(1, slabs)]
     mine = join(phase, packs, planes)

time: 18.8 us -> 18.7 us (level)
    pallas_call x1 -> x2, Pallas kernels: 1.17 us -> 0.99 us  [the longest x1 0.8 us: spread(): pl.pallas_call(body, out_shape=jax.ShapeDtypeStruct((count, CY), jnp.floa...]
    unnamed x2 -> x6, local copies, waits for them, and re-layouts: 0.65 us -> 0.67 us
where the time goes in v4:
time: 18.7 us; the launch traced here: 18.5 us
  starting transfers between devices  9.62 us (51%)
  waiting for transfers between devices  4.42 us (24%)
  Pallas kernels  2.42 us (13%)
  between operations  1.34 us (7%)
  local copies, waits for them, and re-layouts  0.67 us (4%)
    ppermute x4, starting transfers between devices, shift(): lax.ppermute(value, axis, [((i + distance) % count, i) for i in range(cou...  9.55 us
    ppermute x4, waiting for transfers between devices, shift(): lax.ppermute(value, axis, [((i + distance) % count, i) for i in range(cou...  4.04 us
    pallas_call x1, Pallas kernels, spread(): pl.pallas_call(body, out_shape=jax.ShapeDtypeStruct((count, CY), jnp.floa...  0.8 us
    pallas_call x1, Pallas kernels, apply(): pl.pallas_call(body, out_shape=(jax.ShapeDtypeStruct((2 * bands * planes,...  0.8 us
    unnamed x6, local copies, waits for them, and re-layouts  0.67 us
    pallas_call x1, Pallas kernels, phase_of(): pl.pallas_call(body, out_shape=jax.ShapeDtypeStruct((16, CY), jnp.float32...  0.6 us
    ppermute x1, waiting for transfers between devices, body(): other = lax.ppermute(lacking, 'kring', [(i, i ^ 1) for i in range(cycle)])  0.38 us
  transfers between devices with their start and end apart: 5, of which 5 were waited for; matrix products, arithmetic and copies ran while one was open for 0% of the time, Pallas kernels for 3%

profile of v4, /device:TPU:0, one launch (start us, length us, event | category | flops | bytes accessed | tf_op | source)
XLA Modules:
  0.0 18.5 jit_solution(4780289388677784703)
XLA Ops:
  0.6 0.0 copy-start
  0.6 0.8 %spread_mask.1.refs_1_ = f32[32,128]{1,0:T(8,128)S(1)} custom-call(s32[1,32]{1,0:T(1,128)} %occupied_hbm.1), custom_call_target="tpu_custom_call" | custom-call | flops 1000000000 | tf_op jit(solution)/shard_map/spread_mask/pallas_call | solution.py:86
  2.1 0.0 copy-done
  2.1 0.2 %local_fields.1.refs_0_ = f32[112,256]{1,0:T(8,128)S(1)} custom-call(s32[1]{0:T(128)S(6)} %copy.7.refs_0_, f32[32,128]{1,0:T(8,128)S(1)} %spread_mask.1.refs_1_, f32[1024,128]{1,0:T(8,128)S(1)} %bitcast.8), custom_call_target="tpu_custom_call" | custom-call | tf_op jit(solution)/shard_map/local_fields/pallas_call | solution.py:102
  2.3 3.0 %collective-permute-start = (f32[112,256]{1,0:T(8,128)S(1)}, f32[112,256]{1,0:T(8,128)S(1)}, u32[]{:S(2)}, u32[]{:S(2)}) collective-permute-start(f32[112,256]{1,0:T(8,128)S(1)} %local_fields.1.refs_0_), channel_id=1, source_target_pairs={{1,0},{0,1},{3,2},{2,3},{5,4},{4,5},{7,6},{6,7},{9,8},{8,9},{11,10... | collective-permute-start | bytes 344072 | tf_op jit(solution)/shard_map/ppermute | solution.py:286
  5.3 0.0 copy-start.1
  5.3 0.7 %copy-done.1 = s32[16]{0:T(128)S(1)} copy-done((s32[16]{0:T(128)S(1)}, s32[16]{0:T(128)}, u32[]{:S(2)}) %copy-start.1) | copy-done | bytes 88
  6.0 0.6 %phase.1.phase_ref = f32[16,128]{1,0:T(8,128)S(1)} custom-call(s32[1]{0:T(128)} %bitcast.place_ref, s32[16]{0:T(128)S(1)} %copy-done.1), custom_call_target="tpu_custom_call" | custom-call | tf_op jit(solution)/shard_map/phase/pallas_call | solution.py:122
  6.6 0.0 copy-start.2
  6.6 1.9 %collective-permute-done.refs_1_ = f32[112,256]{1,0:T(8,128)S(1)} collective-permute-done((f32[112,256]{1,0:T(8,128)S(1)}, f32[112,256]{1,0:T(8,128)S(1)}, u32[]{:S(2)}, u32[]{:S(2)}) %collective-permute-start) | collective-permute-done | bytes 114720 | tf_op jit(solution)/shard_map/ppermute | solution.py:286
  8.5 1.8 %collective-permute-start.1 = (f32[96,256]{1,0:T(8,128)S(1)}, f32[96,256]{1,0:T(8,128)S(1)}, u32[]{:S(2)}, u32[]{:S(2)}) collective-permute-start(f32[96,256]{1,0:T(8,128)S(1)} %join_slabs.1.refs_0_), channel_id=1, source_target_pairs={{28,0},{30,2},{0,4},{2,6},{4,8},{6,10},{8,12},{10,14},{12,16},{14,... | collective-permute-start | bytes 294920 | tf_op jit(solution)/shard_map/ppermute | solution.py:286
  10.3 3.1 %collective-permute-start.2 = (f32[96,256]{1,0:T(8,128)S(1)}, f32[96,256]{1,0:T(8,128)S(1)}, u32[]{:S(2)}, u32[]{:S(2)}) collective-permute-start(f32[96,256]{1,0:T(8,128)S(1)} %join_slabs.1.refs_0_), channel_id=1, source_target_pairs={{4,0},{6,2},{8,4},{10,6},{12,8},{14,10},{16,12},{18,14},{20,16},{2... | collective-permute-start | bytes 294920 | tf_op jit(solution)/shard_map/ppermute | solution.py:286
  13.4 0.0 copy-done.2
  13.4 1.6 %collective-permute-start.4 = (f32[32,256]{1,0:T(8,128)S(1)}, f32[32,256]{1,0:T(8,128)S(1)}, u32[]{:S(2)}, u32[]{:S(2)}) collective-permute-start(f32[32,256]{1,0:T(8,128)S(1)} %bitcast.9), channel_id=1, source_target_pairs={{1,0},{0,1},{3,2},{2,3},{5,4},{4,5},{7,6},{6,7},{9,8},{8,9},{11,10... | collective-permute-start | bytes 98312 | tf_op jit(solution)/shard_map/ppermute | solution.py:286
  15.0 1.0 %collective-permute-done.1.refs_1_ = f32[96,256]{1,0:T(8,128)S(1)} collective-permute-done((f32[96,256]{1,0:T(8,128)S(1)}, f32[96,256]{1,0:T(8,128)S(1)}, u32[]{:S(2)}, u32[]{:S(2)}) %collective-permute-start.1) | collective-permute-done | bytes 98336 | tf_op jit(solution)/shard_map/ppermute | solution.py:286
  16.0 0.3 %collective-permute-done.2.refs_2_ = f32[96,256]{1,0:T(8,128)S(1)} collective-permute-done((f32[96,256]{1,0:T(8,128)S(1)}, f32[96,256]{1,0:T(8,128)S(1)}, u32[]{:S(2)}, u32[]{:S(2)}) %collective-permute-start.2) | collective-permute-done | bytes 98336 | tf_op jit(solution)/shard_map/ppermute | solution.py:286
  16.3 0.1 collective-permute-start.3
  16.4 0.9 %collective-permute-done.4.refs_1_ = f32[32,256]{1,0:T(8,128)S(1)} collective-permute-done((f32[32,256]{1,0:T(8,128)S(1)}, f32[32,256]{1,0:T(8,128)S(1)}, u32[]{:S(2)}, u32[]{:S(2)}) %collective-permute-start.4) | collective-permute-done | bytes 32800 | tf_op jit(solution)/shard_map/ppermute | solution.py:286
  17.3 0.4 %collective-permute-done.3.refs_3_ = f32[96,256]{1,0:T(8,128)S(1)} collective-permute-done((f32[96,256]{1,0:T(8,128)S(1)}, f32[96,256]{1,0:T(8,128)S(1)}, u32[]{:S(2)}, u32[]{:S(2)}) %collective-permute-start.3) | collective-permute-done | bytes 98336 | tf_op jit(solution)/shard_map/ppermute | solution.py:308
  17.7 0.8 %apply_window.1 = (f32[32,256]{1,0:T(8,128)}, f32[1,2,2,2]{3,2,1,0:T(2,128)}) custom-call(f32[16,128]{1,0:T(8,128)S(1)} %phase.1.phase_ref, f32[96,256]{1,0:T(8,128)S(1)} %join_slabs.1.refs_0_, f32[96,256]{1,0:T(8,128)S(1)} %collective-permute-done.1.refs_1_, f32[96,256]{1,0:T(8,128)S(1)} %collective-permute-done.2.refs_2_, ...), custom_call_target="tpu_custom_call" | custom-call | tf_op jit(solution)/shard_map/apply_window/pallas_call | solution.py:271
  (3 shorter events, 0.1 us)
Async XLA Ops:
  0.6 1.5 %copy-start = (f32[1,32,2,8,256]{4,3,2,1,0:T(8,128)S(1)}, f32[1,32,2,8,256]{4,3,2,1,0:T(8,128)}, u32[]{:S(2)}) copy-start(f32[1,32,2,8,256]{4,3,2,1,0:T(8,128)} %param.6) | copy-start | bytes 1572868
  2.3 6.2 %collective-permute-start = (f32[112,256]{1,0:T(8,128)S(1)}, f32[112,256]{1,0:T(8,128)S(1)}, u32[]{:S(2)}, u32[]{:S(2)}) collective-permute-start(f32[112,256]{1,0:T(8,128)S(1)} %local_fields.1.refs_0_), channel_id=1, source_target_pairs={{1,0},{0,1},{3,2},{2,3},{5,4},{4,5},{7,6},{6,7},{9,8},{8,9},{11,10... | collective-permute-start | bytes 344072 | tf_op jit(solution)/shard_map/ppermute | solution.py:286
  5.3 0.7 %copy-start.1 = (s32[16]{0:T(128)S(1)}, s32[16]{0:T(128)}, u32[]{:S(2)}) copy-start(s32[16]{0:T(128)} %kpoint_hbm.1) | copy-start | bytes 196
  6.6 6.8 %copy-start.2 = (f32[1,2,2,8,256]{4,3,2,1,0:T(8,128)S(1)}, f32[1,2,2,8,256]{4,3,2,1,0:T(8,128)}, u32[]{:S(2)}) copy-start(f32[1,2,2,8,256]{4,3,2,1,0:T(8,128)} %param.5) | copy-start | bytes 98308
  8.5 7.5 %collective-permute-start.1 = (f32[96,256]{1,0:T(8,128)S(1)}, f32[96,256]{1,0:T(8,128)S(1)}, u32[]{:S(2)}, u32[]{:S(2)}) collective-permute-start(f32[96,256]{1,0:T(8,128)S(1)} %join_slabs.1.refs_0_), channel_id=1, source_target_pairs={{28,0},{30,2},{0,4},{2,6},{4,8},{6,10},{8,12},{10,14},{12,16},{14,... | collective-permute-start | bytes 294920 | tf_op jit(solution)/shard_map/ppermute | solution.py:286
  10.3 6.0 %collective-permute-start.2 = (f32[96,256]{1,0:T(8,128)S(1)}, f32[96,256]{1,0:T(8,128)S(1)}, u32[]{:S(2)}, u32[]{:S(2)}) collective-permute-start(f32[96,256]{1,0:T(8,128)S(1)} %join_slabs.1.refs_0_), channel_id=1, source_target_pairs={{4,0},{6,2},{8,4},{10,6},{12,8},{14,10},{16,12},{18,14},{20,16},{2... | collective-permute-start | bytes 294920 | tf_op jit(solution)/shard_map/ppermute | solution.py:286
  13.4 3.9 %collective-permute-start.4 = (f32[32,256]{1,0:T(8,128)S(1)}, f32[32,256]{1,0:T(8,128)S(1)}, u32[]{:S(2)}, u32[]{:S(2)}) collective-permute-start(f32[32,256]{1,0:T(8,128)S(1)} %bitcast.9), channel_id=1, source_target_pairs={{1,0},{0,1},{3,2},{2,3},{5,4},{4,5},{7,6},{6,7},{9,8},{8,9},{11,10... | collective-permute-start | bytes 98312 | tf_op jit(solution)/shard_map/ppermute | solution.py:286
  16.3 1.4 %collective-permute-start.3 = (f32[96,256]{1,0:T(8,128)S(1)}, f32[96,256]{1,0:T(8,128)S(1)}, u32[]{:S(2)}, u32[]{:S(2)}) collective-permute-start(f32[96,256]{1,0:T(8,128)S(1)} %select_add_fusion), channel_id=1, source_target_pairs={{0,2},{2,0},{4,6},{6,4},{8,10},{10,8},{12,14},{14,12},{16,18},{18,... | collective-permute-start | bytes 294920 | tf_op jit(solution)/shard_map/ppermute | solution.py:308

commit v5 on v4

--- a/solution.py
+++ b/solution.py
@@ -71,28 +71,37 @@
                 pack_ref[pl.ds(field_rows + (2 * e + c) * BLOCK, BLOCK), pl.ds(x * CY, CY)] = ends
 
 
-def spread(occupied):
-    count = occupied.shape[1]
-
-    def body(occupied_hbm, out, masks, sem):
-        load = pltpu.make_async_copy(occupied_hbm, masks, sem)
-        load.start()
-        band = lax.broadcasted_iota(jnp.int32, (count, count), 0)
-        lane = lax.broadcasted_iota(jnp.int32, (count, count), 1)
-        load.wait()
-        chosen = jnp.where(band == lane, masks[...].astype(jnp.float32), 0.0)
-        out[...] = jnp.broadcast_to(jnp.sum(chosen, axis=1, keepdims=True), (count, CY))
+def diagonal(count):
+    def body(out):
+        row = lax.broadcasted_iota(jnp.int32, (count, count), 0)
+        column = lax.broadcasted_iota(jnp.int32, (count, count), 1)
+        out[...] = jnp.where(row == column, 1.0, 0.0)
+
+    return pl.pallas_call(
+        body,
+        out_shape=jax.ShapeDtypeStruct((count, count), jnp.float32),
+        out_specs=VMEM,
+        compiler_params=PARAMS,
+        cost_estimate=pl.CostEstimate(flops=1000000000, bytes_accessed=0, transcendentals=0),
+        name="diagonal",
+    )()
+
+
+def spread(mask, ones):
+    count = mask.shape[1]
+
+    def body(mask_ref, ones_ref, out):
+        held = jnp.sum(mask_ref[...] * ones_ref[...], axis=1, keepdims=True)
+        out[...] = jnp.broadcast_to(held, (count, CY))
 
     return pl.pallas_call(
         body,
         out_shape=jax.ShapeDtypeStruct((count, CY), jnp.float32),
-        in_specs=[HBM],
-        out_specs=VMEM,
-        scratch_shapes=[pltpu.VMEM(occupied.shape, jnp.int32), pltpu.SemaphoreType.DMA],
-        compiler_params=PARAMS,
-        cost_estimate=pl.CostEstimate(flops=1000000000, bytes_accessed=0, transcendentals=0),
+        in_specs=[VMEM, VMEM],
+        out_specs=VMEM,
+        compiler_params=PARAMS,
         name="spread_mask",
-    )(occupied)
+    )(mask, ones)
 
 
 def gather(block_index, weights, orb, planes):
@@ -295,8 +304,10 @@
 
     phase = phase_of(kpoint, place, cycle)
 
-    occupied = pltpu.with_memory_space_constraint(occupied, pltpu.HBM)
-    own = gather(block_index, spread(occupied), orb, planes)
+    held = occupied.shape[1]
+    words = occupied + 2 * lax.pad(block_index, jnp.int32(0), [(0, held - 1, 0)]).reshape(1, held)
+    mask = (words & 1).astype(jnp.float32)
+    own = gather(block_index, spread(mask, diagonal(held)), orb, planes)
     packs = [own] + [shift(own, "slab", d) for d in range(1, slabs)]
     psis = [psi] + [shift(psi, "slab", d) for d in range(1, slabs)]
     mine = join(phase, packs, planes)

time: 18.7 us -> 18.2 us (0.973)
  Pallas kernels: 2.42 us -> 1.71 us
  local copies, waits for them, and re-layouts: 0.67 us -> 0.89 us
    pallas_call x1, Pallas kernels: 0.8 us -> 0.08 us  [spread(): pl.pallas_call(body, out_shape=jax.ShapeDtypeStruct((count, CY), jnp.floa...]
    unnamed x6 -> x8, local copies, waits for them, and re-layouts: 0.67 us -> 0.89 us
where the time goes in v5:
time: 18.2 us; the launch traced here: 18.1 us
  starting transfers between devices  9.62 us (53%)
  waiting for transfers between devices  4.42 us (24%)
  Pallas kernels  1.71 us (9%)
  between operations  1.42 us (8%)
  local copies, waits for them, and re-layouts  0.89 us (5%)
    ppermute x4, starting transfers between devices, shift(): lax.ppermute(value, axis, [((i + distance) % count, i) for i in range(cou...  9.55 us
    ppermute x4, waiting for transfers between devices, shift(): lax.ppermute(value, axis, [((i + distance) % count, i) for i in range(cou...  4.04 us
    unnamed x8, local copies, waits for them, and re-layouts  0.89 us
    pallas_call x1, Pallas kernels, apply(): pl.pallas_call(body, out_shape=(jax.ShapeDtypeStruct((2 * bands * planes,...  0.8 us
    pallas_call x1, Pallas kernels, phase_of(): pl.pallas_call(body, out_shape=jax.ShapeDtypeStruct((16, CY), jnp.float32...  0.6 us
    ppermute x1, waiting for transfers between devices, body(): other = lax.ppermute(lacking, 'kring', [(i, i ^ 1) for i in range(cycle)])  0.38 us
  transfers between devices with their start and end apart: 5, of which 5 were waited for; matrix products, arithmetic and copies ran while one was open for 0% of the time, Pallas kernels for 3%

profile of v5, /device:TPU:0, one launch (start us, length us, event | category | flops | bytes accessed | tf_op | source)
XLA Modules:
  0.0 18.1 jit_solution(757997670151474342)
XLA Ops:
  0.6 0.0 copy-start
  0.7 0.0 copy-start.3
  1.4 0.0 copy-done.3
  1.4 0.1 spread_mask.1.refs_1_
  1.5 0.2 %copy-done = f32[1,32,2,8,256]{4,3,2,1,0:T(8,128)S(1)} copy-done((f32[1,32,2,8,256]{4,3,2,1,0:T(8,128)S(1)}, f32[1,32,2,8,256]{4,3,2,1,0:T(8,128)}, u32[]{:S(2)}) %copy-start) | copy-done | bytes 524312
  1.7 0.2 %local_fields.1.refs_0_ = f32[112,256]{1,0:T(8,128)S(1)} custom-call(s32[1]{0:T(128)S(6)} %copy.7.refs_0_, f32[32,128]{1,0:T(8,128)S(1)} %spread_mask.1.refs_1_, f32[1024,128]{1,0:T(8,128)S(1)} %bitcast.14), custom_call_target="tpu_custom_call" | custom-call | tf_op jit(solution)/shard_map/local_fields/pallas_call | solution.py:111
  1.9 3.0 %collective-permute-start = (f32[112,256]{1,0:T(8,128)S(1)}, f32[112,256]{1,0:T(8,128)S(1)}, u32[]{:S(2)}, u32[]{:S(2)}) collective-permute-start(f32[112,256]{1,0:T(8,128)S(1)} %local_fields.1.refs_0_), channel_id=1, source_target_pairs={{1,0},{0,1},{3,2},{2,3},{5,4},{4,5},{7,6},{6,7},{9,8},{8,9},{11,10... | collective-permute-start | bytes 344072 | tf_op jit(solution)/shard_map/ppermute | solution.py:295
  4.9 0.0 copy-start.1
  4.9 0.7 %copy-done.1 = s32[16]{0:T(128)S(1)} copy-done((s32[16]{0:T(128)S(1)}, s32[16]{0:T(128)}, u32[]{:S(2)}) %copy-start.1) | copy-done | bytes 88
  5.6 0.6 %phase.1.phase_ref = f32[16,128]{1,0:T(8,128)S(1)} custom-call(s32[1]{0:T(128)} %bitcast.place_ref, s32[16]{0:T(128)S(1)} %copy-done.1), custom_call_target="tpu_custom_call" | custom-call | tf_op jit(solution)/shard_map/phase/pallas_call | solution.py:131
  6.2 0.0 copy-start.2
  6.2 1.9 %collective-permute-done.refs_1_ = f32[112,256]{1,0:T(8,128)S(1)} collective-permute-done((f32[112,256]{1,0:T(8,128)S(1)}, f32[112,256]{1,0:T(8,128)S(1)}, u32[]{:S(2)}, u32[]{:S(2)}) %collective-permute-start) | collective-permute-done | bytes 114720 | tf_op jit(solution)/shard_map/ppermute | solution.py:295
  8.1 1.8 %collective-permute-start.1 = (f32[96,256]{1,0:T(8,128)S(1)}, f32[96,256]{1,0:T(8,128)S(1)}, u32[]{:S(2)}, u32[]{:S(2)}) collective-permute-start(f32[96,256]{1,0:T(8,128)S(1)} %join_slabs.1.refs_0_), channel_id=1, source_target_pairs={{28,0},{30,2},{0,4},{2,6},{4,8},{6,10},{8,12},{10,14},{12,16},{14,... | collective-permute-start | bytes 294920 | tf_op jit(solution)/shard_map/ppermute | solution.py:295
  9.9 3.1 %collective-permute-start.2 = (f32[96,256]{1,0:T(8,128)S(1)}, f32[96,256]{1,0:T(8,128)S(1)}, u32[]{:S(2)}, u32[]{:S(2)}) collective-permute-start(f32[96,256]{1,0:T(8,128)S(1)} %join_slabs.1.refs_0_), channel_id=1, source_target_pairs={{4,0},{6,2},{8,4},{10,6},{12,8},{14,10},{16,12},{18,14},{20,16},{2... | collective-permute-start | bytes 294920 | tf_op jit(solution)/shard_map/ppermute | solution.py:295
  13.0 0.0 copy-done.2
  13.0 1.6 %collective-permute-start.4 = (f32[32,256]{1,0:T(8,128)S(1)}, f32[32,256]{1,0:T(8,128)S(1)}, u32[]{:S(2)}, u32[]{:S(2)}) collective-permute-start(f32[32,256]{1,0:T(8,128)S(1)} %bitcast.15), channel_id=1, source_target_pairs={{1,0},{0,1},{3,2},{2,3},{5,4},{4,5},{7,6},{6,7},{9,8},{8,9},{11,10... | collective-permute-start | bytes 98312 | tf_op jit(solution)/shard_map/ppermute | solution.py:295
  14.6 1.0 %collective-permute-done.1.refs_1_ = f32[96,256]{1,0:T(8,128)S(1)} collective-permute-done((f32[96,256]{1,0:T(8,128)S(1)}, f32[96,256]{1,0:T(8,128)S(1)}, u32[]{:S(2)}, u32[]{:S(2)}) %collective-permute-start.1) | collective-permute-done | bytes 98336 | tf_op jit(solution)/shard_map/ppermute | solution.py:295
  15.6 0.3 %collective-permute-done.2.refs_2_ = f32[96,256]{1,0:T(8,128)S(1)} collective-permute-done((f32[96,256]{1,0:T(8,128)S(1)}, f32[96,256]{1,0:T(8,128)S(1)}, u32[]{:S(2)}, u32[]{:S(2)}) %collective-permute-start.2) | collective-permute-done | bytes 98336 | tf_op jit(solution)/shard_map/ppermute | solution.py:295
  15.9 0.1 collective-permute-start.3
  16.0 0.9 %collective-permute-done.4.refs_1_ = f32[32,256]{1,0:T(8,128)S(1)} collective-permute-done((f32[32,256]{1,0:T(8,128)S(1)}, f32[32,256]{1,0:T(8,128)S(1)}, u32[]{:S(2)}, u32[]{:S(2)}) %collective-permute-start.4) | collective-permute-done | bytes 32800 | tf_op jit(solution)/shard_map/ppermute | solution.py:295
  16.9 0.4 %collective-permute-done.3.refs_3_ = f32[96,256]{1,0:T(8,128)S(1)} collective-permute-done((f32[96,256]{1,0:T(8,128)S(1)}, f32[96,256]{1,0:T(8,128)S(1)}, u32[]{:S(2)}, u32[]{:S(2)}) %collective-permute-start.3) | collective-permute-done | bytes 98336 | tf_op jit(solution)/shard_map/ppermute | solution.py:319
  17.3 0.8 %apply_window.1 = (f32[32,256]{1,0:T(8,128)}, f32[1,2,2,2]{3,2,1,0:T(2,128)}) custom-call(f32[16,128]{1,0:T(8,128)S(1)} %phase.1.phase_ref, f32[96,256]{1,0:T(8,128)S(1)} %join_slabs.1.refs_0_, f32[96,256]{1,0:T(8,128)S(1)} %collective-permute-done.1.refs_1_, f32[96,256]{1,0:T(8,128)S(1)} %collective-permute-done.2.refs_2_, ...), custom_call_target="tpu_custom_call" | custom-call | tf_op jit(solution)/shard_map/apply_window/pallas_call | solution.py:280
  (5 shorter events, 0.1 us)
Async XLA Ops:
  0.6 1.1 %copy-start = (f32[1,32,2,8,256]{4,3,2,1,0:T(8,128)S(1)}, f32[1,32,2,8,256]{4,3,2,1,0:T(8,128)}, u32[]{:S(2)}) copy-start(f32[1,32,2,8,256]{4,3,2,1,0:T(8,128)} %param.6) | copy-start | bytes 1572868
  0.7 0.7 %copy-start.3 = (s32[1,32]{1,0:T(1,128)S(1)}, s32[1,32]{1,0:T(1,128)}, u32[]{:S(2)}) copy-start(s32[1,32]{1,0:T(1,128)} %param.8) | copy-start | bytes 388
  1.9 6.2 %collective-permute-start = (f32[112,256]{1,0:T(8,128)S(1)}, f32[112,256]{1,0:T(8,128)S(1)}, u32[]{:S(2)}, u32[]{:S(2)}) collective-permute-start(f32[112,256]{1,0:T(8,128)S(1)} %local_fields.1.refs_0_), channel_id=1, source_target_pairs={{1,0},{0,1},{3,2},{2,3},{5,4},{4,5},{7,6},{6,7},{9,8},{8,9},{11,10... | collective-permute-start | bytes 344072 | tf_op jit(solution)/shard_map/ppermute | solution.py:295
  4.9 0.7 %copy-start.1 = (s32[16]{0:T(128)S(1)}, s32[16]{0:T(128)}, u32[]{:S(2)}) copy-start(s32[16]{0:T(128)} %kpoint_hbm.1) | copy-start | bytes 196
  6.2 6.8 %copy-start.2 = (f32[1,2,2,8,256]{4,3,2,1,0:T(8,128)S(1)}, f32[1,2,2,8,256]{4,3,2,1,0:T(8,128)}, u32[]{:S(2)}) copy-start(f32[1,2,2,8,256]{4,3,2,1,0:T(8,128)} %param.5) | copy-start | bytes 98308
  8.1 7.5 %collective-permute-start.1 = (f32[96,256]{1,0:T(8,128)S(1)}, f32[96,256]{1,0:T(8,128)S(1)}, u32[]{:S(2)}, u32[]{:S(2)}) collective-permute-start(f32[96,256]{1,0:T(8,128)S(1)} %join_slabs.1.refs_0_), channel_id=1, source_target_pairs={{28,0},{30,2},{0,4},{2,6},{4,8},{6,10},{8,12},{10,14},{12,16},{14,... | collective-permute-start | bytes 294920 | tf_op jit(solution)/shard_map/ppermute | solution.py:295
  9.9 6.0 %collective-permute-start.2 = (f32[96,256]{1,0:T(8,128)S(1)}, f32[96,256]{1,0:T(8,128)S(1)}, u32[]{:S(2)}, u32[]{:S(2)}) collective-permute-start(f32[96,256]{1,0:T(8,128)S(1)} %join_slabs.1.refs_0_), channel_id=1, source_target_pairs={{4,0},{6,2},{8,4},{10,6},{12,8},{14,10},{16,12},{18,14},{20,16},{2... | collective-permute-start | bytes 294920 | tf_op jit(solution)/shard_map/ppermute | solution.py:295
  13.0 3.9 %collective-permute-start.4 = (f32[32,256]{1,0:T(8,128)S(1)}, f32[32,256]{1,0:T(8,128)S(1)}, u32[]{:S(2)}, u32[]{:S(2)}) collective-permute-start(f32[32,256]{1,0:T(8,128)S(1)} %bitcast.15), channel_id=1, source_target_pairs={{1,0},{0,1},{3,2},{2,3},{5,4},{4,5},{7,6},{6,7},{9,8},{8,9},{11,10... | collective-permute-start | bytes 98312 | tf_op jit(solution)/shard_map/ppermute | solution.py:295
  15.9 1.4 %collective-permute-start.3 = (f32[96,256]{1,0:T(8,128)S(1)}, f32[96,256]{1,0:T(8,128)S(1)}, u32[]{:S(2)}, u32[]{:S(2)}) collective-permute-start(f32[96,256]{1,0:T(8,128)S(1)} %select_add_fusion), channel_id=1, source_target_pairs={{0,2},{2,0},{4,6},{6,4},{8,10},{10,8},{12,14},{14,12},{16,18},{18,... | collective-permute-start | bytes 294920 | tf_op jit(solution)/shard_map/ppermute | solution.py:319

commit v6 on v5

--- a/solution.py
+++ b/solution.py
@@ -12,6 +12,7 @@
 CELLS = CX * CY
 BLOCK = 16
 FIELDS = 6
+NEIGHBOURS = 6
 CHUNKS = 1
 DIAG = 7.0
 
@@ -143,22 +144,85 @@
     return [jnp.concatenate([ref[pl.ds(8 * i, 1), :]] * CX, axis=1) for i in range(2)]
 
 
-def stack(targets):
-    rows = targets[0].shape[0]
+def ready_targets(targets, planes, bands):
+    count = len(targets)
+    cells = count * planes * CELLS
+    values = tile_values(bands)
 
     def body(*refs):
-        for i, ref in enumerate(refs[:-1]):
-            refs[-1][pl.ds(i * rows, rows), :] = ref[...]
-
-    return pl.pallas_call(
-        body,
-        out_shape=jax.ShapeDtypeStruct((len(targets) * rows, CELLS), jnp.float32),
-        in_specs=[VMEM] * len(targets),
-        out_specs=VMEM,
+        ins, near_ref, weight_ref = refs[:count], refs[count], refs[count + 1]
+        row = lax.broadcasted_iota(jnp.int32, (planes, CELLS), 0)
+
+        def psi_at(d, b):
+            return [ins[d % count][pl.ds((2 * b + c) * planes, planes), :] for c in range(2)]
+
+        def above(d, b):
+            here, next_slab = psi_at(d, b), psi_at(d + 1, b)
+            return [
+                jnp.where(row == planes - 1, pltpu.roll(n, planes - 1, 0), pltpu.roll(h, planes - 1, 0))
+                for h, n in zip(here, next_slab)
+            ]
+
+        def below(d, b):
+            here, last_slab = psi_at(d, b), psi_at(d - 1, b)
+            return [jnp.where(row == 0, pltpu.roll(n, 1, 0), pltpu.roll(h, 1, 0)) for h, n in zip(here, last_slab)]
+
+        for b in range(bands):
+            here = psi_at(0, b)
+            neighbours = (
+                here,
+                [swap_x(v) for v in here],
+                [turn(v, 1) for v in here],
+                [turn(v, -1) for v in here],
+                above(0, b),
+                below(0, b),
+            )
+            for n, pair in enumerate(neighbours):
+                for c in range(2):
+                    near_ref[pl.ds(((b * NEIGHBOURS + n) * 2 + c) * planes, planes), :] = pair[c]
+
+        def put(d, q, i, value, scale):
+            weight_ref[pl.ds(((d * len(values) + q) * FIELDS + i) * planes, planes), :] = value * scale
+
+        def mixed(first, second, a, b, part):
+            one = bond(*second[b], *first[a])
+            if a == b:
+                return 2.0 * one[0], -2.0 * one[1]
+            two = bond(*second[a], *first[b])
+            if part == 0:
+                return one[0] + two[0], -(one[1] + two[1])
+            return one[1] - two[1], one[0] - two[0]
+
+        for d in range(count):
+            here = [psi_at(d, b) for b in range(bands)]
+            left = [[halves(v)[0] for v in pair] for pair in here]
+            right = [[halves(v)[1] for v in pair] for pair in here]
+            beside = [[turn(v, 1) for v in pair] for pair in here]
+            over = [above(d, b) for b in range(bands)]
+            for q, (a, b, part) in enumerate(values):
+                put(d, q, 0, bond(*here[b], *here[a])[part], -1.0 / (DIAG * cells))
+                scale = -1.0 / (DIAG * DIAG * cells)
+                put(d, q, 1, jnp.concatenate(mixed(left, right, a, b, part), axis=1), 2.0 * scale)
+                for i, other in ((2, beside), (4, over)):
+                    for c, value in enumerate(mixed(here, other, a, b, part)):
+                        put(d, q, i + c, value, scale)
+
+    return pl.pallas_call(
+        body,
+        out_shape=(
+            jax.ShapeDtypeStruct((bands * NEIGHBOURS * 2 * planes, CELLS), jnp.float32),
+            jax.ShapeDtypeStruct((count * len(values) * FIELDS * planes, CELLS), jnp.float32),
+        ),
+        in_specs=[VMEM] * count,
+        out_specs=(VMEM, VMEM),
         compiler_params=PARAMS,
         cost_estimate=pl.CostEstimate(flops=1000000000, bytes_accessed=0, transcendentals=0),
-        name="stack_targets",
+        name="ready_targets",
     )(*targets)
+
+
+def tile_values(bands):
+    return [(a, b, part) for a in range(bands) for b in range(a, bands) for part in range(2 if b > a else 1)]
 
 
 def join(phase, packs, planes):
@@ -194,87 +258,75 @@
     )(phase, *packs)
 
 
-def apply(phase, parts, targets, planes, bands, count):
+def apply(phase, parts, near, weights, planes, bands, count):
     field_rows = FIELDS * planes
-    scale = 1.0 / (count * planes * CELLS)
+    values = tile_values(bands)
 
     def body(phase_ref, *refs):
-        part_refs, ins = refs[: len(parts)], refs[len(parts)]
-        out_ref, tile_ref = refs[len(parts) + 1 :]
+        part_refs, near_ref, weight_ref = refs[: len(parts)], refs[len(parts)], refs[len(parts) + 1]
+        out_ref, tile_ref = refs[len(parts) + 2 :]
         cosine, sine = phase_rows(phase_ref)
         row = lax.broadcasted_iota(jnp.int32, (planes, CELLS), 0)
 
-        def window(d, i, offset=0):
+        def window(d, i):
             at = pl.ds(d * field_rows + i * planes, planes)
             total = part_refs[0][at, :]
             for ref in part_refs[1:]:
                 total = total + ref[at, :]
             return total
 
-        def psi_at(d, b, c):
-            return ins[pl.ds(((d % count) * 2 * bands + 2 * b + c) * planes, planes), :]
-
-        def above(d, field):
-            return jnp.where(row == planes - 1, pltpu.roll(field(d + 1), planes - 1, 0), pltpu.roll(field(d), planes - 1, 0))
-
-        def below(d, field):
-            return jnp.where(row == 0, pltpu.roll(field(d - 1), 1, 0), pltpu.roll(field(d), 1, 0))
-
-        up = []
+        fields = []
         for d in range(count):
-            re, im = window(d, 4), window(d, 5)
-            up.append((re * cosine - im * sine, im * cosine + re * sine))
-        sums = [[[None, None] for _ in range(bands)] for _ in range(bands)]
-        for d in range(count):
-            dens = window(d, 0) * (1.0 / DIAG)
-            dx_re, dx_im = halves(window(d, 1))
-            x_re = jnp.concatenate([dx_re, dx_re], axis=1) * 2.0
-            x_im = jnp.concatenate([dx_im, -dx_im], axis=1) * 2.0
-            y_re, y_im = window(d, 2), window(d, 3)
-            yb_re, yb_im = turn(y_re, -1), -turn(y_im, -1)
-            z_re, z_im = up[d]
-            zb_re = below(d, lambda e: up[e % count][0])
-            zb_im = -below(d, lambda e: up[e % count][1])
-            results = []
-            for b in range(bands):
-                re, im = psi_at(d, b, 0), psi_at(d, b, 1)
-                acc_re = jnp.zeros_like(re)
-                acc_im = jnp.zeros_like(re)
-                terms = (
-                    (x_re, x_im, swap_x(re), swap_x(im)),
-                    (y_re, y_im, turn(re, 1), turn(im, 1)),
-                    (yb_re, yb_im, turn(re, -1), turn(im, -1)),
-                    (z_re, z_im, above(d, lambda e: psi_at(e, b, 0)), above(d, lambda e: psi_at(e, b, 1))),
-                    (zb_re, zb_im, below(d, lambda e: psi_at(e, b, 0)), below(d, lambda e: psi_at(e, b, 1))),
-                )
-                for wr, wi, vr, vi in terms:
-                    acc_re = acc_re + (wr * vr - wi * vi)
-                    acc_im = acc_im + (wr * vi + wi * vr)
-                out_re = -(dens * re + acc_re * (1.0 / (DIAG * DIAG)))
-                out_im = -(dens * im + acc_im * (1.0 / (DIAG * DIAG)))
-                results.append((out_re, out_im))
-                if d == 0:
-                    out_ref[pl.ds(2 * b * planes, planes), :] = out_re
-                    out_ref[pl.ds((2 * b + 1) * planes, planes), :] = out_im
-            for a in range(bands):
-                re, im = psi_at(d, a, 0), psi_at(d, a, 1)
-                for b in range(bands):
-                    out_re, out_im = results[b]
-                    both = (re * out_re + im * out_im, re * out_im - im * out_re)
-                    for c in range(2):
-                        old = sums[a][b][c]
-                        sums[a][b][c] = both[c] if old is None else old + both[c]
+            held = [window(d, i) for i in range(FIELDS)]
+            re, im = held[4:]
+            fields.append(held[:4] + [re * cosine - im * sine, im * cosine + re * sine])
+
+        dens, x_both, y_re, y_im, z_re, z_im = fields[0]
+        dx_re, dx_im = halves(x_both)
+        below = [
+            jnp.where(row == 0, pltpu.roll(fields[count - 1][i], 1, 0), pltpu.roll(fields[0][i], 1, 0)) for i in (4, 5)
+        ]
+        factors = (
+            (jnp.concatenate([dx_re, dx_re], axis=1) * 2.0, jnp.concatenate([dx_im, -dx_im], axis=1) * 2.0),
+            (y_re, y_im),
+            (turn(y_re, -1), -turn(y_im, -1)),
+            (z_re, z_im),
+            (below[0], -below[1]),
+        )
+        dens = dens * DIAG
+        for b in range(bands):
+            around = [
+                [near_ref[pl.ds(((b * NEIGHBOURS + n) * 2 + c) * planes, planes), :] for c in range(2)]
+                for n in range(NEIGHBOURS)
+            ]
+            acc_re = dens * around[0][0]
+            acc_im = dens * around[0][1]
+            for (wr, wi), (vr, vi) in zip(factors, around[1:]):
+                acc_re = acc_re + (wr * vr - wi * vi)
+                acc_im = acc_im + (wr * vi + wi * vr)
+            out_ref[pl.ds(2 * b * planes, planes), :] = acc_re * (-1.0 / (DIAG * DIAG))
+            out_ref[pl.ds((2 * b + 1) * planes, planes), :] = acc_im * (-1.0 / (DIAG * DIAG))
+
+        found = {}
+        for q, key in enumerate(values):
+            total = jnp.zeros((planes, CELLS), jnp.float32)
+            for d in range(count):
+                for i in range(FIELDS):
+                    at = pl.ds(((d * len(values) + q) * FIELDS + i) * planes, planes)
+                    total = total + fields[d][i] * weight_ref[at, :]
+            total = jnp.sum(total[:, :CY] + total[:, CY:], axis=0, keepdims=True)
+            found[key] = jnp.sum(total, axis=1, keepdims=True)
         shape = (bands, 2)
         first = lax.broadcasted_iota(jnp.int32, shape, 0)
         second = lax.broadcasted_iota(jnp.int32, shape, 1)
         for a in range(bands):
             tile = jnp.zeros(shape, jnp.float32)
             for b in range(bands):
-                for c in range(2):
-                    folded = sums[a][b][c]
-                    folded = folded[:, :CY] + folded[:, CY:]
-                    value = jnp.sum(jnp.sum(folded, axis=0, keepdims=True), axis=1, keepdims=True)
-                    tile = jnp.where((first == b) & (second == c), value * scale, tile)
+                low, high = min(a, b), max(a, b)
+                tile = jnp.where((first == b) & (second == 0), found[low, high, 0], tile)
+                if a != b:
+                    imaginary = found[low, high, 1]
+                    tile = jnp.where((first == b) & (second == 1), imaginary if a < b else -imaginary, tile)
             tile_ref[0, a] = tile
 
     return pl.pallas_call(
@@ -283,11 +335,11 @@
             jax.ShapeDtypeStruct((2 * bands * planes, CELLS), jnp.float32),
             jax.ShapeDtypeStruct((1, bands, bands, 2), jnp.float32),
         ),
-        in_specs=[VMEM] * (len(parts) + 2),
+        in_specs=[VMEM] * (len(parts) + 3),
         out_specs=(VMEM, VMEM),
         compiler_params=PARAMS,
         name="apply_window",
-    )(phase, *parts, targets)
+    )(phase, *parts, near, weights)
 
 
 def shift(value, axis, distance):
@@ -317,8 +369,8 @@
     even = lax.rem(place, 2) == 0
     lacking = mine + jnp.where(even, right, left)
     other = lax.ppermute(lacking, "kring", [(i, i ^ 1) for i in range(cycle)])
-    other, psis = lax.optimization_barrier((other, stack(psis)))
-    exchange, tile = apply(phase, [mine, left, right, other], psis, planes, bands, slabs)
+    other, near, weights = lax.optimization_barrier((other, *ready_targets(psis, planes, bands)))
+    exchange, tile = apply(phase, [mine, right, left, other], near, weights, planes, bands, slabs)
     return exchange.reshape(targets.shape), tile
 
 

time: 18.2 us -> 18.1 us (level)
  transfers between devices with their start and end apart: 5 -> 5, of which waited for: 5 -> 5; matrix products, arithmetic and copies ran while one was open for 0% -> 0% of each run, Pallas kernels for 3% -> 4%
where the time goes in v6:
time: 18.1 us; the launch traced here: 18 us
  starting transfers between devices  9.62 us (53%)
  waiting for transfers between devices  4.32 us (24%)
  Pallas kernels  1.72 us (10%)
  between operations  1.42 us (8%)
  local copies, waits for them, and re-layouts  0.89 us (5%)
    ppermute x4, starting transfers between devices, shift(): lax.ppermute(value, axis, [((i + distance) % count, i) for i in range(cou...  9.55 us
    ppermute x4, waiting for transfers between devices, shift(): lax.ppermute(value, axis, [((i + distance) % count, i) for i in range(cou...  4.04 us
    unnamed x8, local copies, waits for them, and re-layouts  0.89 us
    pallas_call x1, Pallas kernels, apply(): pl.pallas_call(body, out_shape=(jax.ShapeDtypeStruct((2 * bands * planes,...  0.71 us
    pallas_call x1, Pallas kernels, phase_of(): pl.pallas_call(body, out_shape=jax.ShapeDtypeStruct((16, CY), jnp.float32...  0.6 us
  transfers between devices with their start and end apart: 5, of which 5 were waited for; matrix products, arithmetic and copies ran while one was open for 0% of the time, Pallas kernels for 4%

profile of v6, /device:TPU:0, one launch (start us, length us, event | category | flops | bytes accessed | tf_op | source)
XLA Modules:
  0.0 18.0 jit_solution(8042705265009175611)
XLA Ops:
  0.6 0.0 copy-start
  0.7 0.0 copy-start.3
  1.4 0.0 copy-done.3
  1.4 0.1 spread_mask.1.refs_1_
  1.5 0.2 %copy-done = f32[1,32,2,8,256]{4,3,2,1,0:T(8,128)S(1)} copy-done((f32[1,32,2,8,256]{4,3,2,1,0:T(8,128)S(1)}, f32[1,32,2,8,256]{4,3,2,1,0:T(8,128)}, u32[]{:S(2)}) %copy-start) | copy-done | bytes 524312
  1.7 0.2 %local_fields.1.refs_0_ = f32[112,256]{1,0:T(8,128)S(1)} custom-call(s32[1]{0:T(128)S(6)} %copy.7.refs_0_, f32[32,128]{1,0:T(8,128)S(1)} %spread_mask.1.refs_1_, f32[1024,128]{1,0:T(8,128)S(1)} %bitcast.14), custom_call_target="tpu_custom_call" | custom-call | tf_op jit(solution)/shard_map/local_fields/pallas_call | solution.py:112
  1.9 3.0 %collective-permute-start = (f32[112,256]{1,0:T(8,128)S(1)}, f32[112,256]{1,0:T(8,128)S(1)}, u32[]{:S(2)}, u32[]{:S(2)}) collective-permute-start(f32[112,256]{1,0:T(8,128)S(1)} %local_fields.1.refs_0_), channel_id=1, source_target_pairs={{1,0},{0,1},{3,2},{2,3},{5,4},{4,5},{7,6},{6,7},{9,8},{8,9},{11,10... | collective-permute-start | bytes 344072 | tf_op jit(solution)/shard_map/ppermute | solution.py:347
  4.9 0.0 copy-start.1
  4.9 0.7 %copy-done.1 = s32[16]{0:T(128)S(1)} copy-done((s32[16]{0:T(128)S(1)}, s32[16]{0:T(128)}, u32[]{:S(2)}) %copy-start.1) | copy-done | bytes 88
  5.6 0.6 %phase.1.phase_ref = f32[16,128]{1,0:T(8,128)S(1)} custom-call(s32[1]{0:T(128)} %bitcast.place_ref, s32[16]{0:T(128)S(1)} %copy-done.1), custom_call_target="tpu_custom_call" | custom-call | tf_op jit(solution)/shard_map/phase/pallas_call | solution.py:132
  6.2 0.0 copy-start.2
  6.2 1.9 %collective-permute-done.refs_1_ = f32[112,256]{1,0:T(8,128)S(1)} collective-permute-done((f32[112,256]{1,0:T(8,128)S(1)}, f32[112,256]{1,0:T(8,128)S(1)}, u32[]{:S(2)}, u32[]{:S(2)}) %collective-permute-start) | collective-permute-done | bytes 114720 | tf_op jit(solution)/shard_map/ppermute | solution.py:347
  8.1 1.8 %collective-permute-start.2 = (f32[96,256]{1,0:T(8,128)S(1)}, f32[96,256]{1,0:T(8,128)S(1)}, u32[]{:S(2)}, u32[]{:S(2)}) collective-permute-start(f32[96,256]{1,0:T(8,128)S(1)} %join_slabs.1.refs_0_), channel_id=1, source_target_pairs={{28,0},{30,2},{0,4},{2,6},{4,8},{6,10},{8,12},{10,14},{12,16},{14,... | collective-permute-start | bytes 294920 | tf_op jit(solution)/shard_map/ppermute | solution.py:347
  9.9 3.1 %collective-permute-start.1 = (f32[96,256]{1,0:T(8,128)S(1)}, f32[96,256]{1,0:T(8,128)S(1)}, u32[]{:S(2)}, u32[]{:S(2)}) collective-permute-start(f32[96,256]{1,0:T(8,128)S(1)} %join_slabs.1.refs_0_), channel_id=1, source_target_pairs={{4,0},{6,2},{8,4},{10,6},{12,8},{14,10},{16,12},{18,14},{20,16},{2... | collective-permute-start | bytes 294920 | tf_op jit(solution)/shard_map/ppermute | solution.py:347
  13.0 0.0 copy-done.2
  13.0 1.6 %collective-permute-start.4 = (f32[32,256]{1,0:T(8,128)S(1)}, f32[32,256]{1,0:T(8,128)S(1)}, u32[]{:S(2)}, u32[]{:S(2)}) collective-permute-start(f32[32,256]{1,0:T(8,128)S(1)} %bitcast.15), channel_id=1, source_target_pairs={{1,0},{0,1},{3,2},{2,3},{5,4},{4,5},{7,6},{6,7},{9,8},{8,9},{11,10... | collective-permute-start | bytes 98312 | tf_op jit(solution)/shard_map/ppermute | solution.py:347
  14.6 1.0 %collective-permute-done.2.refs_2_ = f32[96,256]{1,0:T(8,128)S(1)} collective-permute-done((f32[96,256]{1,0:T(8,128)S(1)}, f32[96,256]{1,0:T(8,128)S(1)}, u32[]{:S(2)}, u32[]{:S(2)}) %collective-permute-start.2) | collective-permute-done | bytes 98336 | tf_op jit(solution)/shard_map/ppermute | solution.py:347
  15.6 0.3 %collective-permute-done.1.refs_1_ = f32[96,256]{1,0:T(8,128)S(1)} collective-permute-done((f32[96,256]{1,0:T(8,128)S(1)}, f32[96,256]{1,0:T(8,128)S(1)}, u32[]{:S(2)}, u32[]{:S(2)}) %collective-permute-start.1) | collective-permute-done | bytes 98336 | tf_op jit(solution)/shard_map/ppermute | solution.py:347
  15.9 0.1 collective-permute-start.3
  16.0 0.9 %collective-permute-done.4.refs_1_ = f32[32,256]{1,0:T(8,128)S(1)} collective-permute-done((f32[32,256]{1,0:T(8,128)S(1)}, f32[32,256]{1,0:T(8,128)S(1)}, u32[]{:S(2)}, u32[]{:S(2)}) %collective-permute-start.4) | collective-permute-done | bytes 32800 | tf_op jit(solution)/shard_map/ppermute | solution.py:347
  16.9 0.1 ready_targets.1
  17.0 0.3 %collective-permute-done.3.refs_3_ = f32[96,256]{1,0:T(8,128)S(1)} collective-permute-done((f32[96,256]{1,0:T(8,128)S(1)}, f32[96,256]{1,0:T(8,128)S(1)}, u32[]{:S(2)}, u32[]{:S(2)}) %collective-permute-start.3) | collective-permute-done | bytes 98336 | tf_op jit(solution)/shard_map/ppermute | solution.py:371
  17.3 0.7 %apply_window.1 = (f32[32,256]{1,0:T(8,128)}, f32[1,2,2,2]{3,2,1,0:T(2,128)}) custom-call(f32[16,128]{1,0:T(8,128)S(1)} %phase.1.phase_ref, f32[96,256]{1,0:T(8,128)S(1)} %join_slabs.1.refs_0_, f32[96,256]{1,0:T(8,128)S(1)} %collective-permute-done.1.refs_1_, f32[96,256]{1,0:T(8,128)S(1)} %collective-permute-done.2.refs_2_, ...), custom_call_target="tpu_custom_call" | custom-call | tf_op jit(solution)/shard_map/apply_window/pallas_call | solution.py:332
  (4 shorter events, 0.1 us)
Async XLA Ops:
  0.6 1.1 %copy-start = (f32[1,32,2,8,256]{4,3,2,1,0:T(8,128)S(1)}, f32[1,32,2,8,256]{4,3,2,1,0:T(8,128)}, u32[]{:S(2)}) copy-start(f32[1,32,2,8,256]{4,3,2,1,0:T(8,128)} %param.6) | copy-start | bytes 1572868
  0.7 0.7 %copy-start.3 = (s32[1,32]{1,0:T(1,128)S(1)}, s32[1,32]{1,0:T(1,128)}, u32[]{:S(2)}) copy-start(s32[1,32]{1,0:T(1,128)} %param.8) | copy-start | bytes 388
  1.9 6.2 %collective-permute-start = (f32[112,256]{1,0:T(8,128)S(1)}, f32[112,256]{1,0:T(8,128)S(1)}, u32[]{:S(2)}, u32[]{:S(2)}) collective-permute-start(f32[112,256]{1,0:T(8,128)S(1)} %local_fields.1.refs_0_), channel_id=1, source_target_pairs={{1,0},{0,1},{3,2},{2,3},{5,4},{4,5},{7,6},{6,7},{9,8},{8,9},{11,10... | collective-permute-start | bytes 344072 | tf_op jit(solution)/shard_map/ppermute | solution.py:347
  4.9 0.7 %copy-start.1 = (s32[16]{0:T(128)S(1)}, s32[16]{0:T(128)}, u32[]{:S(2)}) copy-start(s32[16]{0:T(128)} %kpoint_hbm.1) | copy-start | bytes 196
  6.2 6.8 %copy-start.2 = (f32[1,2,2,8,256]{4,3,2,1,0:T(8,128)S(1)}, f32[1,2,2,8,256]{4,3,2,1,0:T(8,128)}, u32[]{:S(2)}) copy-start(f32[1,2,2,8,256]{4,3,2,1,0:T(8,128)} %param.5) | copy-start | bytes 98308
  8.1 7.5 %collective-permute-start.2 = (f32[96,256]{1,0:T(8,128)S(1)}, f32[96,256]{1,0:T(8,128)S(1)}, u32[]{:S(2)}, u32[]{:S(2)}) collective-permute-start(f32[96,256]{1,0:T(8,128)S(1)} %join_slabs.1.refs_0_), channel_id=1, source_target_pairs={{28,0},{30,2},{0,4},{2,6},{4,8},{6,10},{8,12},{10,14},{12,16},{14,... | collective-permute-start | bytes 294920 | tf_op jit(solution)/shard_map/ppermute | solution.py:347
  9.9 6.0 %collective-permute-start.1 = (f32[96,256]{1,0:T(8,128)S(1)}, f32[96,256]{1,0:T(8,128)S(1)}, u32[]{:S(2)}, u32[]{:S(2)}) collective-permute-start(f32[96,256]{1,0:T(8,128)S(1)} %join_slabs.1.refs_0_), channel_id=1, source_target_pairs={{4,0},{6,2},{8,4},{10,6},{12,8},{14,10},{16,12},{18,14},{20,16},{2... | collective-permute-start | bytes 294920 | tf_op jit(solution)/shard_map/ppermute | solution.py:347
  13.0 3.9 %collective-permute-start.4 = (f32[32,256]{1,0:T(8,128)S(1)}, f32[32,256]{1,0:T(8,128)S(1)}, u32[]{:S(2)}, u32[]{:S(2)}) collective-permute-start(f32[32,256]{1,0:T(8,128)S(1)} %bitcast.15), channel_id=1, source_target_pairs={{1,0},{0,1},{3,2},{2,3},{5,4},{4,5},{7,6},{6,7},{9,8},{8,9},{11,10... | collective-permute-start | bytes 98312 | tf_op jit(solution)/shard_map/ppermute | solution.py:347
  15.9 1.4 %collective-permute-start.3 = (f32[96,256]{1,0:T(8,128)S(1)}, f32[96,256]{1,0:T(8,128)S(1)}, u32[]{:S(2)}, u32[]{:S(2)}) collective-permute-start(f32[96,256]{1,0:T(8,128)S(1)} %select_add_fusion), channel_id=1, source_target_pairs={{0,2},{2,0},{4,6},{6,4},{8,10},{10,8},{12,14},{14,12},{16,18},{18,... | collective-permute-start | bytes 294920 | tf_op jit(solution)/shard_map/ppermute | solution.py:371

commit v7 on v6

--- a/solution.py
+++ b/solution.py
@@ -12,6 +12,7 @@
 CELLS = CX * CY
 BLOCK = 16
 FIELDS = 6
+SENT = 5
 NEIGHBOURS = 6
 CHUNKS = 1
 DIAG = 7.0
@@ -41,9 +42,9 @@
     return ar * br + ai * bi, ai * br - ar * bi
 
 
-def gather_kernel(planes, index_ref, weight_ref, orb, pack_ref):
+def gather_kernel(planes, index_ref, weight_ref, orb, own_ref, pack_ref):
     rows = 2 * CX * planes
-    field_rows = FIELDS * planes
+    field_rows = SENT * planes
     first = index_ref[0] * BLOCK
     none = jnp.zeros((planes, CY), jnp.float32)
     dens, dy_re, dy_im, dz_re, dz_im = [[none] * CX for _ in range(5)]
@@ -61,9 +62,18 @@
             dy_re[x], dy_im[x] = dy_re[x] + part[0], dy_im[x] + part[1]
             part = bond(re[x], im[x], pltpu.roll(re[x], planes - 1, 0), pltpu.roll(im[x], planes - 1, 0))
             dz_re[x], dz_im[x] = dz_re[x] + part[0], dz_im[x] + part[1]
+    row = lax.broadcasted_iota(jnp.int32, (planes, CY), 0)
     for i, field in enumerate((dens, (dx_re, dx_im), dy_re, dy_im, dz_re, dz_im)):
         for x in range(CX):
-            pack_ref[pl.ds(i * planes, planes), pl.ds(x * CY, CY)] = field[x]
+            own_ref[pl.ds(i * planes, planes), pl.ds(x * CY, CY)] = field[x]
+            if i == SENT:
+                continue
+            sent = field[x]
+            if i < SENT - 1:
+                low = pltpu.roll(dz_im[x], (-2 * i) % planes, 0)
+                high = pltpu.roll(dz_im[x], (planes - 2 - 2 * i) % planes, 0)
+                sent = jnp.where(row == 0, low, jnp.where(row == planes - 1, high, sent))
+            pack_ref[pl.ds(i * planes, planes), pl.ds(x * CY, CY)] = sent
     column = weight_ref[pl.ds(pl.multiple_of(first, BLOCK), BLOCK), :]
     for e, plane in enumerate((0, planes - 1)):
         for c in range(2):
@@ -111,9 +121,12 @@
 
     return pl.pallas_call(
         body,
-        out_shape=jax.ShapeDtypeStruct((FIELDS * planes + 4 * BLOCK, CELLS), jnp.float32),
+        out_shape=(
+            jax.ShapeDtypeStruct((FIELDS * planes, CELLS), jnp.float32),
+            jax.ShapeDtypeStruct((SENT * planes + 4 * BLOCK, CELLS), jnp.float32),
+        ),
         in_specs=[SMEM, VMEM, VMEM],
-        out_specs=VMEM,
+        out_specs=(VMEM, VMEM),
         compiler_params=PARAMS,
         name="local_fields",
     )(block_index, weights, orb)
@@ -225,37 +238,60 @@
     return [(a, b, part) for a in range(bands) for b in range(a, bands) for part in range(2 if b > a else 1)]
 
 
-def join(phase, packs, planes):
+def join(phase, own, packs, planes):
     count = len(packs)
     field_rows = FIELDS * planes
 
-    def body(phase_ref, *refs):
+    def body(phase_ref, own_ref, *refs):
         ins, out = refs[:count], refs[count]
         cosine, sine = phase_rows(phase_ref)
-        last = lax.broadcasted_iota(jnp.int32, (planes, CELLS), 0) == planes - 1
-
-        def end(ref, e, c):
-            return ref[pl.ds(field_rows + (2 * e + c) * BLOCK, BLOCK), :]
+        row = lax.broadcasted_iota(jnp.int32, (planes, CELLS), 0)
+
+        def total(value):
+            return jnp.sum(value, axis=0, keepdims=True)
+
+        def end(ref, e):
+            return [ref[pl.ds(SENT * planes + (2 * e + c) * BLOCK, BLOCK), :] for c in range(2)]
+
+        def rebuilt(ref):
+            held = [ref[pl.ds(i * planes, planes), :] for i in range(SENT)]
+            last = held[0]
+            for i in range(SENT - 1):
+                last = jnp.where(row == 2 * i, pltpu.roll(held[i], 2 * i, 0), last)
+                last = jnp.where(row == 2 * i + 1, pltpu.roll(held[i], (2 * i + 2 - planes) % planes, 0), last)
+            for e, place in ((0, 0), (1, planes - 1)):
+                re, im = end(ref, e)
+                (re0, re1), (im0, im1) = halves(re), halves(im)
+                values = (
+                    re * re + im * im,
+                    jnp.concatenate(bond(re0, im0, re1, im1), axis=1),
+                    *bond(re, im, turn(re, 1), turn(im, 1)),
+                )
+                for i, value in enumerate(values):
+                    held[i] = jnp.where(row == place, total(value), held[i])
+            return held + [last]
 
         for d in range(count):
             here, there = ins[d], ins[(d + 1) % count]
-            out[pl.ds(d * field_rows, 4 * planes), :] = here[pl.ds(0, 4 * planes), :]
-            re, im = bond(end(here, 1, 0), end(here, 1, 1), end(there, 0, 0), end(there, 0, 1))
-            re = jnp.sum(re, axis=0, keepdims=True)
-            im = jnp.sum(im, axis=0, keepdims=True)
-            re = jnp.where(last, re, here[pl.ds(4 * planes, planes), :])
-            im = jnp.where(last, im, here[pl.ds(5 * planes, planes), :])
-            out[pl.ds(d * field_rows + 4 * planes, planes), :] = re * cosine + im * sine
-            out[pl.ds(d * field_rows + 5 * planes, planes), :] = im * cosine - re * sine
+            if d == 0:
+                held = [own_ref[pl.ds(i * planes, planes), :] for i in range(FIELDS)]
+            else:
+                held = rebuilt(here)
+            re, im = bond(*end(here, 1), *end(there, 0))
+            re = jnp.where(row == planes - 1, total(re), held[4])
+            im = jnp.where(row == planes - 1, total(im), held[5])
+            held[4:] = [re * cosine + im * sine, im * cosine - re * sine]
+            for i, field in enumerate(held):
+                out[pl.ds(d * field_rows + i * planes, planes), :] = field
 
     return pl.pallas_call(
         body,
         out_shape=jax.ShapeDtypeStruct((count * field_rows, CELLS), jnp.float32),
-        in_specs=[VMEM] + [VMEM] * count,
+        in_specs=[VMEM] * (2 + count),
         out_specs=VMEM,
         compiler_params=PARAMS,
         name="join_slabs",
-    )(phase, *packs)
+    )(phase, own, *packs)
 
 
 def apply(phase, parts, near, weights, planes, bands, count):
@@ -359,10 +395,10 @@
     held = occupied.shape[1]
     words = occupied + 2 * lax.pad(block_index, jnp.int32(0), [(0, held - 1, 0)]).reshape(1, held)
     mask = (words & 1).astype(jnp.float32)
-    own = gather(block_index, spread(mask, diagonal(held)), orb, planes)
-    packs = [own] + [shift(own, "slab", d) for d in range(1, slabs)]
+    own, pack = gather(block_index, spread(mask, diagonal(held)), orb, planes)
+    packs = [pack] + [shift(pack, "slab", d) for d in range(1, slabs)]
     psis = [psi] + [shift(psi, "slab", d) for d in range(1, slabs)]
-    mine = join(phase, packs, planes)
+    mine = join(phase, own, packs, planes)
 
     left = shift(mine, "kring", -2)
     right = shift(mine, "kring", 2)

time: 18.1 us -> 18 us (level)
  no operation moved by 1% of the time
where the time goes in v7:
time: 18 us; the launch traced here: 17.9 us
  starting transfers between devices  9.62 us (53%)
  waiting for transfers between devices  4.15 us (23%)
  Pallas kernels  1.78 us (10%)
  between operations  1.41 us (8%)
  local copies, waits for them, and re-layouts  0.89 us (5%)
    ppermute x4, starting transfers between devices, shift(): lax.ppermute(value, axis, [((i + distance) % count, i) for i in range(cou...  9.55 us
    ppermute x4, waiting for transfers between devices, shift(): lax.ppermute(value, axis, [((i + distance) % count, i) for i in range(cou...  3.88 us
    unnamed x8, local copies, waits for them, and re-layouts  0.89 us
    pallas_call x1, Pallas kernels, apply(): pl.pallas_call(body, out_shape=(jax.ShapeDtypeStruct((2 * bands * planes,...  0.71 us
    pallas_call x1, Pallas kernels, phase_of(): pl.pallas_call(body, out_shape=jax.ShapeDtypeStruct((16, CY), jnp.float32...  0.6 us
  transfers between devices with their start and end apart: 5, of which 5 were waited for; matrix products, arithmetic and copies ran while one was open for 0% of the time, Pallas kernels for 4%

profile of v7, /device:TPU:0, one launch (start us, length us, event | category | flops | bytes accessed | tf_op | source)
XLA Modules:
  0.0 17.9 jit_solution(17427150962201699497)
XLA Ops:
  0.6 0.0 copy-start
  0.7 0.0 copy-start.3
  1.4 0.0 copy-done.3
  1.4 0.1 spread_mask.1.refs_1_
  1.5 0.2 %copy-done = f32[1,32,2,8,256]{4,3,2,1,0:T(8,128)S(1)} copy-done((f32[1,32,2,8,256]{4,3,2,1,0:T(8,128)S(1)}, f32[1,32,2,8,256]{4,3,2,1,0:T(8,128)}, u32[]{:S(2)}) %copy-start) | copy-done | bytes 524312
  1.7 0.2 %local_fields.1 = (f32[48,256]{1,0:T(8,128)S(1)}, f32[104,256]{1,0:T(8,128)S(1)}) custom-call(s32[1]{0:T(128)S(6)} %copy.7.refs_0_, f32[32,128]{1,0:T(8,128)S(1)} %spread_mask.1.refs_1_, f32[1024,128]{1,0:T(8,128)S(1)} %bitcast.14), custom_call_target="tpu_custom_call" | custom-call | tf_op jit(solution)/shard_map/local_fields/pallas_call | solution.py:122
  1.9 3.0 %collective-permute-start = (f32[104,256]{1,0:T(8,128)S(1)}, f32[104,256]{1,0:T(8,128)S(1)}, u32[]{:S(2)}, u32[]{:S(2)}) collective-permute-start(f32[104,256]{1,0:T(8,128)S(1)} %get-tuple-element.12.refs_0_), channel_id=1, source_target_pairs={{1,0},{0,1},{3,2},{2,3},{5,4},{4,5},{7,6},{6,7},{9,8},{8,9},{11,10... | collective-permute-start | bytes 319496 | tf_op jit(solution)/shard_map/ppermute | solution.py:383
  4.9 0.0 copy-start.1
  4.9 0.7 %copy-done.1 = s32[16]{0:T(128)S(1)} copy-done((s32[16]{0:T(128)S(1)}, s32[16]{0:T(128)}, u32[]{:S(2)}) %copy-start.1) | copy-done | bytes 88
  5.6 0.6 %phase.1.phase_ref = f32[16,128]{1,0:T(8,128)S(1)} custom-call(s32[1]{0:T(128)} %bitcast.place_ref, s32[16]{0:T(128)S(1)} %copy-done.1), custom_call_target="tpu_custom_call" | custom-call | tf_op jit(solution)/shard_map/phase/pallas_call | solution.py:145
  6.2 1.7 %collective-permute-done.refs_1_ = f32[104,256]{1,0:T(8,128)S(1)} collective-permute-done((f32[104,256]{1,0:T(8,128)S(1)}, f32[104,256]{1,0:T(8,128)S(1)}, u32[]{:S(2)}, u32[]{:S(2)}) %collective-permute-start) | collective-permute-done | bytes 106528 | tf_op jit(solution)/shard_map/ppermute | solution.py:383
  7.9 0.0 copy-start.2
  7.9 0.1 join_slabs.1.refs_0_
  8.0 1.8 %collective-permute-start.2 = (f32[96,256]{1,0:T(8,128)S(1)}, f32[96,256]{1,0:T(8,128)S(1)}, u32[]{:S(2)}, u32[]{:S(2)}) collective-permute-start(f32[96,256]{1,0:T(8,128)S(1)} %join_slabs.1.refs_0_), channel_id=1, source_target_pairs={{28,0},{30,2},{0,4},{2,6},{4,8},{6,10},{8,12},{10,14},{12,16},{14,... | collective-permute-start | bytes 294920 | tf_op jit(solution)/shard_map/ppermute | solution.py:383
  9.8 3.1 %collective-permute-start.1 = (f32[96,256]{1,0:T(8,128)S(1)}, f32[96,256]{1,0:T(8,128)S(1)}, u32[]{:S(2)}, u32[]{:S(2)}) collective-permute-start(f32[96,256]{1,0:T(8,128)S(1)} %join_slabs.1.refs_0_), channel_id=1, source_target_pairs={{4,0},{6,2},{8,4},{10,6},{12,8},{14,10},{16,12},{18,14},{20,16},{2... | collective-permute-start | bytes 294920 | tf_op jit(solution)/shard_map/ppermute | solution.py:383
  12.9 0.0 copy-done.2
  12.9 1.6 %collective-permute-start.4 = (f32[32,256]{1,0:T(8,128)S(1)}, f32[32,256]{1,0:T(8,128)S(1)}, u32[]{:S(2)}, u32[]{:S(2)}) collective-permute-start(f32[32,256]{1,0:T(8,128)S(1)} %bitcast.15), channel_id=1, source_target_pairs={{1,0},{0,1},{3,2},{2,3},{5,4},{4,5},{7,6},{6,7},{9,8},{8,9},{11,10... | collective-permute-start | bytes 98312 | tf_op jit(solution)/shard_map/ppermute | solution.py:383
  14.5 1.0 %collective-permute-done.2.refs_2_ = f32[96,256]{1,0:T(8,128)S(1)} collective-permute-done((f32[96,256]{1,0:T(8,128)S(1)}, f32[96,256]{1,0:T(8,128)S(1)}, u32[]{:S(2)}, u32[]{:S(2)}) %collective-permute-start.2) | collective-permute-done | bytes 98336 | tf_op jit(solution)/shard_map/ppermute | solution.py:383
  15.5 0.3 %collective-permute-done.1.refs_1_ = f32[96,256]{1,0:T(8,128)S(1)} collective-permute-done((f32[96,256]{1,0:T(8,128)S(1)}, f32[96,256]{1,0:T(8,128)S(1)}, u32[]{:S(2)}, u32[]{:S(2)}) %collective-permute-start.1) | collective-permute-done | bytes 98336 | tf_op jit(solution)/shard_map/ppermute | solution.py:383
  15.8 0.1 collective-permute-start.3
  15.9 0.9 %collective-permute-done.4.refs_1_ = f32[32,256]{1,0:T(8,128)S(1)} collective-permute-done((f32[32,256]{1,0:T(8,128)S(1)}, f32[32,256]{1,0:T(8,128)S(1)}, u32[]{:S(2)}, u32[]{:S(2)}) %collective-permute-start.4) | collective-permute-done | bytes 32800 | tf_op jit(solution)/shard_map/ppermute | solution.py:383
  16.8 0.1 ready_targets.1
  16.9 0.3 %collective-permute-done.3.refs_3_ = f32[96,256]{1,0:T(8,128)S(1)} collective-permute-done((f32[96,256]{1,0:T(8,128)S(1)}, f32[96,256]{1,0:T(8,128)S(1)}, u32[]{:S(2)}, u32[]{:S(2)}) %collective-permute-start.3) | collective-permute-done | bytes 98336 | tf_op jit(solution)/shard_map/ppermute | solution.py:407
  17.2 0.7 %apply_window.1 = (f32[32,256]{1,0:T(8,128)}, f32[1,2,2,2]{3,2,1,0:T(2,128)}) custom-call(f32[16,128]{1,0:T(8,128)S(1)} %phase.1.phase_ref, f32[96,256]{1,0:T(8,128)S(1)} %join_slabs.1.refs_0_, f32[96,256]{1,0:T(8,128)S(1)} %collective-permute-done.1.refs_1_, f32[96,256]{1,0:T(8,128)S(1)} %collective-permute-done.2.refs_2_, ...), custom_call_target="tpu_custom_call" | custom-call | tf_op jit(solution)/shard_map/apply_window/pallas_call | solution.py:368
  (3 shorter events, 0.0 us)
Async XLA Ops:
  0.6 1.1 %copy-start = (f32[1,32,2,8,256]{4,3,2,1,0:T(8,128)S(1)}, f32[1,32,2,8,256]{4,3,2,1,0:T(8,128)}, u32[]{:S(2)}) copy-start(f32[1,32,2,8,256]{4,3,2,1,0:T(8,128)} %param.6) | copy-start | bytes 1572868
  0.7 0.7 %copy-start.3 = (s32[1,32]{1,0:T(1,128)S(1)}, s32[1,32]{1,0:T(1,128)}, u32[]{:S(2)}) copy-start(s32[1,32]{1,0:T(1,128)} %param.8) | copy-start | bytes 388
  1.9 6.0 %collective-permute-start = (f32[104,256]{1,0:T(8,128)S(1)}, f32[104,256]{1,0:T(8,128)S(1)}, u32[]{:S(2)}, u32[]{:S(2)}) collective-permute-start(f32[104,256]{1,0:T(8,128)S(1)} %get-tuple-element.12.refs_0_), channel_id=1, source_target_pairs={{1,0},{0,1},{3,2},{2,3},{5,4},{4,5},{7,6},{6,7},{9,8},{8,9},{11,10... | collective-permute-start | bytes 319496 | tf_op jit(solution)/shard_map/ppermute | solution.py:383
  4.9 0.7 %copy-start.1 = (s32[16]{0:T(128)S(1)}, s32[16]{0:T(128)}, u32[]{:S(2)}) copy-start(s32[16]{0:T(128)} %kpoint_hbm.1) | copy-start | bytes 196
  7.9 5.0 %copy-start.2 = (f32[1,2,2,8,256]{4,3,2,1,0:T(8,128)S(1)}, f32[1,2,2,8,256]{4,3,2,1,0:T(8,128)}, u32[]{:S(2)}) copy-start(f32[1,2,2,8,256]{4,3,2,1,0:T(8,128)} %param.5) | copy-start | bytes 98308
  8.0 7.5 %collective-permute-start.2 = (f32[96,256]{1,0:T(8,128)S(1)}, f32[96,256]{1,0:T(8,128)S(1)}, u32[]{:S(2)}, u32[]{:S(2)}) collective-permute-start(f32[96,256]{1,0:T(8,128)S(1)} %join_slabs.1.refs_0_), channel_id=1, source_target_pairs={{28,0},{30,2},{0,4},{2,6},{4,8},{6,10},{8,12},{10,14},{12,16},{14,... | collective-permute-start | bytes 294920 | tf_op jit(solution)/shard_map/ppermute | solution.py:383
  9.8 6.0 %collective-permute-start.1 = (f32[96,256]{1,0:T(8,128)S(1)}, f32[96,256]{1,0:T(8,128)S(1)}, u32[]{:S(2)}, u32[]{:S(2)}) collective-permute-start(f32[96,256]{1,0:T(8,128)S(1)} %join_slabs.1.refs_0_), channel_id=1, source_target_pairs={{4,0},{6,2},{8,4},{10,6},{12,8},{14,10},{16,12},{18,14},{20,16},{2... | collective-permute-start | bytes 294920 | tf_op jit(solution)/shard_map/ppermute | solution.py:383
  12.9 3.9 %collective-permute-start.4 = (f32[32,256]{1,0:T(8,128)S(1)}, f32[32,256]{1,0:T(8,128)S(1)}, u32[]{:S(2)}, u32[]{:S(2)}) collective-permute-start(f32[32,256]{1,0:T(8,128)S(1)} %bitcast.15), channel_id=1, source_target_pairs={{1,0},{0,1},{3,2},{2,3},{5,4},{4,5},{7,6},{6,7},{9,8},{8,9},{11,10... | collective-permute-start | bytes 98312 | tf_op jit(solution)/shard_map/ppermute | solution.py:383
  15.8 1.4 %collective-permute-start.3 = (f32[96,256]{1,0:T(8,128)S(1)}, f32[96,256]{1,0:T(8,128)S(1)}, u32[]{:S(2)}, u32[]{:S(2)}) collective-permute-start(f32[96,256]{1,0:T(8,128)S(1)} %select_add_fusion), channel_id=1, source_target_pairs={{0,2},{2,0},{4,6},{6,4},{8,10},{10,8},{12,14},{14,12},{16,18},{18,... | collective-permute-start | bytes 294920 | tf_op jit(solution)/shard_map/ppermute | solution.py:407

commit v8 on v7

--- a/solution.py
+++ b/solution.py
@@ -52,15 +52,17 @@
     for m in range(BLOCK):
         base = pl.multiple_of((first + m) * rows, 8)
         weight = weight_ref[pl.ds(first + m, 1), :]
-        re = [orb[pl.ds(base + x * planes, planes), :] * weight for x in range(CX)]
-        im = [orb[pl.ds(base + (CX + x) * planes, planes), :] * weight for x in range(CX)]
-        part = bond(re[0], im[0], re[1], im[1])
+        raw_re = [orb[pl.ds(base + x * planes, planes), :] for x in range(CX)]
+        raw_im = [orb[pl.ds(base + (CX + x) * planes, planes), :] for x in range(CX)]
+        re = [value * weight for value in raw_re]
+        im = [value * weight for value in raw_im]
+        part = bond(re[0], im[0], raw_re[1], raw_im[1])
         dx_re, dx_im = dx_re + part[0], dx_im + part[1]
         for x in range(CX):
-            dens[x] = dens[x] + (re[x] * re[x] + im[x] * im[x])
-            part = bond(re[x], im[x], pltpu.roll(re[x], CY - 1, 1), pltpu.roll(im[x], CY - 1, 1))
+            dens[x] = dens[x] + (re[x] * raw_re[x] + im[x] * raw_im[x])
+            part = bond(re[x], im[x], pltpu.roll(raw_re[x], CY - 1, 1), pltpu.roll(raw_im[x], CY - 1, 1))
             dy_re[x], dy_im[x] = dy_re[x] + part[0], dy_im[x] + part[1]
-            part = bond(re[x], im[x], pltpu.roll(re[x], planes - 1, 0), pltpu.roll(im[x], planes - 1, 0))
+            part = bond(re[x], im[x], pltpu.roll(raw_re[x], planes - 1, 0), pltpu.roll(raw_im[x], planes - 1, 0))
             dz_re[x], dz_im[x] = dz_re[x] + part[0], dz_im[x] + part[1]
     row = lax.broadcasted_iota(jnp.int32, (planes, CY), 0)
     for i, field in enumerate((dens, (dx_re, dx_im), dy_re, dy_im, dz_re, dz_im)):
@@ -157,13 +159,18 @@
     return [jnp.concatenate([ref[pl.ds(8 * i, 1), :]] * CX, axis=1) for i in range(2)]
 
 
-def ready_targets(targets, planes, bands):
+def ready_targets(targets, parts, planes, bands):
     count = len(targets)
     cells = count * planes * CELLS
     values = tile_values(bands)
 
     def body(*refs):
-        ins, near_ref, weight_ref = refs[:count], refs[count], refs[count + 1]
+        ins, part_refs = refs[:count], refs[count : count + len(parts)]
+        near_ref, weight_ref, sum_ref = refs[count + len(parts) :]
+        total = part_refs[0][...]
+        for ref in part_refs[1:]:
+            total = total + ref[...]
+        sum_ref[...] = total
         row = lax.broadcasted_iota(jnp.int32, (planes, CELLS), 0)
 
         def psi_at(d, b):
@@ -225,13 +232,14 @@
         out_shape=(
             jax.ShapeDtypeStruct((bands * NEIGHBOURS * 2 * planes, CELLS), jnp.float32),
             jax.ShapeDtypeStruct((count * len(values) * FIELDS * planes, CELLS), jnp.float32),
+            jax.ShapeDtypeStruct(parts[0].shape, jnp.float32),
         ),
-        in_specs=[VMEM] * count,
-        out_specs=(VMEM, VMEM),
+        in_specs=[VMEM] * (count + len(parts)),
+        out_specs=(VMEM, VMEM, VMEM),
         compiler_params=PARAMS,
         cost_estimate=pl.CostEstimate(flops=1000000000, bytes_accessed=0, transcendentals=0),
         name="ready_targets",
-    )(*targets)
+    )(*targets, *parts)
 
 
 def tile_values(bands):
@@ -402,11 +410,12 @@
 
     left = shift(mine, "kring", -2)
     right = shift(mine, "kring", 2)
-    even = lax.rem(place, 2) == 0
-    lacking = mine + jnp.where(even, right, left)
+    odd = lax.rem(place, 2) == 1
+    lacking = jnp.where(odd, left, right) + mine
     other = lax.ppermute(lacking, "kring", [(i, i ^ 1) for i in range(cycle)])
-    other, near, weights = lax.optimization_barrier((other, *ready_targets(psis, planes, bands)))
-    exchange, tile = apply(phase, [mine, right, left, other], near, weights, planes, bands, slabs)
+    held = ready_targets(psis, [mine, right, left], planes, bands)
+    other, near, weights, total = lax.optimization_barrier((other, *held))
+    exchange, tile = apply(phase, [total, other], near, weights, planes, bands, slabs)
     return exchange.reshape(targets.shape), tile
 
 

time: 18 us -> 18 us (level)
  no operation moved by 1% of the time
where the time goes in v8:
time: 18 us; the launch traced here: 17.9 us
  starting transfers between devices  9.62 us (53%)
  waiting for transfers between devices  4.16 us (23%)
  Pallas kernels  1.75 us (10%)
  between operations  1.41 us (8%)
  local copies, waits for them, and re-layouts  0.89 us (5%)
    ppermute x4, starting transfers between devices, shift(): lax.ppermute(value, axis, [((i + distance) % count, i) for i in range(cou...  9.55 us
    ppermute x4, waiting for transfers between devices, shift(): lax.ppermute(value, axis, [((i + distance) % count, i) for i in range(cou...  3.88 us
    unnamed x8, local copies, waits for them, and re-layouts  0.89 us
    pallas_call x1, Pallas kernels, apply(): pl.pallas_call(body, out_shape=(jax.ShapeDtypeStruct((2 * bands * planes,...  0.71 us
    pallas_call x1, Pallas kernels, phase_of(): pl.pallas_call(body, out_shape=jax.ShapeDtypeStruct((16, CY), jnp.float32...  0.6 us
  transfers between devices with their start and end apart: 5, of which 5 were waited for; matrix products, arithmetic and copies ran while one was open for 0% of the time, Pallas kernels for 4%

profile of v8, /device:TPU:0, one launch (start us, length us, event | category | flops | bytes accessed | tf_op | source)
XLA Modules:
  0.0 17.9 jit_solution(1192781681082770388)
XLA Ops:
  0.6 0.0 copy-start
  0.7 0.0 copy-start.3
  1.4 0.0 copy-done.3
  1.4 0.1 spread_mask.1.refs_1_
  1.5 0.2 %copy-done = f32[1,32,2,8,256]{4,3,2,1,0:T(8,128)S(1)} copy-done((f32[1,32,2,8,256]{4,3,2,1,0:T(8,128)S(1)}, f32[1,32,2,8,256]{4,3,2,1,0:T(8,128)}, u32[]{:S(2)}) %copy-start) | copy-done | bytes 524312
  1.7 0.2 local_fields.1
  1.9 3.0 %collective-permute-start = (f32[104,256]{1,0:T(8,128)S(1)}, f32[104,256]{1,0:T(8,128)S(1)}, u32[]{:S(2)}, u32[]{:S(2)}) collective-permute-start(f32[104,256]{1,0:T(8,128)S(1)} %get-tuple-element.14.refs_0_), channel_id=1, source_target_pairs={{1,0},{0,1},{3,2},{2,3},{5,4},{4,5},{7,6},{6,7},{9,8},{8,9},{11,10... | collective-permute-start | bytes 319496 | tf_op jit(solution)/shard_map/ppermute | solution.py:391
  4.9 0.0 copy-start.1
  4.9 0.7 %copy-done.1 = s32[16]{0:T(128)S(1)} copy-done((s32[16]{0:T(128)S(1)}, s32[16]{0:T(128)}, u32[]{:S(2)}) %copy-start.1) | copy-done | bytes 88
  5.6 0.6 %phase.1.phase_ref = f32[16,128]{1,0:T(8,128)S(1)} custom-call(s32[1]{0:T(128)} %bitcast.place_ref, s32[16]{0:T(128)S(1)} %copy-done.1), custom_call_target="tpu_custom_call" | custom-call | tf_op jit(solution)/shard_map/phase/pallas_call | solution.py:147
  6.2 1.7 %collective-permute-done.refs_1_ = f32[104,256]{1,0:T(8,128)S(1)} collective-permute-done((f32[104,256]{1,0:T(8,128)S(1)}, f32[104,256]{1,0:T(8,128)S(1)}, u32[]{:S(2)}, u32[]{:S(2)}) %collective-permute-start) | collective-permute-done | bytes 106528 | tf_op jit(solution)/shard_map/ppermute | solution.py:391
  7.9 0.0 copy-start.2
  7.9 0.1 join_slabs.1.refs_2_
  8.0 1.8 %collective-permute-start.1 = (f32[96,256]{1,0:T(8,128)S(1)}, f32[96,256]{1,0:T(8,128)S(1)}, u32[]{:S(2)}, u32[]{:S(2)}) collective-permute-start(f32[96,256]{1,0:T(8,128)S(1)} %join_slabs.1.refs_2_), channel_id=1, source_target_pairs={{28,0},{30,2},{0,4},{2,6},{4,8},{6,10},{8,12},{10,14},{12,16},{14,... | collective-permute-start | bytes 294920 | tf_op jit(solution)/shard_map/ppermute | solution.py:391
  9.7 3.1 %collective-permute-start.2 = (f32[96,256]{1,0:T(8,128)S(1)}, f32[96,256]{1,0:T(8,128)S(1)}, u32[]{:S(2)}, u32[]{:S(2)}) collective-permute-start(f32[96,256]{1,0:T(8,128)S(1)} %join_slabs.1.refs_2_), channel_id=1, source_target_pairs={{4,0},{6,2},{8,4},{10,6},{12,8},{14,10},{16,12},{18,14},{20,16},{2... | collective-permute-start | bytes 294920 | tf_op jit(solution)/shard_map/ppermute | solution.py:391
  12.8 0.0 copy-done.2
  12.9 1.6 %collective-permute-start.4 = (f32[32,256]{1,0:T(8,128)S(1)}, f32[32,256]{1,0:T(8,128)S(1)}, u32[]{:S(2)}, u32[]{:S(2)}) collective-permute-start(f32[32,256]{1,0:T(8,128)S(1)} %bitcast.15), channel_id=1, source_target_pairs={{1,0},{0,1},{3,2},{2,3},{5,4},{4,5},{7,6},{6,7},{9,8},{8,9},{11,10... | collective-permute-start | bytes 98312 | tf_op jit(solution)/shard_map/ppermute | solution.py:391
  14.5 1.0 %collective-permute-done.1.refs_4_ = f32[96,256]{1,0:T(8,128)S(1)} collective-permute-done((f32[96,256]{1,0:T(8,128)S(1)}, f32[96,256]{1,0:T(8,128)S(1)}, u32[]{:S(2)}, u32[]{:S(2)}) %collective-permute-start.1) | collective-permute-done | bytes 98336 | tf_op jit(solution)/shard_map/ppermute | solution.py:391
  15.5 0.3 %collective-permute-done.2.refs_3_ = f32[96,256]{1,0:T(8,128)S(1)} collective-permute-done((f32[96,256]{1,0:T(8,128)S(1)}, f32[96,256]{1,0:T(8,128)S(1)}, u32[]{:S(2)}, u32[]{:S(2)}) %collective-permute-start.2) | collective-permute-done | bytes 98336 | tf_op jit(solution)/shard_map/ppermute | solution.py:391
  15.8 0.1 collective-permute-start.3
  15.9 0.9 %collective-permute-done.4.refs_1_ = f32[32,256]{1,0:T(8,128)S(1)} collective-permute-done((f32[32,256]{1,0:T(8,128)S(1)}, f32[32,256]{1,0:T(8,128)S(1)}, u32[]{:S(2)}, u32[]{:S(2)}) %collective-permute-start.4) | collective-permute-done | bytes 32800 | tf_op jit(solution)/shard_map/ppermute | solution.py:391
  16.8 0.1 ready_targets.1
  16.9 0.3 %collective-permute-done.3.refs_1_ = f32[96,256]{1,0:T(8,128)S(1)} collective-permute-done((f32[96,256]{1,0:T(8,128)S(1)}, f32[96,256]{1,0:T(8,128)S(1)}, u32[]{:S(2)}, u32[]{:S(2)}) %collective-permute-start.3) | collective-permute-done | bytes 98336 | tf_op jit(solution)/shard_map/ppermute | solution.py:415
  17.2 0.7 %apply_window.1 = (f32[32,256]{1,0:T(8,128)}, f32[1,2,2,2]{3,2,1,0:T(2,128)}) custom-call(f32[16,128]{1,0:T(8,128)S(1)} %phase.1.phase_ref, f32[96,256]{1,0:T(8,128)S(1)} %get-tuple-element.18.refs_0_, f32[96,256]{1,0:T(8,128)S(1)} %collective-permute-done.3.refs_1_, f32[192,256]{1,0:T(8,128)S(1)} %get-tuple-element.20.refs_2_, ...), custom_call_target="tpu_custom_call" | custom-call | tf_op jit(solution)/shard_map/apply_window/pallas_call | solution.py:376
  (3 shorter events, 0.0 us)
Async XLA Ops:
  0.6 1.1 %copy-start = (f32[1,32,2,8,256]{4,3,2,1,0:T(8,128)S(1)}, f32[1,32,2,8,256]{4,3,2,1,0:T(8,128)}, u32[]{:S(2)}) copy-start(f32[1,32,2,8,256]{4,3,2,1,0:T(8,128)} %param.6) | copy-start | bytes 1572868
  0.7 0.7 %copy-start.3 = (s32[1,32]{1,0:T(1,128)S(1)}, s32[1,32]{1,0:T(1,128)}, u32[]{:S(2)}) copy-start(s32[1,32]{1,0:T(1,128)} %param.8) | copy-start | bytes 388
  1.9 6.0 %collective-permute-start = (f32[104,256]{1,0:T(8,128)S(1)}, f32[104,256]{1,0:T(8,128)S(1)}, u32[]{:S(2)}, u32[]{:S(2)}) collective-permute-start(f32[104,256]{1,0:T(8,128)S(1)} %get-tuple-element.14.refs_0_), channel_id=1, source_target_pairs={{1,0},{0,1},{3,2},{2,3},{5,4},{4,5},{7,6},{6,7},{9,8},{8,9},{11,10... | collective-permute-start | bytes 319496 | tf_op jit(solution)/shard_map/ppermute | solution.py:391
  4.9 0.7 %copy-start.1 = (s32[16]{0:T(128)S(1)}, s32[16]{0:T(128)}, u32[]{:S(2)}) copy-start(s32[16]{0:T(128)} %kpoint_hbm.1) | copy-start | bytes 196
  7.9 5.0 %copy-start.2 = (f32[1,2,2,8,256]{4,3,2,1,0:T(8,128)S(1)}, f32[1,2,2,8,256]{4,3,2,1,0:T(8,128)}, u32[]{:S(2)}) copy-start(f32[1,2,2,8,256]{4,3,2,1,0:T(8,128)} %param.5) | copy-start | bytes 98308
  8.0 7.5 %collective-permute-start.1 = (f32[96,256]{1,0:T(8,128)S(1)}, f32[96,256]{1,0:T(8,128)S(1)}, u32[]{:S(2)}, u32[]{:S(2)}) collective-permute-start(f32[96,256]{1,0:T(8,128)S(1)} %join_slabs.1.refs_2_), channel_id=1, source_target_pairs={{28,0},{30,2},{0,4},{2,6},{4,8},{6,10},{8,12},{10,14},{12,16},{14,... | collective-permute-start | bytes 294920 | tf_op jit(solution)/shard_map/ppermute | solution.py:391
  9.7 6.0 %collective-permute-start.2 = (f32[96,256]{1,0:T(8,128)S(1)}, f32[96,256]{1,0:T(8,128)S(1)}, u32[]{:S(2)}, u32[]{:S(2)}) collective-permute-start(f32[96,256]{1,0:T(8,128)S(1)} %join_slabs.1.refs_2_), channel_id=1, source_target_pairs={{4,0},{6,2},{8,4},{10,6},{12,8},{14,10},{16,12},{18,14},{20,16},{2... | collective-permute-start | bytes 294920 | tf_op jit(solution)/shard_map/ppermute | solution.py:391
  12.9 3.9 %collective-permute-start.4 = (f32[32,256]{1,0:T(8,128)S(1)}, f32[32,256]{1,0:T(8,128)S(1)}, u32[]{:S(2)}, u32[]{:S(2)}) collective-permute-start(f32[32,256]{1,0:T(8,128)S(1)} %bitcast.15), channel_id=1, source_target_pairs={{1,0},{0,1},{3,2},{2,3},{5,4},{4,5},{7,6},{6,7},{9,8},{8,9},{11,10... | collective-permute-start | bytes 98312 | tf_op jit(solution)/shard_map/ppermute | solution.py:391
  15.8 1.4 %collective-permute-start.3 = (f32[96,256]{1,0:T(8,128)S(1)}, f32[96,256]{1,0:T(8,128)S(1)}, u32[]{:S(2)}, u32[]{:S(2)}) collective-permute-start(f32[96,256]{1,0:T(8,128)S(1)} %select_add_fusion), channel_id=1, source_target_pairs={{0,2},{2,0},{4,6},{6,4},{8,10},{10,8},{12,14},{14,12},{16,18},{18,... | collective-permute-start | bytes 294920 | tf_op jit(solution)/shard_map/ppermute | solution.py:415

commit v9 on v8

--- a/solution.py
+++ b/solution.py
@@ -134,10 +134,11 @@
     )(block_index, weights, orb)
 
 
-def phase_of(kpoint, place, cycle):
-    def body(place_ref, kpoint_hbm, out_ref, labels, sem):
+def phase_of(kpoint, place, cycle, targets):
+    def body(place_ref, kpoint_hbm, targets_ref, out_ref, held_ref, labels, sem):
         load = pltpu.make_async_copy(kpoint_hbm, labels, sem)
         load.start()
+        held_ref[...] = targets_ref[...]
         load.wait()
         label = labels[place_ref[0]].astype(jnp.float32)
         angle = jnp.full((8, CY), label * (2.0 * math.pi / cycle), jnp.float32)
@@ -146,13 +147,16 @@
 
     return pl.pallas_call(
         body,
-        out_shape=jax.ShapeDtypeStruct((16, CY), jnp.float32),
-        in_specs=[SMEM, HBM],
-        out_specs=VMEM,
+        out_shape=(
+            jax.ShapeDtypeStruct((16, CY), jnp.float32),
+            jax.ShapeDtypeStruct(targets.shape, jnp.float32),
+        ),
+        in_specs=[SMEM, HBM, VMEM],
+        out_specs=(VMEM, VMEM),
         scratch_shapes=[pltpu.SMEM(kpoint.shape, jnp.int32), pltpu.SemaphoreType.DMA],
         compiler_params=PARAMS,
         name="phase",
-    )(place.reshape(1), kpoint)
+    )(place.reshape(1), kpoint, targets)
 
 
 def phase_rows(ref):
@@ -398,7 +402,7 @@
     psi = targets.reshape(2 * bands * planes, CELLS)
     orb = orbitals.reshape(-1, planes, CX, CY).transpose(0, 2, 1, 3).reshape(-1, CY)
 
-    phase = phase_of(kpoint, place, cycle)
+    phase, psi = phase_of(kpoint, place, cycle, psi)
 
     held = occupied.shape[1]
     words = occupied + 2 * lax.pad(block_index, jnp.int32(0), [(0, held - 1, 0)]).reshape(1, held)
@@ -410,12 +414,12 @@
 
     left = shift(mine, "kring", -2)
     right = shift(mine, "kring", 2)
+    held = ready_targets(psis, [mine], planes, bands)
+    right, left, near, weights, total = lax.optimization_barrier((right, left, *held))
     odd = lax.rem(place, 2) == 1
     lacking = jnp.where(odd, left, right) + mine
     other = lax.ppermute(lacking, "kring", [(i, i ^ 1) for i in range(cycle)])
-    held = ready_targets(psis, [mine, right, left], planes, bands)
-    other, near, weights, total = lax.optimization_barrier((other, *held))
-    exchange, tile = apply(phase, [total, other], near, weights, planes, bands, slabs)
+    exchange, tile = apply(phase, [total, right, left, other], near, weights, planes, bands, slabs)
     return exchange.reshape(targets.shape), tile
 
 

time: 18 us -> 18 us (level)
  starting transfers between devices: 9.62 us -> 8.06 us
  waiting for transfers between devices: 4.16 us -> 5.71 us
    ppermute x4, starting transfers between devices: 9.55 us -> 7.99 us  [shift(): lax.ppermute(value, axis, [((i + distance) % count, i) for i in range(cou...]
    ppermute x1, waiting for transfers between devices: 0.28 us -> 1.29 us  [body(): other = lax.ppermute(lacking, 'kring', [(i, i ^ 1) for i in range(cycle)])]
    ppermute x4, waiting for transfers between devices: 3.88 us -> 4.43 us  [shift(): lax.ppermute(value, axis, [((i + distance) % count, i) for i in range(cou...]
  transfers between devices with their start and end apart: 5 -> 5, of which waited for: 5 -> 4; matrix products, arithmetic and copies ran while one was open for 0% -> 0% of each run, Pallas kernels for 4% -> 4%
where the time goes in v9:
time: 18 us; the launch traced here: 17.9 us
  starting transfers between devices  8.06 us (45%)
  waiting for transfers between devices  5.71 us (32%)
  Pallas kernels  1.77 us (10%)
  between operations  1.41 us (8%)
  local copies, waits for them, and re-layouts  0.88 us (5%)
    ppermute x4, starting transfers between devices, shift(): lax.ppermute(value, axis, [((i + distance) % count, i) for i in range(cou...  7.99 us
    ppermute x4, waiting for transfers between devices, shift(): lax.ppermute(value, axis, [((i + distance) % count, i) for i in range(cou...  4.43 us
    ppermute x1, waiting for transfers between devices, body(): other = lax.ppermute(lacking, 'kring', [(i, i ^ 1) for i in range(cycle)])  1.29 us
    unnamed x8, local copies, waits for them, and re-layouts  0.88 us
    pallas_call x1, Pallas kernels, apply(): pl.pallas_call(body, out_shape=(jax.ShapeDtypeStruct((2 * bands * planes,...  0.72 us
    pallas_call x1, Pallas kernels, phase_of(): pl.pallas_call(body, out_shape=(jax.ShapeDtypeStruct((16, CY), jnp.float3...  0.6 us
  transfers between devices with their start and end apart: 5, of which 4 were waited for; matrix products, arithmetic and copies ran while one was open for 0% of the time, Pallas kernels for 4%

profile of v9, /device:TPU:0, one launch (start us, length us, event | category | flops | bytes accessed | tf_op | source)
XLA Modules:
  0.0 17.9 jit_solution(8747601517092241744)
XLA Ops:
  0.6 0.0 copy-start
  0.7 0.0 copy-start.3
  1.4 0.0 copy-done.3
  1.4 0.1 spread_mask.1.refs_1_
  1.5 0.2 %copy-done = f32[1,32,2,8,256]{4,3,2,1,0:T(8,128)S(1)} copy-done((f32[1,32,2,8,256]{4,3,2,1,0:T(8,128)S(1)}, f32[1,32,2,8,256]{4,3,2,1,0:T(8,128)}, u32[]{:S(2)}) %copy-start) | copy-done | bytes 524312
  1.7 0.0 copy-start.1
  1.7 0.2 local_fields.1
  1.9 3.0 %collective-permute-start = (f32[104,256]{1,0:T(8,128)S(1)}, f32[104,256]{1,0:T(8,128)S(1)}, u32[]{:S(2)}, u32[]{:S(2)}) collective-permute-start(f32[104,256]{1,0:T(8,128)S(1)} %get-tuple-element.18.refs_0_), channel_id=1, source_target_pairs={{1,0},{0,1},{3,2},{2,3},{5,4},{4,5},{7,6},{6,7},{9,8},{8,9},{11,10... | collective-permute-start | bytes 319496 | tf_op jit(solution)/shard_map/ppermute | solution.py:395
  4.9 0.0 copy-start.2
  4.9 0.0 copy-done.1
  4.9 0.7 %copy-done.2 = s32[16]{0:T(128)S(1)} copy-done((s32[16]{0:T(128)S(1)}, s32[16]{0:T(128)}, u32[]{:S(2)}) %copy-start.2) | copy-done | bytes 88
  5.6 0.6 %phase.1 = (f32[16,128]{1,0:T(8,128)S(1)}, f32[32,256]{1,0:T(8,128)S(1)}) custom-call(s32[1]{0:T(128)} %bitcast.place_ref, s32[16]{0:T(128)S(1)} %copy-done.2, f32[32,256]{1,0:T(8,128)S(1)} %bitcast.15), custom_call_target="tpu_custom_call" | custom-call | tf_op jit(solution)/shard_map/phase/pallas_call | solution.py:148
  6.2 0.1 collective-permute-start.3
  6.3 1.6 %collective-permute-done.refs_1_ = f32[104,256]{1,0:T(8,128)S(1)} collective-permute-done((f32[104,256]{1,0:T(8,128)S(1)}, f32[104,256]{1,0:T(8,128)S(1)}, u32[]{:S(2)}, u32[]{:S(2)}) %collective-permute-start) | collective-permute-done | bytes 106528 | tf_op jit(solution)/shard_map/ppermute | solution.py:395
  7.9 0.1 join_slabs.1.refs_2_
  8.0 1.8 %collective-permute-start.2 = (f32[96,256]{1,0:T(8,128)S(1)}, f32[96,256]{1,0:T(8,128)S(1)}, u32[]{:S(2)}, u32[]{:S(2)}) collective-permute-start(f32[96,256]{1,0:T(8,128)S(1)} %join_slabs.1.refs_2_), channel_id=1, source_target_pairs={{28,0},{30,2},{0,4},{2,6},{4,8},{6,10},{8,12},{10,14},{12,16},{14,... | collective-permute-start | bytes 294920 | tf_op jit(solution)/shard_map/ppermute | solution.py:395
  9.7 3.1 %collective-permute-start.1 = (f32[96,256]{1,0:T(8,128)S(1)}, f32[96,256]{1,0:T(8,128)S(1)}, u32[]{:S(2)}, u32[]{:S(2)}) collective-permute-start(f32[96,256]{1,0:T(8,128)S(1)} %join_slabs.1.refs_2_), channel_id=1, source_target_pairs={{4,0},{6,2},{8,4},{10,6},{12,8},{14,10},{16,12},{18,14},{20,16},{2... | collective-permute-start | bytes 294920 | tf_op jit(solution)/shard_map/ppermute | solution.py:395
  12.8 0.0 collective-permute-done.3.refs_1_
  12.9 0.1 ready_targets.1
  13.0 2.5 %collective-permute-done.2.refs_2_ = f32[96,256]{1,0:T(8,128)S(1)} collective-permute-done((f32[96,256]{1,0:T(8,128)S(1)}, f32[96,256]{1,0:T(8,128)S(1)}, u32[]{:S(2)}, u32[]{:S(2)}) %collective-permute-start.2) | collective-permute-done | bytes 98336 | tf_op jit(solution)/shard_map/ppermute | solution.py:395
  15.5 0.3 %collective-permute-done.1.refs_1_ = f32[96,256]{1,0:T(8,128)S(1)} collective-permute-done((f32[96,256]{1,0:T(8,128)S(1)}, f32[96,256]{1,0:T(8,128)S(1)}, u32[]{:S(2)}, u32[]{:S(2)}) %collective-permute-start.1) | collective-permute-done | bytes 98336 | tf_op jit(solution)/shard_map/ppermute | solution.py:395
  15.8 0.1 collective-permute-start.4
  15.9 1.3 %collective-permute-done.4.refs_3_ = f32[96,256]{1,0:T(8,128)S(1)} collective-permute-done((f32[96,256]{1,0:T(8,128)S(1)}, f32[96,256]{1,0:T(8,128)S(1)}, u32[]{:S(2)}, u32[]{:S(2)}) %collective-permute-start.4) | collective-permute-done | bytes 98336 | tf_op jit(solution)/shard_map/ppermute | solution.py:421
  17.1 0.7 %apply_window.1 = (f32[32,256]{1,0:T(8,128)}, f32[1,2,2,2]{3,2,1,0:T(2,128)}) custom-call(f32[16,128]{1,0:T(8,128)S(1)} %get-tuple-element.16.phase_ref, f32[96,256]{1,0:T(8,128)S(1)} %get-tuple-element.23.refs_0_, f32[96,256]{1,0:T(8,128)S(1)} %collective-permute-done.1.refs_1_, f32[96,256]{1,0:T(8,128)S(1)} %collective-permute-done.2.refs_2_, ...), custom_call_target="tpu_custom_call" | custom-call | tf_op jit(solution)/shard_map/apply_window/pallas_call | solution.py:380
  (3 shorter events, 0.0 us)
Async XLA Ops:
  0.6 1.1 %copy-start = (f32[1,32,2,8,256]{4,3,2,1,0:T(8,128)S(1)}, f32[1,32,2,8,256]{4,3,2,1,0:T(8,128)}, u32[]{:S(2)}) copy-start(f32[1,32,2,8,256]{4,3,2,1,0:T(8,128)} %param.6) | copy-start | bytes 1572868
  0.7 0.7 %copy-start.3 = (s32[1,32]{1,0:T(1,128)S(1)}, s32[1,32]{1,0:T(1,128)}, u32[]{:S(2)}) copy-start(s32[1,32]{1,0:T(1,128)} %param.8) | copy-start | bytes 388
  1.7 3.2 %copy-start.1 = (f32[1,2,2,8,256]{4,3,2,1,0:T(8,128)S(1)}, f32[1,2,2,8,256]{4,3,2,1,0:T(8,128)}, u32[]{:S(2)}) copy-start(f32[1,2,2,8,256]{4,3,2,1,0:T(8,128)} %param.5) | copy-start | bytes 98308
  1.9 6.0 %collective-permute-start = (f32[104,256]{1,0:T(8,128)S(1)}, f32[104,256]{1,0:T(8,128)S(1)}, u32[]{:S(2)}, u32[]{:S(2)}) collective-permute-start(f32[104,256]{1,0:T(8,128)S(1)} %get-tuple-element.18.refs_0_), channel_id=1, source_target_pairs={{1,0},{0,1},{3,2},{2,3},{5,4},{4,5},{7,6},{6,7},{9,8},{8,9},{11,10... | collective-permute-start | bytes 319496 | tf_op jit(solution)/shard_map/ppermute | solution.py:395
  4.9 0.7 %copy-start.2 = (s32[16]{0:T(128)S(1)}, s32[16]{0:T(128)}, u32[]{:S(2)}) copy-start(s32[16]{0:T(128)} %kpoint_hbm.1) | copy-start | bytes 196
  6.2 6.7 %collective-permute-start.3 = (f32[32,256]{1,0:T(8,128)S(1)}, f32[32,256]{1,0:T(8,128)S(1)}, u32[]{:S(2)}, u32[]{:S(2)}) collective-permute-start(f32[32,256]{1,0:T(8,128)S(1)} %get-tuple-element.19.refs_0_), channel_id=1, source_target_pairs={{1,0},{0,1},{3,2},{2,3},{5,4},{4,5},{7,6},{6,7},{9,8},{8,9},{11,10... | collective-permute-start | bytes 98312 | tf_op jit(solution)/shard_map/ppermute | solution.py:395
  8.0 7.5 %collective-permute-start.2 = (f32[96,256]{1,0:T(8,128)S(1)}, f32[96,256]{1,0:T(8,128)S(1)}, u32[]{:S(2)}, u32[]{:S(2)}) collective-permute-start(f32[96,256]{1,0:T(8,128)S(1)} %join_slabs.1.refs_2_), channel_id=1, source_target_pairs={{28,0},{30,2},{0,4},{2,6},{4,8},{6,10},{8,12},{10,14},{12,16},{14,... | collective-permute-start | bytes 294920 | tf_op jit(solution)/shard_map/ppermute | solution.py:395
  9.7 6.0 %collective-permute-start.1 = (f32[96,256]{1,0:T(8,128)S(1)}, f32[96,256]{1,0:T(8,128)S(1)}, u32[]{:S(2)}, u32[]{:S(2)}) collective-permute-start(f32[96,256]{1,0:T(8,128)S(1)} %join_slabs.1.refs_2_), channel_id=1, source_target_pairs={{4,0},{6,2},{8,4},{10,6},{12,8},{14,10},{16,12},{18,14},{20,16},{2... | collective-permute-start | bytes 294920 | tf_op jit(solution)/shard_map/ppermute | solution.py:395
  15.8 1.4 %collective-permute-start.4 = (f32[96,256]{1,0:T(8,128)S(1)}, f32[96,256]{1,0:T(8,128)S(1)}, u32[]{:S(2)}, u32[]{:S(2)}) collective-permute-start(f32[96,256]{1,0:T(8,128)S(1)} %select_add_fusion), channel_id=1, source_target_pairs={{0,2},{2,0},{4,6},{6,4},{8,10},{10,8},{12,14},{14,12},{16,18},{18,... | collective-permute-start | bytes 294920 | tf_op jit(solution)/shard_map/ppermute | solution.py:421
